TPU v7x, 32 devices: a whole 2x2x4 slice. The times are simulated.
32 devices in a mesh: groups: 2 (over y), tensor: 4 (over z), replica: 4 (over x, core).
Axes of the slice: x: 2, y: 2, z: 4, core: 2. Of those that a mesh axis runs over, the one named last changes fastest.
Arguments:
- hidden: bfloat16 [2, 1024, 8192], P(None, ('groups', 'replica'), 'tensor'), parts along dimension 1, may hold values from -6 to 6
- base_weight: bfloat16 [8192, 2048], P('tensor'), may hold values from -0.0625 to 0.0625
- delta_values: bfloat16 [16, 8192, 2048], P(('groups', 'replica'), 'tensor'), parts along dimension 0, may hold values from -4 to 4
- delta_scales: bfloat16 [16, 64, 2048], P(('groups', 'replica'), 'tensor'), parts along dimension 0, may hold values from 0.0019989014 to 0.019897461
- tenant_slot: int32 [8], replicated, may hold values from 0 to 7, each once
- seg_tenant: int32 [8, 4], P(('groups', 'replica')), parts along dimension 0, may hold values from 0 to 7, as said below
- seg_length: int32 [8, 4], P(('groups', 'replica')), parts along dimension 0, may hold values from 1 to 40, 128 in all within a row
- queries: bfloat16 [2, 1024, 8192], P(None, ('groups', 'replica', 'tensor')), parts along dimension 1, may hold values from -48 to 48
- kv_cache: bfloat16 [1024, 128, 2048], P(('groups', 'replica', 'tensor')), parts along dimension 0, may hold values from -48 to 48
- cache_length: int32 [1024], P(('groups', 'replica', 'tensor')), parts along dimension 0, may hold values from 2 to 128
Outputs:
- new_kv: bfloat16 [2, 1024, 2048], P(None, ('groups', 'replica', 'tensor')), parts along dimension 1
- attention: bfloat16 [2, 1024, 8192], P(None, ('groups', 'replica', 'tensor')), parts along dimension 1
There are 2 independent parts, one for each index of `groups`. A program takes and returns all parts, laid end to end along the dimension named above; an argument that names none is the same for every part. Nothing has to cross between parts.
Inputs may be any that keep to these rules, and one draw needn't show every extreme that they name: `seg_tenant`: the 4 tenants of one replica are distinct. `tenant_slot`: each tenant has exactly one slot. `seg_length`: a replica's lengths sum to 128; its largest is exactly 40.
All inputs are finite; a program needn't handle non-finite values.
Results may differ from a plain program's by a relative error of at most 0.0056.
Values may be sent and summed in bfloat16 or wider, within the bound.
No kernel may reach another device: no remote copies, remote signals or barrier semaphores. Data moves between devices by JAX's collectives and lax.ppermute only.
A program may use at most 256 MiB of HBM per device.

v0:
```python
import math

import jax
import jax.numpy as jnp
from jax import lax
from jax.sharding import PartitionSpec as P

HEADS = 64
KVH = 8
HD = 128


def dequantize(values, scales):
    count_slots, feature_rows, columns = values.shape
    blocks = scales.shape[1]
    widened = (
        values.astype(jnp.float32).reshape(count_slots, blocks, feature_rows // blocks, columns)
        * scales.astype(jnp.float32)[:, :, None, :]
    )
    return widened.reshape(count_slots, feature_rows, columns).astype(jnp.bfloat16)


def attend(queries, new_kv, kv_cache, cache_length):
    shard_rows = queries.shape[1]
    cache_len = kv_cache.shape[1]
    group_size = HEADS // KVH
    key_width = KVH * HD
    query_heads = queries.reshape(2, shard_rows, KVH, group_size, HD)
    cache_keys = kv_cache[:, :, :key_width].reshape(shard_rows, cache_len, KVH, HD)
    cache_vals = kv_cache[:, :, key_width:].reshape(shard_rows, cache_len, KVH, HD)
    new_keys = new_kv[:, :, :key_width].reshape(2, shard_rows, KVH, HD)
    new_vals = new_kv[:, :, key_width:].reshape(2, shard_rows, KVH, HD)
    inv_scale = 1.0 / math.sqrt(HD)
    score_cache = (
        jnp.einsum("srkgd,rpkd->srkgp", query_heads, cache_keys, preferred_element_type=jnp.float32)
        * inv_scale
    )
    score_new = (
        jnp.einsum("srkgd,trkd->srkgt", query_heads, new_keys, preferred_element_type=jnp.float32)
        * inv_scale
    )
    positions = jnp.arange(cache_len, dtype=jnp.int32)
    live_cache = positions[None, :] < cache_length[:, None]
    steps_idx = jnp.arange(2, dtype=jnp.int32)
    live_new = steps_idx[None, :] <= steps_idx[:, None]
    score_cache = jnp.where(live_cache[None, :, None, None, :], score_cache, -1e30)
    score_new = jnp.where(live_new[:, None, None, None, :], score_new, -1e30)
    row_max = jnp.maximum(jnp.max(score_cache, axis=-1), jnp.max(score_new, axis=-1))[..., None]
    expo_cache = jnp.exp(score_cache - row_max)
    expo_new = jnp.exp(score_new - row_max)
    denominator = jnp.sum(expo_cache, axis=-1, keepdims=True) + jnp.sum(
        expo_new, axis=-1, keepdims=True
    )
    prob_cache = (expo_cache / denominator).astype(jnp.bfloat16)
    prob_new = (expo_new / denominator).astype(jnp.bfloat16)
    out_cache = jnp.einsum(
        "srkgp,rpkd->srkgd", prob_cache, cache_vals, preferred_element_type=jnp.float32
    )
    out_new = jnp.einsum(
        "srkgt,trkd->srkgd", prob_new, new_vals, preferred_element_type=jnp.float32
    )
    return (out_cache + out_new).astype(jnp.bfloat16).reshape(2, shard_rows, HEADS * HD)


def local(
    hidden,
    base_weight,
    delta_values,
    delta_scales,
    tenant_slot,
    seg_tenant,
    seg_length,
    queries,
    kv_cache,
    cache_length,
):
    rows_all = hidden.shape[1]
    width = hidden.shape[2]
    kv_width = base_weight.shape[1]
    lengths = seg_length[0]
    seg_ends = jnp.cumsum(lengths)
    row_ids = jnp.arange(rows_all, dtype=jnp.int32)
    seg_of_row = jnp.sum((row_ids[:, None] >= seg_ends[None, :]).astype(jnp.int32), axis=1)
    tenant_ids = jnp.arange(tenant_slot.shape[0], dtype=jnp.int32)
    seg_slot = jnp.sum(
        jnp.where(seg_tenant[0][:, None] == tenant_ids[None, :], tenant_slot[None, :], 0), axis=1
    )
    seg_ids = jnp.arange(lengths.shape[0], dtype=jnp.int32)
    seg_onehot = seg_of_row[:, None] == seg_ids[None, :]
    row_slot = jnp.sum(jnp.where(seg_onehot, seg_slot[None, :], 0), axis=1)
    flat_x = hidden.reshape(2 * rows_all, width)
    base_term = jnp.dot(flat_x, base_weight, preferred_element_type=jnp.float32)
    both_slots = jnp.tile(row_slot, 2)
    weights = dequantize(
        lax.all_gather(delta_values, "replica", axis=0, tiled=True),
        lax.all_gather(delta_scales, "replica", axis=0, tiled=True),
    )
    products = jnp.einsum(
        "rd,kdc->krc", flat_x, weights, preferred_element_type=jnp.float32
    ).astype(jnp.bfloat16)
    products = lax.optimization_barrier(products)
    slot_ids = jnp.arange(weights.shape[0], dtype=jnp.int32)
    hits = both_slots[None, :] == slot_ids[:, None]
    delta_term = jnp.sum(jnp.where(hits[:, :, None], products.astype(jnp.float32), 0.0), axis=0)
    partial_kv = (base_term + delta_term).reshape(2, rows_all, kv_width)
    shard_rows = rows_all // lax.axis_size("tensor")
    summed = lax.psum(partial_kv, "tensor")
    mine = lax.dynamic_slice_in_dim(summed, lax.axis_index("tensor") * shard_rows, shard_rows, 1)
    new_kv = mine.astype(jnp.bfloat16)
    attention = attend(queries, new_kv, kv_cache, cache_length)
    return (new_kv, attention)


def solution(mesh):
    placed = (
        P(None, ("groups", "replica"), "tensor"),
        P("tensor", None),
        P(("groups", "replica"), "tensor", None),
        P(("groups", "replica"), "tensor", None),
        P(),
        P(("groups", "replica"), None),
        P(("groups", "replica"), None),
        P(None, ("groups", "replica", "tensor"), None),
        P(("groups", "replica", "tensor"), None, None),
        P(("groups", "replica", "tensor")),
    )
    return jax.shard_map(
        local,
        mesh=mesh,
        in_specs=placed,
        out_specs=(
            P(None, ("groups", "replica", "tensor"), None),
            P(None, ("groups", "replica", "tensor"), None),
        ),
        check_vma=False,
    )
```

profile of v0, /device:TPU:0, one launch (start us, length us, event | category | flops | bytes accessed | tf_op | source)
XLA Modules:
  0.0 604.5 jit_solution(14189943830436077005)
XLA Ops:
  7.3 0.7 all-gather.2.cloned.1.call-update
  8.2 8.6 %all_gather.7 = bf16[8,16,2048]{2,1,0:T(8,128)(2,1)S(1)} all-gather(bf16[2,16,2048]{2,1,0:T(8,128)(2,1)S(1)} %copy-done.3), channel_id=1, replica_groups=mesh['groups'=2,'tensor'=4,'replica'=4] {'replica'}, dimensions={0}, use_global_device_ids=true | all-gather | bytes 655360 | tf_op jit(solution)/shard_map/all_gather | solution.py:96
  16.8 1.1 convert_element_type.35
  18.0 1.4 copy.62
  19.4 18.5 %fusion.22 = (bf16[32,128,1024]{2,1,0:T(8,128)(2,1)}, bf16[32,128,1024]{2,1,0:T(8,128)(2,1)}) fusion(bf16[32,128,2048]{2,1,0:T(8,128)(2,1)} %param.18), kind=kLoop, calls=%fused_computation.47 | loop fusion | bytes 33554432 | tf_op jit(solution)/shard_map/slice | solution.py:30
  37.9 12.5 %copy.60 = bf16[32,128,1024]{1,2,0:T(8,128)(2,1)} copy(bf16[32,128,1024]{2,1,0:T(8,128)(2,1)} %get-tuple-element.3) | data formatting | bytes 16777216
  50.3 12.4 %copy.61 = bf16[32,128,1024]{1,2,0:T(8,128)(2,1)} copy(bf16[32,128,1024]{2,1,0:T(8,128)(2,1)} %get-tuple-element.2) | data formatting | bytes 16777216
  63.2 6.1 %bitcast_reduce_fusion = (f32[2,32,8,8]{3,0,2,1:T(2,128)S(1)}, f32[32,8,128,2,8]{2,4,3,1,0:T(8,128)S(1)}) fusion(pred[32,128]{1,0:T(8,128)(4,1)S(1)} %iota_compare_fusion, bf16[32,128,8,128,1]{1,3,4,2,0:T(8,128)(2,1)} %bitcast.75, bf16[2,32,8,8,128]{4,3,2,1,0:T(8,128)(2,1)} %bitcast.79), kind=kOutput, calls=%fused_computation.8 | convolution fusion | flops 135786496 | bytes 11554816 | tf_op jit(solution)/shard_map/srkgd,rpkd->srkgp/dot_general | solution.py:35
  69.3 335.7 %all-gather.2.cloned.1.call-done = bf16[8,2048,2048]{2,1,0:T(8,128)(2,1)} async-done(((bf16[2,2048,2048]{2,1,0:T(8,128)(2,1)}), bf16[8,2048,2048]{2,1,0:T(8,128)(2,1)}) %all-gather.2.cloned.1.call-update) | async-done | bytes 67108880 | tf_op jit(solution)/shard_map/all_gather | solution.py:95
  405.1 44.5 %fusion = bf16[8,2048,2048]{2,1,0:T(8,128)(2,1)} fusion(bf16[8,2048,2048]{2,1,0:T(8,128)(2,1)} %all-gather.2.cloned.1.call-done, f32[8,16,2048]{2,1,0:T(8,128)} %convert_element_type.35), kind=kLoop, calls=%fused_computation.1 | loop fusion | flops 100663296 | bytes 135266304 | tf_op jit(solution)/shard_map/convert_element_type | solution.py:20
  449.6 30.3 %convert_bitcast_fusion = bf16[8,256,2048]{1,2,0:T(8,128)(2,1)} fusion(bf16[8,2048,2048]{2,1,0:T(8,128)(2,1)} %fusion, bf16[256,2048,1]{1,0,2:T(8,128)(2,1)S(1)} %bitcast.73), kind=kOutput, calls=%fused_computation.3 | convolution fusion | flops 17184063488 | bytes 76546048 | tf_op jit(solution)/shard_map/rd,kdc->krc/dot_general | solution.py:98
  479.9 6.7 %select_reduce_fusion = f32[256,2048]{0,1:T(8,128)} fusion(bf16[8,256,2048]{1,2,0:T(8,128)(2,1)} %convert_bitcast_fusion, pred[8,256]{1,0:T(8,128)(4,1)S(1)} %iota_compare_fusion.1), kind=kLoop, calls=%fused_computation.2 | loop fusion | flops 12058624 | bytes 10487808 | tf_op jit(solution)/shard_map/reduce_sum | solution.py:104
  486.6 2.9 copy.37
  489.5 7.7 %convolution_add_fusion = f32[256,2048]{1,0:T(8,128)} fusion(f32[256,2048]{1,0:T(8,128)} %copy.37, bf16[256,2048]{1,0:T(8,128)(2,1)S(1)} %bitcast.74, bf16[2048,2048]{1,0:T(8,128)(2,1)} %param.11), kind=kOutput, calls=%fused_computation.4 | convolution fusion | flops 2148007936 | bytes 13631488 | tf_op jit(solution)/shard_map/dot_general | solution.py:92
  497.2 79.4 %all-reduce.1 = bf16[2,128,2048]{2,1,0:T(8,128)(2,1)} all-reduce(f32[2,128,2048]{2,1,0:T(8,128)} %bitcast.81), channel_id=1, replica_groups=mesh['groups'=2,'tensor'=4,'replica'=4] {'tensor'}, use_global_device_ids=true, to_apply=%region_5.6 | all-reduce | flops 524288 | bytes 3145728 | tf_op jit(solution)/shard_map/psum | solution.py:107
  576.7 1.0 dynamic-slice_convert_fusion
  577.7 0.6 copy-done.1
  578.4 6.3 %fusion.24 = (f32[2,32,8,8]{3,0,2,1:T(2,128)S(1)}, f32[2,32,8,8,2]{3,4,0,2,1:T(2,128)S(1)}) fusion(bf16[2,32,8,8,128]{4,3,2,1,0:T(8,128)(2,1)} %bitcast.80, bf16[2,32,8,128,1]{3,2,1,0,4:T(8,128)(2,1)S(1)} %bitcast_bitcast_fusion.1, pred[2,2]{1,0:T(4,128)(4,1)S(1)} %iota_compare_fusion.5), kind=kOutput, calls=%fused_computation.49 | convolution fusion | flops 2117632 | bytes 1228804 | tf_op jit(solution)/shard_map/srkgd,trkd->srkgt/dot_general | solution.py:39
  584.8 1.5 fusion.3
  586.3 1.0 fusion.14
  587.5 2.2 fusion.15
  589.7 0.6 slice-done.1
  590.2 5.9 fusion.1
  596.4 1.3 reshape.131
  (36 shorter events, 1.6 us)
Async XLA Ops:
  7.2 442.5 %copy-start = (bf16[2,128,2048]{2,1,0:T(8,128)(2,1)S(1)}, bf16[2,128,2048]{2,1,0:T(8,128)(2,1)}, u32[]{:S(2)}) copy-start(bf16[2,128,2048]{2,1,0:T(8,128)(2,1)} %param.10) | copy-start | bytes 3145732
  7.2 1.0 copy-start.3
  7.2 10.7 %copy-start.5 = (s32[1,4]{1,0:T(1,128)S(1)}, s32[1,4]{1,0:T(1,128)}, u32[]{:S(2)}) copy-start(s32[1,4]{1,0:T(1,128)} %param.16) | copy-start | bytes 52
  7.2 10.8 %copy-start.2 = (bf16[2,32,8192]{2,1,0:T(8,128)(2,1)S(1)}, bf16[2,32,8192]{2,1,0:T(8,128)(2,1)}, u32[]{:S(2)}) copy-start(bf16[2,32,8192]{2,1,0:T(8,128)(2,1)} %param.17) | copy-start | bytes 3145732
  7.2 397.9 %all-gather.2.cloned.1.call-start = ((), (), s32[]{:S(2)}) async-start(), calls=%async_computation | async-start | bytes 83886080 | tf_op jit(solution)/shard_map/all_gather | solution.py:95
  50.3 12.5 %copy-start.6 = (s32[8]{0:T(128)S(1)}, s32[8]{0:T(128)}, u32[]{:S(2)}) copy-start(s32[8]{0:T(128)} %param.14) | copy-start | bytes 100
  50.3 12.5 %copy-start.7 = (s32[1,4]{1,0:T(1,128)S(1)}, s32[1,4]{1,0:T(1,128)}, u32[]{:S(2)}) copy-start(s32[1,4]{1,0:T(1,128)} %param.15) | copy-start | bytes 52
  50.3 12.8 %copy-start.4 = (s32[32]{0:T(128)S(1)}, s32[32]{0:T(128)}, u32[]{:S(2)}) copy-start(s32[32]{0:T(128)} %param.19) | copy-start | bytes 388
  577.6 0.7 copy-start.1
  578.3 11.3 %slice-start = ((s8[8388608]{0:T(1024)(128)(4,1)}), s8[4194304]{0:T(1024)(128)(4,1)S(1)}, s32[]{:S(2)}) async-start(s8[8388608]{0:T(1024)(128)(4,1)} %bitcast.76), calls=%async_computation.1 | async-start | bytes 8388608
  587.3 2.9 slice-start.1
Sparse Core Ops, SparseCore 0:
  9.6 395.4 all-gather.1
where the time goes:
time: 606 us; the launch traced here: 605 us
  waiting for transfers between devices  336 us (55%)
  blocking collectives  88 us (15%)
  matrix products  58.4 us (10%)
  other arithmetic  55.7 us (9%)
  local copies, waits for them, and re-layouts  51.7 us (9%)
  between operations  14.2 us (2%)
    all_gather x1, waiting for transfers between devices, local(): lax.all_gather(delta_values, 'replica', axis=0, tiled=True)  336 us
    psum x1, blocking collectives, local(): summed = lax.psum(partial_kv, 'tensor')  79.4 us
    convert_element_type x1, other arithmetic, dequantize(): widened.reshape(count_slots, feature_rows, columns).astype(jnp.bfloat16)  44.5 us
    dot_general x1, matrix products, local(): jnp.einsum('rd,kdc->krc', flat_x, weights, preferred_element_type=jnp.flo...  30.3 us
    unnamed x25, local copies, waits for them, and re-layouts  27.7 us
    slice x1, local copies, waits for them, and re-layouts, attend(): kv_cache[:, :, key_width:].reshape(shard_rows, cache_len, KVH, HD)  18.5 us
  transfers between devices with their start and end apart: 1, of which 1 were waited for; matrix products, arithmetic and copies ran while one was open for 9% of the time, Pallas kernels for 0%

commit v1 on v0

v1 whole, which is shorter than its diff:
```python
import functools
import math

import jax
import jax.numpy as jnp
from jax import lax
from jax.experimental import pallas as pl
from jax.experimental.pallas import tpu as pltpu
from jax.sharding import PartitionSpec as P

HEADS = 64
KVH = 8
HD = 128
GROUP = HEADS // KVH
KEYS = KVH * HD
BLOCK = 128
SEG_MOST = 40
SLOTS = 2
NEG = -1e30
VMEM_LIMIT = 40 * 1024 * 1024


def row_positions(meta_ref, slot_ref, first, steps, rows, shape, axis):
    index = lax.broadcasted_iota(jnp.int32, shape, axis)
    source = index // (steps * rows)
    step = (index // rows) % steps
    row = index % rows
    per_slot = 2 * steps * SEG_MOST
    place = jnp.full(shape, -1, jnp.int32)
    for src in range(2):
        begin = jnp.int32(0)
        for seg in range(meta_ref.shape[1] // 2):
            slot = slot_ref[meta_ref[src, seg]] - first
            length = meta_ref[src, meta_ref.shape[1] // 2 + seg]
            end = begin + length
            held = jnp.logical_and(slot >= 0, slot < SLOTS)
            offset = jnp.where(held, slot * per_slot + src * steps * SEG_MOST - begin, -(1 << 20))
            inside = (source == src) & (row >= begin) & (row < end)
            place = jnp.where(inside, offset + step * SEG_MOST + row, place)
            begin = end
    return place


def delta_body(with_base, steps, rows, *refs):
    if with_base:
        (first_ref, meta_ref, slot_ref, xa_ref, xb_ref, val_ref, sc_ref, base_ref, da_ref, db_ref,
         xc_ref, scatter_ref) = refs
    else:
        (first_ref, meta_ref, slot_ref, xa_ref, xb_ref, val_ref, sc_ref, da_ref, db_ref,
         xc_ref, scatter_ref) = refs
    width = val_ref.shape[1]
    tile = val_ref.shape[2]
    half = steps * rows
    taken = SLOTS * 2 * steps * SEG_MOST
    per_slot = taken // SLOTS

    @pl.when(pl.program_id(0) == 0)
    def _():
        first = first_ref[0]
        along = row_positions(meta_ref, slot_ref, first, steps, rows, (1, 2 * half), 1)
        picks = (lax.broadcasted_iota(jnp.int32, (taken, 2 * half), 0) == along).astype(jnp.bfloat16)
        down = row_positions(meta_ref, slot_ref, first, steps, rows, (2 * half, 1), 0)
        scatter_ref[...] = (
            lax.broadcasted_iota(jnp.int32, (2 * half, taken), 1) == down
        ).astype(jnp.bfloat16)
        xa = xa_ref[...].reshape(half, width)
        xb = xb_ref[...].reshape(half, width)
        got = jnp.dot(picks[:, :half], xa, preferred_element_type=jnp.float32)
        got += jnp.dot(picks[:, half:], xb, preferred_element_type=jnp.float32)
        xc_ref[...] = got.astype(jnp.bfloat16)

    parts = []
    for slot in range(SLOTS):
        scaled = [
            val_ref[slot, b * BLOCK:(b + 1) * BLOCK, :] * sc_ref[slot, b:b + 1, :]
            for b in range(width // BLOCK)
        ]
        weight = jnp.concatenate(scaled, axis=0)
        parts.append(
            jnp.dot(
                xc_ref[slot * per_slot:(slot + 1) * per_slot, :], weight,
                preferred_element_type=jnp.float32,
            ).astype(jnp.bfloat16)
        )
    spread = jnp.dot(
        scatter_ref[...], jnp.concatenate(parts, axis=0), preferred_element_type=jnp.float32
    )
    own = spread[:half]
    if with_base:
        own = own + jnp.dot(
            xa_ref[...].reshape(half, width), base_ref[...], preferred_element_type=jnp.float32
        )
    da_ref[...] = own.reshape(steps, rows, tile).astype(da_ref.dtype)
    db_ref[...] = spread[half:].reshape(steps, rows, tile).astype(db_ref.dtype)


def delta_rows(first, meta, slots, xa, xb, values, scales, base=None):
    steps, rows, width = xa.shape
    columns = values.shape[2]
    tile = min(256, columns)
    smem = pl.BlockSpec(memory_space=pltpu.SMEM)
    whole = pl.BlockSpec((steps, rows, width), lambda i: (0, 0, 0))
    in_specs = [
        smem, smem, smem, whole, whole,
        pl.BlockSpec((SLOTS, width, tile), lambda i: (0, 0, i)),
        pl.BlockSpec((SLOTS, width // BLOCK, tile), lambda i: (0, 0, i)),
    ]
    args = [first, meta, slots, xa, xb, values, scales]
    flops = 2 * SLOTS * 2 * steps * SEG_MOST * width * columns
    size = values.size * 2
    if base is not None:
        in_specs.append(pl.BlockSpec((width, tile), lambda i: (0, i)))
        args.append(base)
        flops += 2 * steps * rows * width * columns
        size += base.size * 2
    out = pl.BlockSpec((steps, rows, tile), lambda i: (0, 0, i))
    taken = SLOTS * 2 * steps * SEG_MOST
    return pl.pallas_call(
        functools.partial(delta_body, base is not None, steps, rows),
        grid=(columns // tile,),
        in_specs=in_specs,
        out_specs=(out, out),
        out_shape=(
            jax.ShapeDtypeStruct(
                (steps, rows, columns), jnp.float32 if base is not None else jnp.bfloat16
            ),
            jax.ShapeDtypeStruct((steps, rows, columns), jnp.bfloat16),
        ),
        scratch_shapes=[
            pltpu.VMEM((taken, width), jnp.bfloat16),
            pltpu.VMEM((2 * steps * rows, taken), jnp.bfloat16),
        ],
        cost_estimate=pl.CostEstimate(flops=flops, bytes_accessed=size, transcendentals=0),
        compiler_params=pltpu.CompilerParams(vmem_limit_bytes=VMEM_LIMIT),
        name="delta_rows",
    )(*args)


def cache_body(len_ref, q_ref, kv_ref, o_ref, lse_ref):
    block = q_ref.shape[0]
    cached = kv_ref.shape[1]
    rows_of = 2 * GROUP
    scale = 1.0 / math.sqrt(HD)
    position = lax.broadcasted_iota(jnp.int32, (HEADS * 2, cached), 1)
    for r in range(block):
        length = len_ref[pl.program_id(0) * block + r]
        scores = jnp.concatenate(
            [
                lax.dot_general(
                    q_ref[r, k * rows_of:(k + 1) * rows_of, :],
                    kv_ref[r, :, k * HD:(k + 1) * HD],
                    (((1,), (1,)), ((), ())),
                    preferred_element_type=jnp.float32,
                )
                for k in range(KVH)
            ],
            axis=0,
        ) * scale
        scores = jnp.where(position < length, scores, NEG)
        top = jnp.max(scores, axis=1, keepdims=True)
        expo = jnp.exp(scores - top)
        total = jnp.sum(expo, axis=1, keepdims=True)
        expo = expo.astype(jnp.bfloat16)
        out = jnp.concatenate(
            [
                jnp.dot(
                    expo[k * rows_of:(k + 1) * rows_of, :],
                    kv_ref[r, :, KEYS + k * HD:KEYS + (k + 1) * HD],
                    preferred_element_type=jnp.float32,
                )
                for k in range(KVH)
            ],
            axis=0,
        )
        o_ref[r] = out / total
        lse_ref[r] = top + jnp.log(total)


def attend_cache(lengths, q, kv_cache):
    rows, heads2, _ = q.shape
    cached, width = kv_cache.shape[1:]
    block = min(4, rows)
    return pl.pallas_call(
        cache_body,
        grid=(rows // block,),
        in_specs=[
            pl.BlockSpec(memory_space=pltpu.SMEM),
            pl.BlockSpec((block, heads2, HD), lambda i: (i, 0, 0)),
            pl.BlockSpec((block, cached, width), lambda i: (i, 0, 0)),
        ],
        out_specs=(
            pl.BlockSpec((block, heads2, HD), lambda i: (i, 0, 0)),
            pl.BlockSpec((block, heads2, 1), lambda i: (i, 0, 0)),
        ),
        out_shape=(
            jax.ShapeDtypeStruct((rows, heads2, HD), jnp.float32),
            jax.ShapeDtypeStruct((rows, heads2, 1), jnp.float32),
        ),
        cost_estimate=pl.CostEstimate(
            flops=4 * rows * heads2 * cached * HD,
            bytes_accessed=kv_cache.size * 2,
            transcendentals=rows * heads2 * cached,
        ),
        compiler_params=pltpu.CompilerParams(vmem_limit_bytes=VMEM_LIMIT),
        name="attend_cache",
    )(lengths, q, kv_cache)


def join_body(q_ref, o_ref, lse_ref, k_ref, v_ref, out_ref):
    block = q_ref.shape[0]
    pairs = 2 * KVH
    shape = (2 * HEADS, pairs)
    row = lax.broadcasted_iota(jnp.int32, shape, 0)
    col = lax.broadcasted_iota(jnp.int32, shape, 1)
    live = (row // (2 * GROUP) == col % KVH) & (col // KVH <= (row // GROUP) % 2)
    scale = 1.0 / math.sqrt(HD)
    for r in range(block):
        scores = lax.dot_general(
            q_ref[r], k_ref[r], (((1,), (1,)), ((), ())), preferred_element_type=jnp.float32
        ) * scale
        scores = jnp.where(live, scores, NEG)
        lse = lse_ref[r]
        top = jnp.maximum(jnp.max(scores, axis=1, keepdims=True), lse)
        expo = jnp.exp(scores - top)
        before = jnp.exp(lse - top)
        total = before + jnp.sum(expo, axis=1, keepdims=True)
        out = o_ref[r] * before + jnp.dot(
            expo.astype(jnp.bfloat16), v_ref[r], preferred_element_type=jnp.float32
        )
        out_ref[r] = (out / total).astype(jnp.bfloat16)


def attend_join(q, o, lse, new_keys, new_vals):
    rows, heads2, _ = q.shape
    pairs = new_keys.shape[1]
    block = min(8, rows)

    def spec(second, last):
        return pl.BlockSpec((block, second, last), lambda i: (i, 0, 0))

    return pl.pallas_call(
        join_body,
        grid=(rows // block,),
        in_specs=[
            spec(heads2, HD), spec(heads2, HD), spec(heads2, 1), spec(pairs, HD), spec(pairs, HD),
        ],
        out_specs=spec(heads2, HD),
        out_shape=jax.ShapeDtypeStruct((rows, heads2, HD), jnp.bfloat16),
        compiler_params=pltpu.CompilerParams(vmem_limit_bytes=VMEM_LIMIT),
        name="attend_join",
    )(q, o, lse, new_keys, new_vals)


def scatter_sum(partial, tensor):
    steps, rows, columns = partial.shape
    shard = rows // tensor
    me = lax.axis_index("tensor")

    def block(at):
        return lax.dynamic_slice_in_dim(partial, at * shard, shard, 1)

    total = block(me).astype(jnp.float32)
    for shift in range(1, tensor):
        pairs = [(i, (i + shift) % tensor) for i in range(tensor)]
        sent = lax.ppermute(block((me + shift) % tensor), "tensor", pairs)
        total = total + sent.astype(jnp.float32)
    return total


def local(
    replicas,
    tensor,
    hidden,
    base_weight,
    delta_values,
    delta_scales,
    tenant_slot,
    seg_tenant,
    seg_length,
    queries,
    kv_cache,
    cache_length,
):
    def swap(value, mask):
        return lax.ppermute(value, "replica", [(i, i ^ mask) for i in range(replicas)])

    first = (lax.axis_index("replica") * SLOTS).reshape(1)
    meta = jnp.concatenate([seg_tenant, seg_length], axis=1)
    meta = jnp.concatenate([meta, swap(meta, 1)], axis=0)
    sibling = swap(hidden, 1)
    far = []
    for mask in range(2, replicas, 2):
        far.append((mask, swap(meta, mask), [swap(hidden[s:s + 1], mask) for s in range(2)]))

    own, other = delta_rows(
        first, meta, tenant_slot, hidden, sibling, delta_values, delta_scales, base_weight
    )
    own = own + swap(other, 1).astype(jnp.float32)

    steps = [own[0:1], own[1:2]]
    for mask, far_meta, chunks in far:
        for s, chunk in enumerate(chunks):
            chunk_sibling = swap(chunk, 1)
            mine, theirs = delta_rows(
                first, far_meta, tenant_slot, chunk, chunk_sibling, delta_values, delta_scales
            )
            both = mine + swap(theirs, 1)
            steps[s] = steps[s] + swap(both, mask).astype(jnp.float32)

    shard_rows = queries.shape[1]
    q = queries.reshape(2, shard_rows, KVH, GROUP, HD).transpose(1, 2, 0, 3, 4)
    q = q.reshape(shard_rows, 2 * HEADS, HD)
    cache_out, cache_lse = attend_cache(cache_length, q, kv_cache)

    if tensor <= 4:
        sums = [scatter_sum(part.astype(jnp.bfloat16), tensor) for part in steps]
    else:
        sums = [
            lax.psum_scatter(part, "tensor", scatter_dimension=1, tiled=True) for part in steps
        ]
    new_kv = jnp.concatenate([part.astype(jnp.bfloat16) for part in sums], axis=0)
    split = new_kv.reshape(2, shard_rows, 2, KVH, HD).transpose(2, 1, 0, 3, 4)
    split = split.reshape(2, shard_rows, 2 * KVH, HD)
    joined = attend_join(q, cache_out, cache_lse, split[0], split[1])
    attention = joined.reshape(shard_rows, KVH, 2, GROUP, HD).transpose(2, 0, 1, 3, 4)
    return (new_kv, attention.reshape(2, shard_rows, HEADS * HD))


def solution(mesh):
    placed = (
        P(None, ("groups", "replica"), "tensor"),
        P("tensor", None),
        P(("groups", "replica"), "tensor", None),
        P(("groups", "replica"), "tensor", None),
        P(),
        P(("groups", "replica"), None),
        P(("groups", "replica"), None),
        P(None, ("groups", "replica", "tensor"), None),
        P(("groups", "replica", "tensor"), None, None),
        P(("groups", "replica", "tensor")),
    )
    return jax.shard_map(
        functools.partial(local, mesh.shape["replica"], mesh.shape["tensor"]),
        mesh=mesh,
        in_specs=placed,
        out_specs=(
            P(None, ("groups", "replica", "tensor"), None),
            P(None, ("groups", "replica", "tensor"), None),
        ),
        check_vma=False,
    )
```

time: 606 us -> 153 us (0.25)
  waiting for transfers between devices: 336 us -> 57.8 us
  blocking collectives: 88 us -> 0 us
  matrix products: 58.4 us -> 0 us
  Pallas kernels: 0 us -> 57.9 us
  other arithmetic: 55.7 us -> 4.41 us
  local copies, waits for them, and re-layouts: 51.7 us -> 10.8 us
  starting transfers between devices: 0.04 us -> 20.3 us
  between operations: 14.2 us -> 0.88 us
    all_gather x1 -> x0, waiting for transfers between devices: 336 us -> none  [local(): lax.all_gather(delta_values, 'replica', axis=0, tiled=True)]
    psum x1 -> x0, blocking collectives: 79.4 us -> none  [local(): summed = lax.psum(partial_kv, 'tensor')]
    dot_general x6 -> x0, matrix products: 58.4 us -> none  [the longest x1 30.3 us: local(): jnp.einsum('rd,kdc->krc', flat_x, weights, preferred_element_type=jnp.flo...]
    pallas_call x0 -> x5, Pallas kernels: none -> 57.9 us  [the longest x3 38 us: delta_rows(): pl.pallas_call(functools.partial(delta_body, base is not None, steps, row...]
    ppermute x0 -> x18, waiting for transfers between devices: none -> 57.8 us  [the longest x12 45.7 us: swap(): lax.ppermute(value, 'replica', [(i, i ^ mask) for i in range(replicas)])]
    convert_element_type x2 -> x3, other arithmetic: 45.6 us -> 0.42 us  [the longest x1 0.28 us: local(): sums = [scatter_sum(part.astype(jnp.bfloat16), tensor) for part in steps]]
    ppermute x0 -> x18, starting transfers between devices: none -> 20.3 us  [the longest x6 12.1 us: scatter_sum(): sent = lax.ppermute(block((me + shift) % tensor), 'tensor', pairs)]
    unnamed x25 -> x32, local copies, waits for them, and re-layouts: 27.7 us -> 7.68 us
  transfers between devices with their start and end apart: 1 -> 18, of which waited for: 1 -> 9; matrix products, arithmetic and copies ran while one was open for 9% -> 4% of each run, Pallas kernels for 0% -> 34%
where the time goes in v1:
time: 153 us; the launch traced here: 152 us
  Pallas kernels  57.9 us (38%)
  waiting for transfers between devices  57.8 us (38%)
  starting transfers between devices  20.3 us (13%)
  local copies, waits for them, and re-layouts  10.8 us (7%)
  other arithmetic  4.41 us (3%)
    ppermute x12, waiting for transfers between devices, swap(): lax.ppermute(value, 'replica', [(i, i ^ mask) for i in range(replicas)])  45.7 us
    pallas_call x3, Pallas kernels, delta_rows(): pl.pallas_call(functools.partial(delta_body, base is not None, steps, row...  38 us
    pallas_call x1, Pallas kernels, attend_cache(): pl.pallas_call(cache_body, grid=(rows // block,), in_specs=[pl.BlockSpec(...  13.9 us
    ppermute x6, waiting for transfers between devices, scatter_sum(): sent = lax.ppermute(block((me + shift) % tensor), 'tensor', pairs)  12.1 us
    ppermute x6, starting transfers between devices, scatter_sum(): sent = lax.ppermute(block((me + shift) % tensor), 'tensor', pairs)  12.1 us
    ppermute x12, starting transfers between devices, swap(): lax.ppermute(value, 'replica', [(i, i ^ mask) for i in range(replicas)])  8.25 us
    unnamed x32, local copies, waits for them, and re-layouts  7.68 us
    pallas_call x1, Pallas kernels, attend_join(): pl.pallas_call(join_body, grid=(rows // block,), in_specs=[spec(heads2, H...  6.05 us
  transfers between devices with their start and end apart: 18, of which 9 were waited for; matrix products, arithmetic and copies ran while one was open for 4% of the time, Pallas kernels for 34%

profile of v1, /device:TPU:0, one launch (start us, length us, event | category | flops | bytes accessed | tf_op | source)
XLA Modules:
  0.0 152.2 jit_solution(8914963765937048253)
XLA Ops:
  1.2 1.3 fusion.2
  2.5 2.7 %collective-permute-start.11 = (bf16[1,128,2048]{2,1,0:T(8,128)(2,1)S(1)}, bf16[1,128,2048]{2,1,0:T(8,128)(2,1)}, u32[]{:S(2)}, u32[]{:S(2)}) collective-permute-start(bf16[1,128,2048]{2,1,0:T(8,128)(2,1)S(1)} %get-tuple-element.21), channel_id=1, source_target_pairs={{0,2},{1,3},{2,0},{3,1},{4,6},{5,7},{6,4},{7,5},{8,10},{9,11},{10,... | collective-permute-start | bytes 1572872 | tf_op jit(solution)/shard_map/ppermute | solution.py:285
  6.5 11.5 %collective-permute-done.11.refs_3_ = bf16[1,128,2048]{2,1,0:T(8,128)(2,1)} collective-permute-done((bf16[1,128,2048]{2,1,0:T(8,128)(2,1)S(1)}, bf16[1,128,2048]{2,1,0:T(8,128)(2,1)}, u32[]{:S(2)}, u32[]{:S(2)}) %collective-permute-start.11) | collective-permute-done | bytes 524320 | tf_op jit(solution)/shard_map/ppermute | solution.py:285
  18.0 10.9 %collective-permute-done.4.refs_3_ = bf16[1,128,2048]{2,1,0:T(8,128)(2,1)} collective-permute-done((bf16[1,128,2048]{2,1,0:T(8,128)(2,1)S(1)}, bf16[1,128,2048]{2,1,0:T(8,128)(2,1)}, u32[]{:S(2)}, u32[]{:S(2)}) %collective-permute-start.4) | collective-permute-done | bytes 524320 | tf_op jit(solution)/shard_map/ppermute | solution.py:285
  30.0 3.4 %copy-done = bf16[2048,2048]{1,0:T(8,128)(2,1)S(1)} copy-done((bf16[2048,2048]{1,0:T(8,128)(2,1)S(1)}, bf16[2048,2048]{1,0:T(8,128)(2,1)}, u32[]{:S(2)}) %copy-start) | copy-done | bytes 8388632
  33.3 1.2 copy-done.4
  34.6 14.2 %delta_rows.3 = (f32[2,128,2048]{2,1,0:T(8,128)S(1)}, bf16[2,128,2048]{2,1,0:T(8,128)(2,1)}) custom-call(s32[1]{0:T(128)} %bitcast.refs_0_, s32[2,8]{1,0:T(2,128)S(1)} %pad_add_fusion.refs_1_, s32[8]{0:T(128)S(1)} %copy-done.9, bf16[2,128,2048]{2,1,0:T(8,128)(2,1)S(1)} %copy-done.1, bf16[2,128,2048]{2,1,0:T(8,128)(2,1)S(1)} %copy-done.4, ...), custom_call_target="tpu_custom_call" | custom-call | flops 4831838208 | bytes 25165824 | tf_op jit(solution)/shard_map/delta_rows/pallas_call | solution.py:118
  49.2 1.8 %collective-permute-start.3 = (s32[2,8]{1,0:T(2,128)S(1)}, s32[2,8]{1,0:T(2,128)S(1)}, u32[]{:S(2)}, u32[]{:S(2)}) collective-permute-start(s32[2,8]{1,0:T(2,128)S(1)} %pad_add_fusion.refs_1_), channel_id=1, source_target_pairs={{0,2},{1,3},{2,0},{3,1},{4,6},{5,7},{6,4},{7,5},{8,10},{9,11},{10,... | collective-permute-start | bytes 200 | tf_op jit(solution)/shard_map/ppermute | solution.py:285
  51.0 1.8 %collective-permute-done.3.refs_1_ = s32[2,8]{1,0:T(2,128)S(1)} collective-permute-done((s32[2,8]{1,0:T(2,128)S(1)}, s32[2,8]{1,0:T(2,128)S(1)}, u32[]{:S(2)}, u32[]{:S(2)}) %collective-permute-start.3) | collective-permute-done | bytes 96 | tf_op jit(solution)/shard_map/ppermute | solution.py:285
  52.8 11.9 %delta_rows.5 = (bf16[1,128,2048]{2,1,0:T(8,128)(2,1)S(1)}, bf16[1,128,2048]{2,1,0:T(8,128)(2,1)}) custom-call(s32[1]{0:T(128)} %bitcast.refs_0_, s32[2,8]{1,0:T(2,128)S(1)} %collective-permute-done.3.refs_1_, s32[8]{0:T(128)S(1)} %copy-done.9, bf16[1,128,2048]{2,1,0:T(8,128)(2,1)} %collective-permute-done.11.refs_3_, ...), custom_call_target="tpu_custom_call" | custom-call | flops 1342177280 | bytes 16777216 | tf_op jit(solution)/shard_map/delta_rows/pallas_call | solution.py:118
  65.5 12.0 %delta_rows.4 = (bf16[1,128,2048]{2,1,0:T(8,128)(2,1)S(1)}, bf16[1,128,2048]{2,1,0:T(8,128)(2,1)}) custom-call(s32[1]{0:T(128)} %bitcast.refs_0_, s32[2,8]{1,0:T(2,128)S(1)} %collective-permute-done.3.refs_1_, s32[8]{0:T(128)S(1)} %copy-done.9, bf16[1,128,2048]{2,1,0:T(8,128)(2,1)} %collective-permute-done.4.refs_3_, ...), custom_call_target="tpu_custom_call" | custom-call | flops 1342177280 | bytes 16777216 | tf_op jit(solution)/shard_map/delta_rows/pallas_call | solution.py:118
  79.3 13.9 %attend_cache.1 = (f32[32,128,128]{2,1,0:T(8,128)S(1)}, f32[32,128,1]{2,1,0:T(8,128)S(1)}) custom-call(s32[32]{0:T(128)S(1)} %copy-done.10, bf16[32,128,128]{2,1,0:T(8,128)(2,1)S(1)} %bitcast.24, bf16[32,128,2048]{2,1,0:T(8,128)(2,1)} %kv_ref.1), custom_call_target="tpu_custom_call" | custom-call | flops 268435456 | bytes 16777216 | tf_op jit(solution)/shard_map/attend_cache/pallas_call | solution.py:183
  93.2 1.2 add.90
  94.4 1.8 %collective-permute-start.14 = (bf16[1,128,2048]{2,1,0:T(8,128)(2,1)S(1)}, bf16[1,128,2048]{2,1,0:T(8,128)(2,1)S(1)}, u32[]{:S(2)}, u32[]{:S(2)}) collective-permute-start(bf16[1,128,2048]{2,1,0:T(8,128)(2,1)S(1)} %add.90), channel_id=1, source_target_pairs={{0,2},{1,3},{2,0},{3,1},{4,6},{5,7},{6,4},{7,5},{8,10},{9,11},{10,... | collective-permute-start | bytes 1572872 | tf_op jit(solution)/shard_map/ppermute | solution.py:285
  97.7 1.5 convert_add_fusion
  99.2 10.0 %collective-permute-done.14 = bf16[1,128,2048]{2,1,0:T(8,128)(2,1)S(1)} collective-permute-done((bf16[1,128,2048]{2,1,0:T(8,128)(2,1)S(1)}, bf16[1,128,2048]{2,1,0:T(8,128)(2,1)S(1)}, u32[]{:S(2)}, u32[]{:S(2)}) %collective-permute-start.14) | collective-permute-done | bytes 524320 | tf_op jit(solution)/shard_map/ppermute | solution.py:285
  109.2 10.4 %collective-permute-done.7 = bf16[1,128,2048]{2,1,0:T(8,128)(2,1)S(1)} collective-permute-done((bf16[1,128,2048]{2,1,0:T(8,128)(2,1)S(1)}, bf16[1,128,2048]{2,1,0:T(8,128)(2,1)S(1)}, u32[]{:S(2)}, u32[]{:S(2)}) %collective-permute-start.7) | collective-permute-done | bytes 524320 | tf_op jit(solution)/shard_map/ppermute | solution.py:285
  120.0 3.9 %collective-permute-start.10 = (bf16[1,32,2048]{2,1,0:T(8,128)(2,1)S(1)}, bf16[1,32,2048]{2,1,0:T(8,128)(2,1)S(1)}, u32[]{:S(2)}, u32[]{:S(2)}) collective-permute-start(bf16[1,32,2048]{2,1,0:T(8,128)(2,1)S(1)} %get-tuple-element.23), channel_id=1, source_target_pairs={{0,12},{4,0},{8,4},{12,8},{1,13},{5,1},{9,5},{13,9},{2,14},{6,2},{... | collective-permute-start | bytes 393224 | tf_op jit(solution)/shard_map/ppermute | solution.py:265
  124.9 3.4 %collective-permute-start.15 = (bf16[1,32,2048]{2,1,0:T(8,128)(2,1)S(1)}, bf16[1,32,2048]{2,1,0:T(8,128)(2,1)S(1)}, u32[]{:S(2)}, u32[]{:S(2)}) collective-permute-start(bf16[1,32,2048]{2,1,0:T(8,128)(2,1)S(1)} %get-tuple-element.25), channel_id=1, source_target_pairs={{0,4},{4,8},{8,12},{12,0},{1,5},{5,9},{9,13},{13,1},{2,6},{6,10},{... | collective-permute-start | bytes 393224 | tf_op jit(solution)/shard_map/ppermute | solution.py:265
  128.4 3.8 %collective-permute-start.17 = (bf16[1,32,2048]{2,1,0:T(8,128)(2,1)S(1)}, bf16[1,32,2048]{2,1,0:T(8,128)(2,1)S(1)}, u32[]{:S(2)}, u32[]{:S(2)}) collective-permute-start(bf16[1,32,2048]{2,1,0:T(8,128)(2,1)S(1)} %get-tuple-element.26), channel_id=1, source_target_pairs={{0,12},{4,0},{8,4},{12,8},{1,13},{5,1},{9,5},{13,9},{2,14},{6,2},{... | collective-permute-start | bytes 393224 | tf_op jit(solution)/shard_map/ppermute | solution.py:265
  132.3 9.2 %collective-permute-done.9 = bf16[1,32,2048]{2,1,0:T(8,128)(2,1)S(1)} collective-permute-done((bf16[1,32,2048]{2,1,0:T(8,128)(2,1)S(1)}, bf16[1,32,2048]{2,1,0:T(8,128)(2,1)S(1)}, u32[]{:S(2)}, u32[]{:S(2)}) %collective-permute-start.9) | collective-permute-done | bytes 131104 | tf_op jit(solution)/shard_map/ppermute | solution.py:265
  141.6 2.7 %collective-permute-done.16 = bf16[1,32,2048]{2,1,0:T(8,128)(2,1)S(1)} collective-permute-done((bf16[1,32,2048]{2,1,0:T(8,128)(2,1)S(1)}, bf16[1,32,2048]{2,1,0:T(8,128)(2,1)S(1)}, u32[]{:S(2)}, u32[]{:S(2)}) %collective-permute-start.16) | collective-permute-done | bytes 131104 | tf_op jit(solution)/shard_map/ppermute | solution.py:265
  144.6 6.0 %attend_join.1 = bf16[32,128,128]{2,1,0:T(8,128)(2,1)S(1)} custom-call(bf16[32,128,128]{2,1,0:T(8,128)(2,1)S(1)} %bitcast.25, f32[32,128,128]{2,1,0:T(8,128)S(1)} %get-tuple-element.16.o_ref, f32[32,128,1]{2,1,0:T(8,128)S(1)} %get-tuple-element.17.lse_ref, bf16[32,16,128]{2,1,0:T(8,128)(2,1)S(1)} %get-tuple-element.29.k_ref, ...), custom_call_target="tpu_custom_call" | custom-call | tf_op jit(solution)/shard_map/attend_join/pallas_call | solution.py:241
  151.0 1.3 reshape.32
  (66 shorter events, 9.6 us)
Async XLA Ops:
  0.6 29.3 %copy-start.1 = (bf16[2,128,2048]{2,1,0:T(8,128)(2,1)S(1)}, bf16[2,128,2048]{2,1,0:T(8,128)(2,1)}, u32[]{:S(2)}) copy-start(bf16[2,128,2048]{2,1,0:T(8,128)(2,1)} %refs_3_.1) | copy-start | bytes 3145732
  0.7 29.3 %copy-start.2 = (bf16[2,16,2048]{2,1,0:T(8,128)(2,1)S(1)}, bf16[2,16,2048]{2,1,0:T(8,128)(2,1)}, u32[]{:S(2)}) copy-start(bf16[2,16,2048]{2,1,0:T(8,128)(2,1)} %refs_6_.5) | copy-start | bytes 393220
  0.7 29.3 %copy-start.9 = (s32[8]{0:T(128)S(1)}, s32[8]{0:T(128)}, u32[]{:S(2)}) copy-start(s32[8]{0:T(128)} %refs_2_.5) | copy-start | bytes 100
  0.7 28.3 %collective-permute-start.1 = (bf16[2,128,2048]{2,1,0:T(8,128)(2,1)}, bf16[2,128,2048]{2,1,0:T(8,128)(2,1)S(1)}, u32[]{:S(2)}, u32[]{:S(2)}) collective-permute-start(bf16[2,128,2048]{2,1,0:T(8,128)(2,1)} %refs_3_.1), channel_id=1, source_target_pairs={{0,1},{1,0},{2,3},{3,2},{4,5},{5,4},{6,7},{7,6},{8,9},{9,8},{10,11... | collective-permute-start | bytes 3145736 | tf_op jit(solution)/shard_map/ppermute | solution.py:285
  2.5 15.5 %collective-permute-start.11 = (bf16[1,128,2048]{2,1,0:T(8,128)(2,1)S(1)}, bf16[1,128,2048]{2,1,0:T(8,128)(2,1)}, u32[]{:S(2)}, u32[]{:S(2)}) collective-permute-start(bf16[1,128,2048]{2,1,0:T(8,128)(2,1)S(1)} %get-tuple-element.21), channel_id=1, source_target_pairs={{0,2},{1,3},{2,0},{3,1},{4,6},{5,7},{6,4},{7,5},{8,10},{9,11},{10,... | collective-permute-start | bytes 1572872 | tf_op jit(solution)/shard_map/ppermute | solution.py:285
  5.1 23.8 %collective-permute-start.4 = (bf16[1,128,2048]{2,1,0:T(8,128)(2,1)S(1)}, bf16[1,128,2048]{2,1,0:T(8,128)(2,1)}, u32[]{:S(2)}, u32[]{:S(2)}) collective-permute-start(bf16[1,128,2048]{2,1,0:T(8,128)(2,1)S(1)} %get-tuple-element.20), channel_id=1, source_target_pairs={{0,2},{1,3},{2,0},{3,1},{4,6},{5,7},{6,4},{7,5},{8,10},{9,11},{10,... | collective-permute-start | bytes 1572872 | tf_op jit(solution)/shard_map/ppermute | solution.py:285
  5.3 1.1 collective-permute-start
  18.0 34.8 %collective-permute-start.12 = (bf16[1,128,2048]{2,1,0:T(8,128)(2,1)}, bf16[1,128,2048]{2,1,0:T(8,128)(2,1)S(1)}, u32[]{:S(2)}, u32[]{:S(2)}) collective-permute-start(bf16[1,128,2048]{2,1,0:T(8,128)(2,1)} %collective-permute-done.11.refs_3_), channel_id=1, source_target_pairs={{0,1},{1,0},{2,3},{3,2},{4,5},{5,4},{6,7},{7,6},{8,9},{9,8},{10,11... | collective-permute-start | bytes 1572872 | tf_op jit(solution)/shard_map/ppermute | solution.py:285
  29.0 36.5 %collective-permute-start.5 = (bf16[1,128,2048]{2,1,0:T(8,128)(2,1)}, bf16[1,128,2048]{2,1,0:T(8,128)(2,1)S(1)}, u32[]{:S(2)}, u32[]{:S(2)}) collective-permute-start(bf16[1,128,2048]{2,1,0:T(8,128)(2,1)} %collective-permute-done.4.refs_3_), channel_id=1, source_target_pairs={{0,1},{1,0},{2,3},{3,2},{4,5},{5,4},{6,7},{7,6},{8,9},{9,8},{10,11... | collective-permute-start | bytes 1572872 | tf_op jit(solution)/shard_map/ppermute | solution.py:285
  48.7 49.0 %collective-permute-start.2 = (bf16[2,128,2048]{2,1,0:T(8,128)(2,1)}, bf16[2,128,2048]{2,1,0:T(8,128)(2,1)}, u32[]{:S(2)}, u32[]{:S(2)}) collective-permute-start(bf16[2,128,2048]{2,1,0:T(8,128)(2,1)} %get-tuple-element.11), channel_id=1, source_target_pairs={{0,1},{1,0},{2,3},{3,2},{4,5},{5,4},{6,7},{7,6},{8,9},{9,8},{10,11... | collective-permute-start | bytes 3145736 | tf_op jit(solution)/shard_map/ppermute | solution.py:285
  49.2 3.6 %collective-permute-start.3 = (s32[2,8]{1,0:T(2,128)S(1)}, s32[2,8]{1,0:T(2,128)S(1)}, u32[]{:S(2)}, u32[]{:S(2)}) collective-permute-start(s32[2,8]{1,0:T(2,128)S(1)} %pad_add_fusion.refs_1_), channel_id=1, source_target_pairs={{0,2},{1,3},{2,0},{3,1},{4,6},{5,7},{6,4},{7,5},{8,10},{9,11},{10,... | collective-permute-start | bytes 200 | tf_op jit(solution)/shard_map/ppermute | solution.py:285
  65.5 13.2 %copy-start.11 = (bf16[2,32,8192]{2,1,0:T(8,128)(2,1)S(1)}, bf16[2,32,8192]{2,1,0:T(8,128)(2,1)}, u32[]{:S(2)}) copy-start(bf16[2,32,8192]{2,1,0:T(8,128)(2,1)} %param.17) | copy-start | bytes 3145732
  65.5 27.7 %collective-permute-start.13 = (bf16[1,128,2048]{2,1,0:T(8,128)(2,1)}, bf16[1,128,2048]{2,1,0:T(8,128)(2,1)}, u32[]{:S(2)}, u32[]{:S(2)}) collective-permute-start(bf16[1,128,2048]{2,1,0:T(8,128)(2,1)} %get-tuple-element.15), channel_id=1, source_target_pairs={{0,1},{1,0},{2,3},{3,2},{4,5},{5,4},{6,7},{7,6},{8,9},{9,8},{10,11... | collective-permute-start | bytes 1572872 | tf_op jit(solution)/shard_map/ppermute | solution.py:285
  78.3 18.0 %collective-permute-start.6 = (bf16[1,128,2048]{2,1,0:T(8,128)(2,1)}, bf16[1,128,2048]{2,1,0:T(8,128)(2,1)}, u32[]{:S(2)}, u32[]{:S(2)}) collective-permute-start(bf16[1,128,2048]{2,1,0:T(8,128)(2,1)} %get-tuple-element.13), channel_id=1, source_target_pairs={{0,1},{1,0},{2,3},{3,2},{4,5},{5,4},{6,7},{7,6},{8,9},{9,8},{10,11... | collective-permute-start | bytes 1572872 | tf_op jit(solution)/shard_map/ppermute | solution.py:285
  79.3 13.9 %copy-start.6 = (bf16[1,128,2048]{2,1,0:T(8,128)(2,1)S(1)}, bf16[1,128,2048]{2,1,0:T(8,128)(2,1)}, u32[]{:S(2)}) copy-start(bf16[1,128,2048]{2,1,0:T(8,128)(2,1)} %copy-done.5) | copy-start | bytes 1572868
  79.3 16.9 %copy-start.8 = (bf16[1,128,2048]{2,1,0:T(8,128)(2,1)S(1)}, bf16[1,128,2048]{2,1,0:T(8,128)(2,1)}, u32[]{:S(2)}) copy-start(bf16[1,128,2048]{2,1,0:T(8,128)(2,1)} %copy-done.7) | copy-start | bytes 1572868
  94.4 14.8 %collective-permute-start.14 = (bf16[1,128,2048]{2,1,0:T(8,128)(2,1)S(1)}, bf16[1,128,2048]{2,1,0:T(8,128)(2,1)S(1)}, u32[]{:S(2)}, u32[]{:S(2)}) collective-permute-start(bf16[1,128,2048]{2,1,0:T(8,128)(2,1)S(1)} %add.90), channel_id=1, source_target_pairs={{0,2},{1,3},{2,0},{3,1},{4,6},{5,7},{6,4},{7,5},{8,10},{9,11},{10,... | collective-permute-start | bytes 1572872 | tf_op jit(solution)/shard_map/ppermute | solution.py:285
  97.4 22.3 %collective-permute-start.7 = (bf16[1,128,2048]{2,1,0:T(8,128)(2,1)S(1)}, bf16[1,128,2048]{2,1,0:T(8,128)(2,1)S(1)}, u32[]{:S(2)}, u32[]{:S(2)}) collective-permute-start(bf16[1,128,2048]{2,1,0:T(8,128)(2,1)S(1)} %add.75), channel_id=1, source_target_pairs={{0,2},{1,3},{2,0},{3,1},{4,6},{5,7},{6,4},{7,5},{8,10},{9,11},{10,... | collective-permute-start | bytes 1572872 | tf_op jit(solution)/shard_map/ppermute | solution.py:285
  120.0 8.4 %collective-permute-start.10 = (bf16[1,32,2048]{2,1,0:T(8,128)(2,1)S(1)}, bf16[1,32,2048]{2,1,0:T(8,128)(2,1)S(1)}, u32[]{:S(2)}, u32[]{:S(2)}) collective-permute-start(bf16[1,32,2048]{2,1,0:T(8,128)(2,1)S(1)} %get-tuple-element.23), channel_id=1, source_target_pairs={{0,12},{4,0},{8,4},{12,8},{1,13},{5,1},{9,5},{13,9},{2,14},{6,2},{... | collective-permute-start | bytes 393224 | tf_op jit(solution)/shard_map/ppermute | solution.py:265
  123.9 8.4 %collective-permute-start.8 = (bf16[1,32,2048]{2,1,0:T(8,128)(2,1)S(1)}, bf16[1,32,2048]{2,1,0:T(8,128)(2,1)S(1)}, u32[]{:S(2)}, u32[]{:S(2)}) collective-permute-start(bf16[1,32,2048]{2,1,0:T(8,128)(2,1)S(1)} %get-tuple-element.22), channel_id=1, source_target_pairs={{0,4},{4,8},{8,12},{12,0},{1,5},{5,9},{9,13},{13,1},{2,6},{6,10},{... | collective-permute-start | bytes 393224 | tf_op jit(solution)/shard_map/ppermute | solution.py:265
  123.9 17.6 %collective-permute-start.9 = (bf16[1,32,2048]{2,1,0:T(8,128)(2,1)S(1)}, bf16[1,32,2048]{2,1,0:T(8,128)(2,1)S(1)}, u32[]{:S(2)}, u32[]{:S(2)}) collective-permute-start(bf16[1,32,2048]{2,1,0:T(8,128)(2,1)S(1)} %get-tuple-element.24), channel_id=1, source_target_pairs={{0,8},{4,12},{8,0},{12,4},{1,9},{5,13},{9,1},{13,5},{2,10},{6,14},... | collective-permute-start | bytes 393224 | tf_op jit(solution)/shard_map/ppermute | solution.py:265
  124.9 16.7 %collective-permute-start.15 = (bf16[1,32,2048]{2,1,0:T(8,128)(2,1)S(1)}, bf16[1,32,2048]{2,1,0:T(8,128)(2,1)S(1)}, u32[]{:S(2)}, u32[]{:S(2)}) collective-permute-start(bf16[1,32,2048]{2,1,0:T(8,128)(2,1)S(1)} %get-tuple-element.25), channel_id=1, source_target_pairs={{0,4},{4,8},{8,12},{12,0},{1,5},{5,9},{9,13},{13,1},{2,6},{6,10},{... | collective-permute-start | bytes 393224 | tf_op jit(solution)/shard_map/ppermute | solution.py:265
  128.4 16.0 %collective-permute-start.16 = (bf16[1,32,2048]{2,1,0:T(8,128)(2,1)S(1)}, bf16[1,32,2048]{2,1,0:T(8,128)(2,1)S(1)}, u32[]{:S(2)}, u32[]{:S(2)}) collective-permute-start(bf16[1,32,2048]{2,1,0:T(8,128)(2,1)S(1)} %get-tuple-element.27), channel_id=1, source_target_pairs={{0,8},{4,12},{8,0},{12,4},{1,9},{5,13},{9,1},{13,5},{2,10},{6,14},... | collective-permute-start | bytes 393224 | tf_op jit(solution)/shard_map/ppermute | solution.py:265
  128.4 16.0 %collective-permute-start.17 = (bf16[1,32,2048]{2,1,0:T(8,128)(2,1)S(1)}, bf16[1,32,2048]{2,1,0:T(8,128)(2,1)S(1)}, u32[]{:S(2)}, u32[]{:S(2)}) collective-permute-start(bf16[1,32,2048]{2,1,0:T(8,128)(2,1)S(1)} %get-tuple-element.26), channel_id=1, source_target_pairs={{0,12},{4,0},{8,4},{12,8},{1,13},{5,1},{9,5},{13,9},{2,14},{6,2},{... | collective-permute-start | bytes 393224 | tf_op jit(solution)/shard_map/ppermute | solution.py:265
  (9 other events, 23.2 us)

commit v2 on v1

v2 whole, which is shorter than its diff:
```python
import functools
import math

import jax
import jax.numpy as jnp
from jax import lax
from jax.experimental import pallas as pl
from jax.experimental.pallas import tpu as pltpu
from jax.sharding import PartitionSpec as P

HEADS = 64
KVH = 8
HD = 128
GROUP = HEADS // KVH
KEYS = KVH * HD
BLOCK = 128
SEG_MOST = 40
SLOTS = 2
NEG = -1e30
VMEM_LIMIT = 52 * 1024 * 1024
LIGHT = pl.CostEstimate(flops=1, bytes_accessed=1, transcendentals=0)
COVER = pl.CostEstimate(flops=1 << 34, bytes_accessed=1 << 26, transcendentals=0)


def row_positions(meta_ref, slot_ref, first, steps, rows, shape, axis):
    index = lax.broadcasted_iota(jnp.int32, shape, axis)
    source = index // (steps * rows)
    step = (index // rows) % steps
    row = index % rows
    per_slot = 2 * steps * SEG_MOST
    place = jnp.full(shape, -1, jnp.int32)
    for src in range(2):
        begin = jnp.int32(0)
        for seg in range(meta_ref.shape[1] // 2):
            slot = slot_ref[meta_ref[src, seg]] - first
            length = meta_ref[src, meta_ref.shape[1] // 2 + seg]
            end = begin + length
            held = jnp.logical_and(slot >= 0, slot < SLOTS)
            offset = jnp.where(held, slot * per_slot + src * steps * SEG_MOST - begin, -(1 << 20))
            inside = (source == src) & (row >= begin) & (row < end)
            place = jnp.where(inside, offset + step * SEG_MOST + row, place)
            begin = end
    return place


def delta_body(with_base, chunks, steps, rows, *refs):
    first_ref, meta_ref, slot_ref = refs[:3]
    xa_refs, xb_refs = refs[3:3 + chunks], refs[3 + chunks:3 + 2 * chunks]
    val_ref, sc_ref = refs[3 + 2 * chunks:5 + 2 * chunks]
    da_ref, db_ref, xc_ref, scatter_ref = refs[-4:]
    width = val_ref.shape[1]
    tile = val_ref.shape[2]
    half = steps * rows
    taken = SLOTS * 2 * steps * SEG_MOST
    per_slot = taken // SLOTS

    @pl.when(pl.program_id(0) == 0)
    def _():
        first = first_ref[0]
        along = row_positions(meta_ref, slot_ref, first, steps, rows, (1, 2 * half), 1)
        picks = (lax.broadcasted_iota(jnp.int32, (taken, 2 * half), 0) == along).astype(jnp.bfloat16)
        down = row_positions(meta_ref, slot_ref, first, steps, rows, (2 * half, 1), 0)
        scatter_ref[...] = (
            lax.broadcasted_iota(jnp.int32, (2 * half, taken), 1) == down
        ).astype(jnp.bfloat16)
        begin = 0
        got = jnp.zeros(xc_ref.shape, jnp.float32)
        for xa_ref, xb_ref in zip(xa_refs, xb_refs):
            end = begin + xa_ref.shape[0]
            got += jnp.dot(picks[:, begin:end], xa_ref[...], preferred_element_type=jnp.float32)
            got += jnp.dot(
                picks[:, half + begin:half + end], xb_ref[...], preferred_element_type=jnp.float32
            )
            begin = end
        xc_ref[...] = got.astype(jnp.bfloat16)

    parts = []
    for slot in range(SLOTS):
        scaled = [
            val_ref[slot, b * BLOCK:(b + 1) * BLOCK, :] * sc_ref[slot, b:b + 1, :]
            for b in range(width // BLOCK)
        ]
        weight = jnp.concatenate(scaled, axis=0)
        parts.append(
            jnp.dot(
                xc_ref[slot * per_slot:(slot + 1) * per_slot, :], weight,
                preferred_element_type=jnp.float32,
            ).astype(jnp.bfloat16)
        )
    spread = jnp.dot(
        scatter_ref[...], jnp.concatenate(parts, axis=0), preferred_element_type=jnp.float32
    )
    own = spread[:half]
    if with_base:
        own = own + jnp.dot(
            xa_refs[0][...], refs[-5][...], preferred_element_type=jnp.float32
        )
    da_ref[...] = own.reshape(steps, rows, tile).astype(da_ref.dtype)
    db_ref[...] = spread[half:].reshape(steps, rows, tile).astype(db_ref.dtype)


def delta_rows(first, meta, slots, xa, xb, values, scales, base=None, start=0, columns=None):
    steps = 2
    rows = sum(x.shape[0] for x in xa) // steps
    width = values.shape[1]
    columns = columns or values.shape[2]
    tile = min(512, columns)
    skip = start // tile
    smem = pl.BlockSpec(memory_space=pltpu.SMEM)
    in_specs = [smem, smem, smem]
    in_specs += [pl.BlockSpec(x.shape, lambda i: (0, 0)) for x in (*xa, *xb)]
    in_specs += [
        pl.BlockSpec((SLOTS, width, tile), lambda i: (0, 0, i + skip)),
        pl.BlockSpec((SLOTS, width // BLOCK, tile), lambda i: (0, 0, i + skip)),
    ]
    args = [first, meta, slots, *xa, *xb, values, scales]
    if base is not None:
        in_specs.append(pl.BlockSpec((width, tile), lambda i: (0, i + skip)))
        args.append(base)
    out = pl.BlockSpec((steps, rows, tile), lambda i: (0, 0, i))
    taken = SLOTS * 2 * steps * SEG_MOST
    return pl.pallas_call(
        functools.partial(delta_body, base is not None, len(xa), steps, rows),
        grid=(columns // tile,),
        in_specs=in_specs,
        out_specs=(out, out),
        out_shape=(
            jax.ShapeDtypeStruct(
                (steps, rows, columns), jnp.bfloat16
            ),
            jax.ShapeDtypeStruct((steps, rows, columns), jnp.bfloat16),
        ),
        scratch_shapes=[
            pltpu.VMEM((taken, width), jnp.bfloat16),
            pltpu.VMEM((2 * steps * rows, taken), jnp.bfloat16),
        ],
        cost_estimate=LIGHT,
        compiler_params=pltpu.CompilerParams(vmem_limit_bytes=VMEM_LIMIT),
        name="delta_rows",
    )(*args)


def head_rows(ref, r):
    some = 2 * GROUP
    return jnp.concatenate(
        [ref[s, r, p * some:(p + 1) * some, :] for p in range(KVH // 2) for s in range(2)], axis=0
    )


def cache_body(start, len_ref, q_ref, kv_ref, *refs):
    o_ref, lse_ref = refs[-2:]
    block = q_ref.shape[1]
    cached = kv_ref.shape[1]
    some = 4 * GROUP
    scale = 1.0 / math.sqrt(HD)
    position = lax.broadcasted_iota(jnp.int32, (2 * HEADS, cached), 1)
    wide = (some, 2 * HD)
    diagonal = (lax.broadcasted_iota(jnp.int32, wide, 0) // GROUP) % 2 == (
        lax.broadcasted_iota(jnp.int32, wide, 1) // HD
    )
    first = (lax.broadcasted_iota(jnp.int32, (some, HD), 0) // GROUP) % 2 == 0
    scores = []
    for r in range(block):
        rows = head_rows(q_ref, r)
        parts = []
        for p in range(KVH // 2):
            q = rows[p * some:(p + 1) * some]
            q = jnp.concatenate([q, q], axis=1)
            q = jnp.where(diagonal, q, jnp.zeros_like(q))
            parts.append(
                lax.dot_general(
                    q, kv_ref[r, :, p * 2 * HD:(p + 1) * 2 * HD], (((1,), (1,)), ((), ())),
                    preferred_element_type=jnp.float32,
                )
            )
        one = jnp.concatenate(parts, axis=0) * scale
        length = len_ref[start + pl.program_id(0) * block + r]
        scores.append(jnp.where(position < length, one, NEG))
    scores = jnp.concatenate(scores, axis=0)
    top = jnp.max(scores, axis=1, keepdims=True)
    expo = jnp.exp(scores - top)
    total = jnp.sum(expo, axis=1, keepdims=True)
    lse = top + jnp.log(total)
    inverse = 1.0 / total
    expo = expo.astype(jnp.bfloat16)
    for r in range(block):
        base = r * 2 * HEADS
        parts = []
        for p in range(KVH // 2):
            out = jnp.dot(
                expo[base + p * some:base + (p + 1) * some],
                kv_ref[r, :, KEYS + p * 2 * HD:KEYS + (p + 1) * 2 * HD],
                preferred_element_type=jnp.float32,
            )
            parts.append(jnp.where(first, out[:, :HD], out[:, HD:]))
        o_ref[r] = jnp.concatenate(parts, axis=0) * inverse[base:base + 2 * HEADS]
        lse_ref[r] = lse[base:base + 2 * HEADS]


def attend_cache(lengths, q, kv_cache, start, count, before):
    rows = q.shape[1]
    cached, width = kv_cache.shape[1:]
    block = max(1, count // 2)
    skip = start // block
    any_spec = pl.BlockSpec(memory_space=pl.ANY)
    return pl.pallas_call(
        functools.partial(cache_body, start),
        grid=(count // block,),
        in_specs=[
            pl.BlockSpec(memory_space=pltpu.SMEM),
            pl.BlockSpec((2, block, HEADS, HD), lambda i: (0, i + skip, 0, 0)),
            pl.BlockSpec((block, cached, width), lambda i: (i + skip, 0, 0)),
            *[any_spec for _ in before],
        ],
        out_specs=(
            pl.BlockSpec((block, 2 * HEADS, HD), lambda i: (i + skip, 0, 0)),
            pl.BlockSpec((block, 2 * HEADS, 1), lambda i: (i + skip, 0, 0)),
        ),
        out_shape=(
            jax.ShapeDtypeStruct((rows, 2 * HEADS, HD), jnp.float32),
            jax.ShapeDtypeStruct((rows, 2 * HEADS, 1), jnp.float32),
        ),
        input_output_aliases={3 + i: i for i in range(len(before))},
        cost_estimate=COVER,
        compiler_params=pltpu.CompilerParams(vmem_limit_bytes=VMEM_LIMIT),
        name="attend_cache",
    )(lengths, q, kv_cache, *before)


def join_body(q_ref, o_ref, lse_ref, new_ref, out_ref):
    block = q_ref.shape[1]
    pairs = 2 * KVH
    shape = (2 * HEADS, pairs)
    row = lax.broadcasted_iota(jnp.int32, shape, 0)
    col = lax.broadcasted_iota(jnp.int32, shape, 1)
    head = row // (4 * GROUP) * 2 + (row // GROUP) % 2
    step = (row // (2 * GROUP)) % 2
    live = (head == col % KVH) & (col // KVH <= step)
    scale = 1.0 / math.sqrt(HD)
    scores = []
    for r in range(block):
        keys = jnp.concatenate([new_ref[s, r, :KVH, :] for s in range(2)], axis=0)
        one = lax.dot_general(
            head_rows(q_ref, r), keys.astype(jnp.bfloat16), (((1,), (1,)), ((), ())),
            preferred_element_type=jnp.float32,
        ) * scale
        scores.append(jnp.where(live, one, NEG))
    scores = jnp.concatenate(scores, axis=0)
    lse = lse_ref[...].reshape(block * 2 * HEADS, 1)
    top = jnp.maximum(jnp.max(scores, axis=1, keepdims=True), lse)
    expo = jnp.exp(scores - top)
    before = jnp.exp(lse - top)
    inverse = 1.0 / (before + jnp.sum(expo, axis=1, keepdims=True))
    before = before * inverse
    expo = (expo * inverse).astype(jnp.bfloat16)
    some = 2 * GROUP
    for r in range(block):
        rows = slice(r * 2 * HEADS, (r + 1) * 2 * HEADS)
        vals = jnp.concatenate([new_ref[s, r, KVH:, :] for s in range(2)], axis=0)
        out = o_ref[r] * before[rows] + jnp.dot(
            expo[rows], vals.astype(jnp.bfloat16), preferred_element_type=jnp.float32
        )
        out = out.astype(jnp.bfloat16)
        for p in range(KVH // 2):
            for s in range(2):
                at = (2 * p + s) * some
                out_ref[s, r, p * some:(p + 1) * some, :] = out[at:at + some]


def attend_join(q, o, lse, new_kv):
    rows = q.shape[1]
    block = min(8, rows)
    heads = pl.BlockSpec((2, block, HEADS, HD), lambda i: (0, i, 0, 0))
    return pl.pallas_call(
        join_body,
        grid=(rows // block,),
        in_specs=[
            heads,
            pl.BlockSpec((block, 2 * HEADS, HD), lambda i: (i, 0, 0)),
            pl.BlockSpec((block, 2 * HEADS, 1), lambda i: (i, 0, 0)),
            pl.BlockSpec((2, block, 2 * KVH, HD), lambda i: (0, i, 0, 0)),
        ],
        out_specs=heads,
        out_shape=jax.ShapeDtypeStruct((2, rows, HEADS, HD), jnp.bfloat16),
        cost_estimate=LIGHT,
        compiler_params=pltpu.CompilerParams(vmem_limit_bytes=VMEM_LIMIT),
        name="attend_join",
    )(q, o, lse, new_kv)


def after(value, *others):
    return lax.optimization_barrier((value, *others))[0]


def tensor_start(terms, tensor, mask):
    steps, blocks, rows, columns = terms[0].shape
    bit = (lax.axis_index("tensor") // mask) % 2

    def half(at):
        pairs = [t.reshape(steps, blocks // 2, 2, rows, columns) for t in terms]
        return sum(lax.dynamic_index_in_dim(p, at, 2, False).astype(jnp.float32) for p in pairs)

    sent = half(1 - bit).astype(jnp.bfloat16)
    ring = [(i, i ^ mask) for i in range(tensor)]
    return half(bit), sent, lax.ppermute(sent, "tensor", ring)


def local(
    replicas,
    tensor,
    hidden,
    base_weight,
    delta_values,
    delta_scales,
    tenant_slot,
    seg_tenant,
    seg_length,
    queries,
    kv_cache,
    cache_length,
):
    def swap(value, mask):
        return lax.ppermute(value, "replica", [(i, i ^ mask) for i in range(replicas)])

    rows = hidden.shape[1]
    columns = base_weight.shape[1]
    shard_rows = rows // tensor
    half = columns // 2
    parts = [slice(0, half), slice(half, columns)]
    masks = [1 << i for i in range(tensor.bit_length() - 1)]

    def split(value):
        return value.reshape(2, tensor, shard_rows, value.shape[2])

    flat = hidden.reshape(2 * rows, hidden.shape[2])
    cuts = [0, 2 * rows * 11 // 16, 2 * rows]
    sends = [flat[begin:end] for begin, end in zip(cuts[:-1], cuts[1:])]
    piece = shard_rows // 4

    first = (lax.axis_index("replica") * SLOTS).reshape(1)
    meta = jnp.concatenate([seg_tenant, seg_length], axis=1)
    meta = jnp.concatenate([meta, swap(meta, 1)], axis=0)
    sibling = swap(flat, 1)
    masks_far = list(range(2, replicas, 2))
    far_meta = [swap(meta, mask) for mask in masks_far]
    q = queries.reshape(2, shard_rows, HEADS, HD)

    def cached(at, before, *gates):
        return attend_cache(
            cache_length, after(q, *gates), kv_cache, at * piece, piece, before
        )

    early = [swap(sends[0], mask) for mask in masks_far]
    own, other = delta_rows(
        first, meta, tenant_slot, [flat], [after(sibling, q, *sends)], delta_values, delta_scales,
        base_weight,
    )
    early = [after(chunk, own) for chunk in early]
    later = [swap(send, mask) for send in (after(sends[1], own),) for mask in masks_far]
    done = cached(0, (), own, *early)
    back = after(swap(other, 1), *done)
    kept, sent, came = tensor_start([split(own), split(back)], tensor, masks[0])
    done = cached(1, done, sent)
    later = [after(chunk, *done) for chunk in later]
    near = [kept, after(came, *done, *later)]
    for mask in masks[1:-1]:
        kept, sent, came = tensor_start(near, tensor, mask)
        near = [kept, came]
    kept, last, came = tensor_start(near, tensor, masks[-1])

    flying = [[0, None, kept, came]]
    order = [(at, part) for at in range(len(masks_far)) for part in parts]
    theirs_in = [[swap(chunk, 1) for chunk in (early[at], later[at])] for at in range(len(masks_far))]
    for count, (at, part) in enumerate(order):
        mine, theirs = delta_rows(
            first, after(far_meta[at], last), tenant_slot, [early[at], later[at]], theirs_in[at],
            delta_values, delta_scales, None, part.start, half,
        )
        back = swap(theirs, 1)
        flying[-1][3] = after(flying[-1][3], theirs)
        if count < 2:
            done = cached(2 + count, done, theirs, flying[-1][3])
            back = after(back, *done)
        kept, last, came = tensor_start([split(mine), split(back)], tensor, masks[0])
        flying.append([masks_far[at], part, kept, came])
    _, _, kept, came = flying.pop(0)
    near = kept + came.astype(jnp.float32)
    totals = [near[:, 0, :, part] for part in parts]

    for mask, part, kept, came in flying:
        value = [kept, came]
        for step in masks[1:]:
            kept, _, came = tensor_start(value, tensor, step)
            value = [kept, came]
        value = sum(term.astype(jnp.float32) for term in value)
        value = swap(value[:, 0].astype(jnp.bfloat16), mask)
        at = parts.index(part)
        totals[at] = totals[at] + value.astype(jnp.float32)

    new_kv = jnp.concatenate(totals, axis=2).astype(jnp.bfloat16)
    tokens = new_kv.astype(jnp.float32).reshape(2, shard_rows, 2 * KVH, HD)
    attention = attend_join(q, *done, tokens)
    return (new_kv, attention.reshape(2, shard_rows, HEADS * HD))


def solution(mesh):
    placed = (
        P(None, ("groups", "replica"), "tensor"),
        P("tensor", None),
        P(("groups", "replica"), "tensor", None),
        P(("groups", "replica"), "tensor", None),
        P(),
        P(("groups", "replica"), None),
        P(("groups", "replica"), None),
        P(None, ("groups", "replica", "tensor"), None),
        P(("groups", "replica", "tensor"), None, None),
        P(("groups", "replica", "tensor")),
    )
    return jax.shard_map(
        functools.partial(local, mesh.shape["replica"], mesh.shape["tensor"]),
        mesh=mesh,
        in_specs=placed,
        out_specs=(
            P(None, ("groups", "replica", "tensor"), None),
            P(None, ("groups", "replica", "tensor"), None),
        ),
        check_vma=False,
    )
```

time: 153 us -> 108 us (0.71)
  waiting for transfers between devices: 57.8 us -> 25.5 us
  Pallas kernels: 57.9 us -> 49.3 us
  local copies, waits for them, and re-layouts: 10.8 us -> 7.38 us
    ppermute x12, waiting for transfers between devices: 45.7 us -> 5.69 us  [swap(): lax.ppermute(value, 'replica', [(i, i ^ mask) for i in range(replicas)])]
    pallas_call x5 -> x8, Pallas kernels: 57.9 us -> 49.3 us  [the longest x3 28.1 us: delta_rows(): pl.pallas_call(functools.partial(delta_body, base is not None, len(xa), s...]
    ppermute x6, waiting for transfers between devices: 12.1 us -> 19.8 us  [tensor_start(): return (half(bit), sent, lax.ppermute(sent, 'tensor', ring))]
    unnamed x32 -> x35, local copies, waits for them, and re-layouts: 7.68 us -> 2.29 us
    add x3 -> x4, other arithmetic: 3.81 us -> 0.32 us  [the longest x3 0.25 us: half(): sum((lax.dynamic_index_in_dim(p, at, 2, False).astype(jnp.float32) for p...]
    convert_element_type x3 -> x9, other arithmetic: 0.42 us -> 3.14 us  [the longest x6 2.09 us: tensor_start(): sent = half(1 - bit).astype(jnp.bfloat16)]
    slice x1 -> x2, local copies, waits for them, and re-layouts: 1.27 us -> 3.77 us  [local(): sends = [flat[begin:end] for begin, end in zip(cuts[:-1], cuts[1:])]]
    ppermute x6, starting transfers between devices: 12.1 us -> 10.4 us  [tensor_start(): return (half(bit), sent, lax.ppermute(sent, 'tensor', ring))]
  transfers between devices with their start and end apart: 18 -> 18, of which waited for: 9 -> 7; matrix products, arithmetic and copies ran while one was open for 4% -> 7% of each run, Pallas kernels for 34% -> 40%
where the time goes in v2:
time: 108 us
  Pallas kernels  49.3 us (46%)
  waiting for transfers between devices  25.5 us (24%)
  starting transfers between devices  19.7 us (18%)
  local copies, waits for them, and re-layouts  7.38 us (7%)
  other arithmetic  5.06 us (5%)
    pallas_call x3, Pallas kernels, delta_rows(): pl.pallas_call(functools.partial(delta_body, base is not None, len(xa), s...  28.1 us
    ppermute x6, waiting for transfers between devices, tensor_start(): return (half(bit), sent, lax.ppermute(sent, 'tensor', ring))  19.8 us
    pallas_call x4, Pallas kernels, attend_cache(): pl.pallas_call(functools.partial(cache_body, start), grid=(count // block...  15.4 us
    ppermute x6, starting transfers between devices, tensor_start(): return (half(bit), sent, lax.ppermute(sent, 'tensor', ring))  10.4 us
    ppermute x12, starting transfers between devices, swap(): lax.ppermute(value, 'replica', [(i, i ^ mask) for i in range(replicas)])  9.23 us
    pallas_call x1, Pallas kernels, attend_join(): pl.pallas_call(join_body, grid=(rows // block,), in_specs=[heads, pl.Bloc...  5.78 us
    ppermute x12, waiting for transfers between devices, swap(): lax.ppermute(value, 'replica', [(i, i ^ mask) for i in range(replicas)])  5.69 us
    slice x2, local copies, waits for them, and re-layouts, local(): sends = [flat[begin:end] for begin, end in zip(cuts[:-1], cuts[1:])]  3.77 us
  transfers between devices with their start and end apart: 18, of which 7 were waited for; matrix products, arithmetic and copies ran while one was open for 7% of the time, Pallas kernels for 40%

profile of v2, /device:TPU:0, one launch (start us, length us, event | category | flops | bytes accessed | tf_op | source)
XLA Modules:
  0.0 107.8 jit_solution(13114696901233105191)
XLA Ops:
  1.2 2.1 %slice.16 = bf16[176,2048]{1,0:T(8,128)(2,1)} slice(bf16[256,2048]{1,0:T(8,128)(2,1)} %bitcast.88), slice={[0:176], [0:2048]} | slice | bytes 1441792 | tf_op jit(solution)/shard_map/slice | solution.py:337
  3.3 2.6 %collective-permute-start.3 = (bf16[176,2048]{1,0:T(8,128)(2,1)}, bf16[176,2048]{1,0:T(8,128)(2,1)}, u32[]{:S(2)}, u32[]{:S(2)}) collective-permute-start(bf16[176,2048]{1,0:T(8,128)(2,1)} %slice.16), channel_id=1, source_target_pairs={{0,2},{1,3},{2,0},{3,1},{4,6},{5,7},{6,4},{7,5},{8,10},{9,11},{10,... | collective-permute-start | bytes 2162696 | tf_op jit(solution)/shard_map/ppermute | solution.py:323
  6.7 1.7 %slice.17 = bf16[80,2048]{1,0:T(8,128)(2,1)} slice(bf16[256,2048]{1,0:T(8,128)(2,1)} %bitcast.89), slice={[176:256], [0:2048]} | slice | bytes 655360 | tf_op jit(solution)/shard_map/slice | solution.py:337
  10.0 14.1 %delta_rows.3 = (bf16[2,128,2048]{2,1,0:T(8,128)(2,1)S(1)}, bf16[2,128,2048]{2,1,0:T(8,128)(2,1)}) custom-call(s32[1]{0:T(128)} %bitcast.refs_0_, s32[2,8]{1,0:T(2,128)S(1)} %pad_add_fusion.refs_1_, s32[8]{0:T(128)S(1)} %copy-done.2, bf16[256,2048]{1,0:T(8,128)(2,1)} %bitcast.90, bf16[256,2048]{1,0:T(8,128)(2,1)} %copy-done.5, ...), custom_call_target="tpu_custom_call" | custom-call | flops 1 | bytes 1 | tf_op jit(solution)/shard_map/delta_rows/pallas_call | solution.py:122
  24.9 3.8 %attend_cache.4 = (f32[32,128,128]{2,1,0:T(8,128)}, f32[32,128,1]{2,1,0:T(8,128)}) custom-call(s32[32]{0:T(128)S(1)} %copy-done.3, bf16[2,32,64,128]{3,2,1,0:T(8,128)(2,1)S(1)} %bitcast.76, bf16[32,128,2048]{2,1,0:T(8,128)(2,1)} %kv_ref.7), custom_call_target="tpu_custom_call" | custom-call | flops 17179869184 | bytes 67108864 | tf_op jit(solution)/shard_map/attend_cache/pallas_call | solution.py:206
  28.8 1.8 %collective-permute-start.4 = (bf16[2,2,32,2048]{3,2,0,1:T(8,128)(2,1)S(1)}, bf16[2,2,32,2048]{3,2,0,1:T(8,128)(2,1)S(1)}, u32[]{:S(2)}, u32[]{:S(2)}) collective-permute-start(bf16[2,2,32,2048]{3,2,0,1:T(8,128)(2,1)S(1)} %fusion), channel_id=1, source_target_pairs={{0,4},{4,0},{8,12},{12,8},{1,5},{5,1},{9,13},{13,9},{2,6},{6,2},{1... | collective-permute-start | bytes 1572872 | tf_op jit(solution)/shard_map/ppermute | solution.py:305
  30.6 3.8 %attend_cache.5 = (f32[32,128,128]{2,1,0:T(8,128)}, f32[32,128,1]{2,1,0:T(8,128)}) custom-call(s32[32]{0:T(128)S(1)} %copy-done.3, bf16[2,32,64,128]{3,2,1,0:T(8,128)(2,1)S(1)} %bitcast.77, bf16[32,128,2048]{2,1,0:T(8,128)(2,1)} %kv_ref.7, f32[32,128,128]{2,1,0:T(8,128)} %get-tuple-element.37.refs_0_, ...), custom_call_target="tpu_custom_call", output_to_operand_aliasing={{0}: (3, {}), {1}: (4, {})} | custom-call | flops 17179869184 | bytes 67108864 | tf_op jit(solution)/shard_map/attend_cache/pallas_call | solution.py:206
  34.8 8.4 %collective-permute-done.4 = bf16[2,2,32,2048]{3,2,0,1:T(8,128)(2,1)S(1)} collective-permute-done((bf16[2,2,32,2048]{3,2,0,1:T(8,128)(2,1)S(1)}, bf16[2,2,32,2048]{3,2,0,1:T(8,128)(2,1)S(1)}, u32[]{:S(2)}, u32[]{:S(2)}) %collective-permute-start.4) | collective-permute-done | bytes 524320 | tf_op jit(solution)/shard_map/ppermute | solution.py:305
  43.2 2.8 %collective-permute-start.6 = (bf16[2,1,32,2048]{3,2,0,1:T(8,128)(2,1)S(1)}, bf16[2,1,32,2048]{3,2,0,1:T(8,128)(2,1)S(1)}, u32[]{:S(2)}, u32[]{:S(2)}) collective-permute-start(bf16[2,1,32,2048]{3,2,0,1:T(8,128)(2,1)S(1)} %fusion.1), channel_id=1, source_target_pairs={{0,8},{4,12},{8,0},{12,4},{1,9},{5,13},{9,1},{13,5},{2,10},{6,14},... | collective-permute-start | bytes 786440 | tf_op jit(solution)/shard_map/ppermute | solution.py:305
  46.1 1.5 %collective-permute-start.7 = (s32[2,8]{1,0:T(2,128)S(1)}, s32[2,8]{1,0:T(2,128)S(1)}, u32[]{:S(2)}, u32[]{:S(2)}) collective-permute-start(s32[2,8]{1,0:T(2,128)S(1)} %pad_add_fusion.refs_1_), channel_id=1, source_target_pairs={{0,2},{1,3},{2,0},{3,1},{4,6},{5,7},{6,4},{7,5},{8,10},{9,11},{10,... | collective-permute-start | bytes 200 | tf_op jit(solution)/shard_map/ppermute | solution.py:323
  47.6 2.1 %collective-permute-done.7.refs_1_ = s32[2,8]{1,0:T(2,128)S(1)} collective-permute-done((s32[2,8]{1,0:T(2,128)S(1)}, s32[2,8]{1,0:T(2,128)S(1)}, u32[]{:S(2)}, u32[]{:S(2)}) %collective-permute-start.7) | collective-permute-done | bytes 96 | tf_op jit(solution)/shard_map/ppermute | solution.py:323
  50.5 7.0 %delta_rows.4 = (bf16[2,128,1024]{2,1,0:T(8,128)(2,1)S(1)}, bf16[2,128,1024]{2,1,0:T(8,128)(2,1)S(1)}) custom-call(s32[1]{0:T(128)} %bitcast.refs_0_, s32[2,8]{1,0:T(2,128)S(1)} %collective-permute-done.7.refs_1_, s32[8]{0:T(128)S(1)} %copy-done.2, bf16[176,2048]{1,0:T(8,128)(2,1)} %collective-permute-done.3.refs_3_, ...), custom_call_target="tpu_custom_call" | custom-call | flops 1 | bytes 1 | tf_op jit(solution)/shard_map/delta_rows/pallas_call | solution.py:122
  57.9 3.9 %attend_cache.6 = (f32[32,128,128]{2,1,0:T(8,128)}, f32[32,128,1]{2,1,0:T(8,128)}) custom-call(s32[32]{0:T(128)S(1)} %copy-done.3, bf16[2,32,64,128]{3,2,1,0:T(8,128)(2,1)S(1)} %bitcast.78, bf16[32,128,2048]{2,1,0:T(8,128)(2,1)} %kv_ref.7, f32[32,128,128]{2,1,0:T(8,128)} %get-tuple-element.41.refs_0_, ...), custom_call_target="tpu_custom_call", output_to_operand_aliasing={{0}: (3, {}), {1}: (4, {})} | custom-call | flops 17179869184 | bytes 67108864 | tf_op jit(solution)/shard_map/attend_cache/pallas_call | solution.py:206
  62.7 1.3 %collective-permute-start.11 = (bf16[2,2,32,1024]{3,2,0,1:T(8,128)(2,1)}, bf16[2,2,32,1024]{3,2,0,1:T(8,128)(2,1)}, u32[]{:S(2)}, u32[]{:S(2)}) collective-permute-start(bf16[2,2,32,1024]{3,2,0,1:T(8,128)(2,1)} %fusion.3), channel_id=1, source_target_pairs={{0,4},{4,0},{8,12},{12,8},{1,5},{5,1},{9,13},{13,9},{2,6},{6,2},{1... | collective-permute-start | bytes 786440 | tf_op jit(solution)/shard_map/ppermute | solution.py:305
  64.0 7.0 %delta_rows.5 = (bf16[2,128,1024]{2,1,0:T(8,128)(2,1)S(1)}, bf16[2,128,1024]{2,1,0:T(8,128)(2,1)S(1)}) custom-call(s32[1]{0:T(128)} %bitcast.refs_0_, s32[2,8]{1,0:T(2,128)S(1)} %collective-permute-done.7.refs_1_, s32[8]{0:T(128)S(1)} %copy-done.2, bf16[176,2048]{1,0:T(8,128)(2,1)} %collective-permute-done.3.refs_3_, ...), custom_call_target="tpu_custom_call" | custom-call | flops 1 | bytes 1 | tf_op jit(solution)/shard_map/delta_rows/pallas_call | solution.py:122
  71.5 3.9 %attend_cache.7 = (f32[32,128,128]{2,1,0:T(8,128)}, f32[32,128,1]{2,1,0:T(8,128)}) custom-call(s32[32]{0:T(128)S(1)} %copy-done.3, bf16[2,32,64,128]{3,2,1,0:T(8,128)(2,1)S(1)} %bitcast.79, bf16[32,128,2048]{2,1,0:T(8,128)(2,1)} %kv_ref.7, f32[32,128,128]{2,1,0:T(8,128)} %get-tuple-element.51.refs_0_, ...), custom_call_target="tpu_custom_call", output_to_operand_aliasing={{0}: (3, {}), {1}: (4, {})} | custom-call | flops 17179869184 | bytes 67108864 | tf_op jit(solution)/shard_map/attend_cache/pallas_call | solution.py:206
  75.4 1.6 %collective-permute-start.15 = (bf16[2,2,32,1024]{3,2,0,1:T(8,128)(2,1)S(1)}, bf16[2,2,32,1024]{3,2,0,1:T(8,128)(2,1)S(1)}, u32[]{:S(2)}, u32[]{:S(2)}) collective-permute-start(bf16[2,2,32,1024]{3,2,0,1:T(8,128)(2,1)S(1)} %fusion.4), channel_id=1, source_target_pairs={{0,4},{4,0},{8,12},{12,8},{1,5},{5,1},{9,13},{13,9},{2,6},{6,2},{1... | collective-permute-start | bytes 786440 | tf_op jit(solution)/shard_map/ppermute | solution.py:305
  78.1 2.4 %collective-permute-start.12 = (bf16[2,1,32,1024]{3,2,0,1:T(8,128)(2,1)S(1)}, bf16[2,1,32,1024]{3,2,0,1:T(8,128)(2,1)S(1)}, u32[]{:S(2)}, u32[]{:S(2)}) collective-permute-start(bf16[2,1,32,1024]{3,2,0,1:T(8,128)(2,1)S(1)} %fusion.12), channel_id=1, source_target_pairs={{0,8},{4,12},{8,0},{12,4},{1,9},{5,13},{9,1},{13,5},{2,10},{6,14},... | collective-permute-start | bytes 393224 | tf_op jit(solution)/shard_map/ppermute | solution.py:305
  80.5 6.2 %collective-permute-done.15 = bf16[2,2,32,1024]{3,2,0,1:T(8,128)(2,1)S(1)} collective-permute-done((bf16[2,2,32,1024]{3,2,0,1:T(8,128)(2,1)S(1)}, bf16[2,2,32,1024]{3,2,0,1:T(8,128)(2,1)S(1)}, u32[]{:S(2)}, u32[]{:S(2)}) %collective-permute-start.15) | collective-permute-done | bytes 262176 | tf_op jit(solution)/shard_map/ppermute | solution.py:305
  88.2 1.6 %collective-permute-start.13 = (bf16[2,32,1024]{2,1,0:T(8,128)(2,1)S(1)}, bf16[2,32,1024]{2,1,0:T(8,128)(2,1)S(1)}, u32[]{:S(2)}, u32[]{:S(2)}) collective-permute-start(bf16[2,32,1024]{2,1,0:T(8,128)(2,1)S(1)} %fusion.15), channel_id=1, source_target_pairs={{0,2},{1,3},{2,0},{3,1},{4,6},{5,7},{6,4},{7,5},{8,10},{9,11},{10,... | collective-permute-start | bytes 393224 | tf_op jit(solution)/shard_map/ppermute | solution.py:323
  89.8 4.8 %collective-permute-done.16 = bf16[2,1,32,1024]{3,2,0,1:T(8,128)(2,1)S(1)} collective-permute-done((bf16[2,1,32,1024]{3,2,0,1:T(8,128)(2,1)S(1)}, bf16[2,1,32,1024]{3,2,0,1:T(8,128)(2,1)S(1)}, u32[]{:S(2)}, u32[]{:S(2)}) %collective-permute-start.16) | collective-permute-done | bytes 131104 | tf_op jit(solution)/shard_map/ppermute | solution.py:305
  94.6 1.6 %collective-permute-start.17 = (bf16[2,32,1024]{2,1,0:T(8,128)(2,1)S(1)}, bf16[2,32,1024]{2,1,0:T(8,128)(2,1)S(1)}, u32[]{:S(2)}, u32[]{:S(2)}) collective-permute-start(bf16[2,32,1024]{2,1,0:T(8,128)(2,1)S(1)} %fusion.16), channel_id=1, source_target_pairs={{0,2},{1,3},{2,0},{3,1},{4,6},{5,7},{6,4},{7,5},{8,10},{9,11},{10,... | collective-permute-start | bytes 393224 | tf_op jit(solution)/shard_map/ppermute | solution.py:323
  96.3 3.6 %collective-permute-done.17 = bf16[2,32,1024]{2,1,0:T(8,128)(2,1)S(1)} collective-permute-done((bf16[2,32,1024]{2,1,0:T(8,128)(2,1)S(1)}, bf16[2,32,1024]{2,1,0:T(8,128)(2,1)S(1)}, u32[]{:S(2)}, u32[]{:S(2)}) %collective-permute-start.17) | collective-permute-done | bytes 131104 | tf_op jit(solution)/shard_map/ppermute | solution.py:323
  100.7 5.8 %attend_join.1 = bf16[2,32,64,128]{3,2,1,0:T(8,128)(2,1)S(1)} custom-call(bf16[2,32,64,128]{3,2,1,0:T(8,128)(2,1)} %bitcast.80, f32[32,128,128]{2,1,0:T(8,128)} %get-tuple-element.59.o_ref, f32[32,128,1]{2,1,0:T(8,128)} %get-tuple-element.60.lse_ref, f32[2,32,16,128]{3,2,1,0:T(8,128)S(1)} %maximum_convert_fusion.new_ref), custom_call_target="tpu_custom_call" | custom-call | flops 1 | bytes 1 | tf_op jit(solution)/shard_map/attend_join/pallas_call | solution.py:274
  (76 shorter events, 11.6 us)
Async XLA Ops:
  0.7 9.3 %copy-start.1 = (bf16[2,16,2048]{2,1,0:T(8,128)(2,1)S(1)}, bf16[2,16,2048]{2,1,0:T(8,128)(2,1)}, u32[]{:S(2)}) copy-start(bf16[2,16,2048]{2,1,0:T(8,128)(2,1)} %refs_8_.3) | copy-start | bytes 393220
  0.7 8.2 %collective-permute-start.1 = (bf16[256,2048]{1,0:T(8,128)(2,1)}, bf16[256,2048]{1,0:T(8,128)(2,1)S(1)}, u32[]{:S(2)}, u32[]{:S(2)}) collective-permute-start(bf16[256,2048]{1,0:T(8,128)(2,1)} %bitcast.87), channel_id=1, source_target_pairs={{0,1},{1,0},{2,3},{3,2},{4,5},{5,4},{6,7},{7,6},{8,9},{9,8},{10,11... | collective-permute-start | bytes 3145736 | tf_op jit(solution)/shard_map/ppermute | solution.py:323
  3.3 20.8 %collective-permute-start.3 = (bf16[176,2048]{1,0:T(8,128)(2,1)}, bf16[176,2048]{1,0:T(8,128)(2,1)}, u32[]{:S(2)}, u32[]{:S(2)}) collective-permute-start(bf16[176,2048]{1,0:T(8,128)(2,1)} %slice.16), channel_id=1, source_target_pairs={{0,2},{1,3},{2,0},{3,1},{4,6},{5,7},{6,4},{7,5},{8,10},{9,11},{10,... | collective-permute-start | bytes 2162696 | tf_op jit(solution)/shard_map/ppermute | solution.py:323
  6.6 2.2 %collective-permute-start = (s32[1,8]{1,0:T(1,128)S(1)}, s32[1,8]{1,0:T(1,128)S(1)}, u32[]{:S(2)}, u32[]{:S(2)}) collective-permute-start(s32[1,8]{1,0:T(1,128)S(1)} %pad_add_fusion.1), channel_id=1, source_target_pairs={{0,1},{1,0},{2,3},{3,2},{4,5},{5,4},{6,7},{7,6},{8,9},{9,8},{10,11... | collective-permute-start | bytes 104 | tf_op jit(solution)/shard_map/ppermute | solution.py:323
  8.7 62.8 %copy-start = (bf16[8,8,64,128]{3,2,1,0:T(8,128)(2,1)}, bf16[8,8,64,128]{3,2,1,0:T(8,128)(2,1)S(1)}, u32[]{:S(2)}) copy-start(bf16[8,8,64,128]{3,2,1,0:T(8,128)(2,1)S(1)} %copy.30) | copy-start | bytes 3145732
  10.0 14.5 %copy-start.11 = (bf16[80,2048]{1,0:T(8,128)(2,1)S(1)}, bf16[80,2048]{1,0:T(8,128)(2,1)}, u32[]{:S(2)}) copy-start(bf16[80,2048]{1,0:T(8,128)(2,1)} %slice.17) | copy-start | bytes 983044
  10.0 14.9 %copy-start.3 = (s32[32]{0:T(128)S(1)}, s32[32]{0:T(128)}, u32[]{:S(2)}) copy-start(s32[32]{0:T(128)} %len_ref.7) | copy-start | bytes 388
  24.0 25.6 %collective-permute-start.8 = (bf16[176,2048]{1,0:T(8,128)(2,1)}, bf16[176,2048]{1,0:T(8,128)(2,1)S(1)}, u32[]{:S(2)}, u32[]{:S(2)}) collective-permute-start(bf16[176,2048]{1,0:T(8,128)(2,1)} %collective-permute-done.3.refs_3_), channel_id=1, source_target_pairs={{0,1},{1,0},{2,3},{3,2},{4,5},{5,4},{6,7},{7,6},{8,9},{9,8},{10,11... | collective-permute-start | bytes 2162696 | tf_op jit(solution)/shard_map/ppermute | solution.py:323
  24.5 10.0 %collective-permute-start.5 = (bf16[80,2048]{1,0:T(8,128)(2,1)S(1)}, bf16[80,2048]{1,0:T(8,128)(2,1)S(1)}, u32[]{:S(2)}, u32[]{:S(2)}) collective-permute-start(bf16[80,2048]{1,0:T(8,128)(2,1)S(1)} %copy-done.11), channel_id=1, source_target_pairs={{0,2},{1,3},{2,0},{3,1},{4,6},{5,7},{6,4},{7,5},{8,10},{9,11},{10,... | collective-permute-start | bytes 983048 | tf_op jit(solution)/shard_map/ppermute | solution.py:323
  24.6 4.0 %collective-permute-start.2 = (bf16[2,128,2048]{2,1,0:T(8,128)(2,1)}, bf16[2,128,2048]{2,1,0:T(8,128)(2,1)S(1)}, u32[]{:S(2)}, u32[]{:S(2)}) collective-permute-start(bf16[2,128,2048]{2,1,0:T(8,128)(2,1)} %get-tuple-element.34), channel_id=1, source_target_pairs={{0,1},{1,0},{2,3},{3,2},{4,5},{5,4},{6,7},{7,6},{8,9},{9,8},{10,11... | collective-permute-start | bytes 3145736 | tf_op jit(solution)/shard_map/ppermute | solution.py:323
  28.8 14.4 %collective-permute-start.4 = (bf16[2,2,32,2048]{3,2,0,1:T(8,128)(2,1)S(1)}, bf16[2,2,32,2048]{3,2,0,1:T(8,128)(2,1)S(1)}, u32[]{:S(2)}, u32[]{:S(2)}) collective-permute-start(bf16[2,2,32,2048]{3,2,0,1:T(8,128)(2,1)S(1)} %fusion), channel_id=1, source_target_pairs={{0,4},{4,0},{8,12},{12,8},{1,5},{5,1},{9,13},{13,9},{2,6},{6,2},{1... | collective-permute-start | bytes 1572872 | tf_op jit(solution)/shard_map/ppermute | solution.py:305
  34.4 15.2 %collective-permute-start.9 = (bf16[80,2048]{1,0:T(8,128)(2,1)S(1)}, bf16[80,2048]{1,0:T(8,128)(2,1)S(1)}, u32[]{:S(2)}, u32[]{:S(2)}) collective-permute-start(bf16[80,2048]{1,0:T(8,128)(2,1)S(1)} %collective-permute-done.5.refs_4_), channel_id=1, source_target_pairs={{0,1},{1,0},{2,3},{3,2},{4,5},{5,4},{6,7},{7,6},{8,9},{9,8},{10,11... | collective-permute-start | bytes 983048 | tf_op jit(solution)/shard_map/ppermute | solution.py:323
  43.2 14.6 %collective-permute-start.6 = (bf16[2,1,32,2048]{3,2,0,1:T(8,128)(2,1)S(1)}, bf16[2,1,32,2048]{3,2,0,1:T(8,128)(2,1)S(1)}, u32[]{:S(2)}, u32[]{:S(2)}) collective-permute-start(bf16[2,1,32,2048]{3,2,0,1:T(8,128)(2,1)S(1)} %fusion.1), channel_id=1, source_target_pairs={{0,8},{4,12},{8,0},{12,4},{1,9},{5,13},{9,1},{13,5},{2,10},{6,14},... | collective-permute-start | bytes 786440 | tf_op jit(solution)/shard_map/ppermute | solution.py:305
  46.1 3.6 %collective-permute-start.7 = (s32[2,8]{1,0:T(2,128)S(1)}, s32[2,8]{1,0:T(2,128)S(1)}, u32[]{:S(2)}, u32[]{:S(2)}) collective-permute-start(s32[2,8]{1,0:T(2,128)S(1)} %pad_add_fusion.refs_1_), channel_id=1, source_target_pairs={{0,2},{1,3},{2,0},{3,1},{4,6},{5,7},{6,4},{7,5},{8,10},{9,11},{10,... | collective-permute-start | bytes 200 | tf_op jit(solution)/shard_map/ppermute | solution.py:323
  57.5 4.3 %collective-permute-start.10 = (bf16[2,128,1024]{2,1,0:T(8,128)(2,1)S(1)}, bf16[2,128,1024]{2,1,0:T(8,128)(2,1)S(1)}, u32[]{:S(2)}, u32[]{:S(2)}) collective-permute-start(bf16[2,128,1024]{2,1,0:T(8,128)(2,1)S(1)} %get-tuple-element.47), channel_id=1, source_target_pairs={{0,1},{1,0},{2,3},{3,2},{4,5},{5,4},{6,7},{7,6},{8,9},{9,8},{10,11... | collective-permute-start | bytes 1572872 | tf_op jit(solution)/shard_map/ppermute | solution.py:323
  62.7 8.8 %collective-permute-start.11 = (bf16[2,2,32,1024]{3,2,0,1:T(8,128)(2,1)}, bf16[2,2,32,1024]{3,2,0,1:T(8,128)(2,1)}, u32[]{:S(2)}, u32[]{:S(2)}) collective-permute-start(bf16[2,2,32,1024]{3,2,0,1:T(8,128)(2,1)} %fusion.3), channel_id=1, source_target_pairs={{0,4},{4,0},{8,12},{12,8},{1,5},{5,1},{9,13},{13,9},{2,6},{6,2},{1... | collective-permute-start | bytes 786440 | tf_op jit(solution)/shard_map/ppermute | solution.py:305
  71.1 4.2 %collective-permute-start.14 = (bf16[2,128,1024]{2,1,0:T(8,128)(2,1)S(1)}, bf16[2,128,1024]{2,1,0:T(8,128)(2,1)S(1)}, u32[]{:S(2)}, u32[]{:S(2)}) collective-permute-start(bf16[2,128,1024]{2,1,0:T(8,128)(2,1)S(1)} %get-tuple-element.55), channel_id=1, source_target_pairs={{0,1},{1,0},{2,3},{3,2},{4,5},{5,4},{6,7},{7,6},{8,9},{9,8},{10,11... | collective-permute-start | bytes 1572872 | tf_op jit(solution)/shard_map/ppermute | solution.py:323
  75.4 20.8 %copy-start.8 = (bf16[2,2,32,2048]{3,2,0,1:T(8,128)(2,1)S(1)}, bf16[2,2,32,2048]{3,2,0,1:T(8,128)(2,1)}, u32[]{:S(2)}) copy-start(bf16[2,2,32,2048]{3,2,0,1:T(8,128)(2,1)} %copy-done.7) | copy-start | bytes 1572868
  75.4 20.7 %copy-start.13 = (bf16[2,1,32,2048]{3,2,0,1:T(8,128)(2,1)S(1)}, bf16[2,1,32,2048]{3,2,0,1:T(8,128)(2,1)}, u32[]{:S(2)}) copy-start(bf16[2,1,32,2048]{3,2,0,1:T(8,128)(2,1)} %copy-done.12) | copy-start | bytes 786436
  75.4 11.3 %collective-permute-start.15 = (bf16[2,2,32,1024]{3,2,0,1:T(8,128)(2,1)S(1)}, bf16[2,2,32,1024]{3,2,0,1:T(8,128)(2,1)S(1)}, u32[]{:S(2)}, u32[]{:S(2)}) collective-permute-start(bf16[2,2,32,1024]{3,2,0,1:T(8,128)(2,1)S(1)} %fusion.4), channel_id=1, source_target_pairs={{0,4},{4,0},{8,12},{12,8},{1,5},{5,1},{9,13},{13,9},{2,6},{6,2},{1... | collective-permute-start | bytes 786440 | tf_op jit(solution)/shard_map/ppermute | solution.py:305
  78.1 9.2 %collective-permute-start.12 = (bf16[2,1,32,1024]{3,2,0,1:T(8,128)(2,1)S(1)}, bf16[2,1,32,1024]{3,2,0,1:T(8,128)(2,1)S(1)}, u32[]{:S(2)}, u32[]{:S(2)}) collective-permute-start(bf16[2,1,32,1024]{3,2,0,1:T(8,128)(2,1)S(1)} %fusion.12), channel_id=1, source_target_pairs={{0,8},{4,12},{8,0},{12,4},{1,9},{5,13},{9,1},{13,5},{2,10},{6,14},... | collective-permute-start | bytes 393224 | tf_op jit(solution)/shard_map/ppermute | solution.py:305
  86.8 7.8 %collective-permute-start.16 = (bf16[2,1,32,1024]{3,2,0,1:T(8,128)(2,1)S(1)}, bf16[2,1,32,1024]{3,2,0,1:T(8,128)(2,1)S(1)}, u32[]{:S(2)}, u32[]{:S(2)}) collective-permute-start(bf16[2,1,32,1024]{3,2,0,1:T(8,128)(2,1)S(1)} %fusion.9), channel_id=1, source_target_pairs={{0,8},{4,12},{8,0},{12,4},{1,9},{5,13},{9,1},{13,5},{2,10},{6,14},... | collective-permute-start | bytes 393224 | tf_op jit(solution)/shard_map/ppermute | solution.py:305
  88.2 8.0 %collective-permute-start.13 = (bf16[2,32,1024]{2,1,0:T(8,128)(2,1)S(1)}, bf16[2,32,1024]{2,1,0:T(8,128)(2,1)S(1)}, u32[]{:S(2)}, u32[]{:S(2)}) collective-permute-start(bf16[2,32,1024]{2,1,0:T(8,128)(2,1)S(1)} %fusion.15), channel_id=1, source_target_pairs={{0,2},{1,3},{2,0},{3,1},{4,6},{5,7},{6,4},{7,5},{8,10},{9,11},{10,... | collective-permute-start | bytes 393224 | tf_op jit(solution)/shard_map/ppermute | solution.py:323
  94.6 5.2 %collective-permute-start.17 = (bf16[2,32,1024]{2,1,0:T(8,128)(2,1)S(1)}, bf16[2,32,1024]{2,1,0:T(8,128)(2,1)S(1)}, u32[]{:S(2)}, u32[]{:S(2)}) collective-permute-start(bf16[2,32,1024]{2,1,0:T(8,128)(2,1)S(1)} %fusion.16), channel_id=1, source_target_pairs={{0,2},{1,3},{2,0},{3,1},{4,6},{5,7},{6,4},{7,5},{8,10},{9,11},{10,... | collective-permute-start | bytes 393224 | tf_op jit(solution)/shard_map/ppermute | solution.py:323
  (10 other events, 52.6 us)

commit v3 on v2

v3 whole, which is shorter than its diff:
```python
import functools
import math

import jax
import jax.numpy as jnp
from jax import lax
from jax.experimental import pallas as pl
from jax.experimental.pallas import tpu as pltpu
from jax.sharding import PartitionSpec as P

HEADS = 64
KVH = 8
HD = 128
GROUP = HEADS // KVH
KEYS = KVH * HD
BLOCK = 128
SEG_MOST = 40
SLOTS = 2
NEG = -1e30
DELTA_VMEM = 50 * 1024 * 1024
ATTEND_VMEM = 50 * 1024 * 1024
LIGHT = pl.CostEstimate(flops=1, bytes_accessed=1, transcendentals=0)
FLAG = pltpu.HBM((8, 128), jnp.float32)
COVER = pl.CostEstimate(flops=1 << 34, bytes_accessed=1 << 26, transcendentals=0)


def in_hbm(*values):
    return [pltpu.with_memory_space_constraint(value, pltpu.HBM) for value in values]


def in_vmem(*values):
    return [pltpu.with_memory_space_constraint(value, pltpu.VMEM) for value in values]


def scatter_order(me, tensor, steps, rows, shape, axis):
    out = lax.broadcasted_iota(jnp.int32, shape, axis) % (steps * rows)
    shard = rows // tensor
    turn = tensor - 1 - out // (steps * shard)
    bits = tensor.bit_length() - 1
    apart = jnp.zeros(shape, jnp.int32)
    for bit in range(bits):
        apart = apart | (((turn >> (bits - 1 - bit)) & 1) << bit)
    step = (out // shard) % steps
    return step * rows + (apart ^ me) * shard + out % shard


def row_positions(meta_ref, slot_ref, first, steps, rows, source, index):
    step = index // rows
    row = index % rows
    per_slot = 2 * steps * SEG_MOST
    place = jnp.full(index.shape, -1, jnp.int32)
    for src in range(2):
        begin = jnp.int32(0)
        for seg in range(meta_ref.shape[1] // 2):
            slot = slot_ref[meta_ref[src, seg]] - first
            length = meta_ref[src, meta_ref.shape[1] // 2 + seg]
            end = begin + length
            held = jnp.logical_and(slot >= 0, slot < SLOTS)
            offset = jnp.where(held, slot * per_slot + src * steps * SEG_MOST - begin, -(1 << 20))
            inside = (source == src) & (row >= begin) & (row < end)
            place = jnp.where(inside, offset + step * SEG_MOST + row, place)
            begin = end
    return place


def delta_body(with_base, tensor, steps, rows, *refs):
    place_ref, slot_ref, meta_ref, xa_ref, xb_ref, val_ref, sc_ref, base_ref = refs[:8]
    if with_base:
        da_ref, db_ref, _, xc_ref, scatter_ref, xo_ref = refs[-6:]
    else:
        da_ref, db_ref, _, xc_ref, scatter_ref = refs[-5:]
    width = val_ref.shape[1]
    half = steps * rows
    taken = SLOTS * 2 * steps * SEG_MOST
    per_slot = taken // SLOTS

    @pl.when(pl.program_id(0) == 0)
    def _():
        first, me = place_ref[0], place_ref[1]
        flat = lax.broadcasted_iota(jnp.int32, (1, 2 * half), 1)
        along = row_positions(meta_ref, slot_ref, first, steps, rows, flat // half, flat % half)
        picks = (lax.broadcasted_iota(jnp.int32, (taken, 2 * half), 0) == along).astype(jnp.bfloat16)
        got = jnp.dot(picks[:, :half], xa_ref[...], preferred_element_type=jnp.float32)
        got += jnp.dot(picks[:, half:], xb_ref[...], preferred_element_type=jnp.float32)
        xc_ref[...] = got.astype(jnp.bfloat16)
        order = scatter_order(me, tensor, steps, rows, (1, 2 * half), 1)
        along = row_positions(meta_ref, slot_ref, first, steps, rows, flat // half, order)
        picks = lax.broadcasted_iota(jnp.int32, (taken, 2 * half), 0) == along
        scatter_ref[...] = picks.astype(jnp.float32).T.astype(jnp.bfloat16)
        if with_base:
            picks = lax.broadcasted_iota(jnp.int32, (half, half), 0) == order[:, :half]
            xo_ref[...] = jnp.dot(
                picks.astype(jnp.float32).T.astype(jnp.bfloat16), xa_ref[...],
                preferred_element_type=jnp.float32,
            ).astype(jnp.bfloat16)

    parts = []
    for slot in range(SLOTS):
        scaled = [
            val_ref[slot, b * BLOCK:(b + 1) * BLOCK, :] * sc_ref[slot, b:b + 1, :]
            for b in range(width // BLOCK)
        ]
        weight = jnp.concatenate(scaled, axis=0)
        parts.append(
            jnp.dot(
                xc_ref[slot * per_slot:(slot + 1) * per_slot, :], weight,
                preferred_element_type=jnp.float32,
            ).astype(jnp.bfloat16)
        )
    spread = jnp.dot(
        scatter_ref[...], jnp.concatenate(parts, axis=0), preferred_element_type=jnp.float32
    )
    own = spread[:half]
    if with_base:
        own = own + jnp.dot(xo_ref[...], base_ref[...], preferred_element_type=jnp.float32)
    da_ref[...] = own.astype(da_ref.dtype)
    db_ref[...] = spread[half:].astype(db_ref.dtype)


def delta_rows(place, slots, meta, xa, xb, values, scales, tensor, base=None, start=0, columns=None, gates=()):
    steps = 2
    rows = xa.shape[0] // steps
    width = values.shape[1]
    columns = columns or values.shape[2]
    tile = min(512, columns)
    skip = start // tile
    smem = pl.BlockSpec(memory_space=pltpu.SMEM)
    whole = pl.BlockSpec(xa.shape, lambda i: (0, 0))
    in_specs = [
        smem, smem, smem, whole, whole,
        pl.BlockSpec((SLOTS, width, tile), lambda i: (0, 0, i + skip)),
        pl.BlockSpec((SLOTS, width // BLOCK, tile), lambda i: (0, 0, i + skip)),
    ]
    args = [place, *in_hbm(slots), meta, *in_vmem(xa, xb), *in_hbm(values, scales)]
    if base is not None:
        in_specs.append(pl.BlockSpec((width, tile), lambda i: (0, i + skip)))
        args += in_hbm(base)
    in_specs += [pl.BlockSpec(memory_space=pltpu.HBM) for _ in gates]
    args += in_hbm(*gates)
    taken = SLOTS * 2 * steps * SEG_MOST
    out = pl.BlockSpec((steps * rows, tile), lambda i: (0, i))
    shape = pltpu.HBM((steps * rows, columns), jnp.bfloat16)
    scratch = [
        pltpu.VMEM((taken, width), jnp.bfloat16),
        pltpu.VMEM((2 * steps * rows, taken), jnp.bfloat16),
    ]
    if base is not None:
        scratch.append(pltpu.VMEM((steps * rows, width), jnp.bfloat16))
    return pl.pallas_call(
        functools.partial(delta_body, base is not None, tensor, steps, rows),
        grid=(columns // tile,),
        in_specs=in_specs,
        out_specs=(out, out, pl.BlockSpec(memory_space=pltpu.HBM)),
        out_shape=(shape, shape, FLAG),
        scratch_shapes=scratch,
        cost_estimate=LIGHT,
        compiler_params=pltpu.CompilerParams(vmem_limit_bytes=DELTA_VMEM),
        name="delta_rows",
    )(*args)


def head_rows(ref, r):
    some = 2 * GROUP
    return jnp.concatenate(
        [ref[s, r, p * some:(p + 1) * some, :] for p in range(KVH // 2) for s in range(2)], axis=0
    )


def cache_body(start, len_ref, q_ref, kv_ref, *refs):
    o_ref, lse_ref, _ = refs[-3:]
    block = q_ref.shape[1]
    cached = kv_ref.shape[1]
    some = 4 * GROUP
    scale = 1.0 / math.sqrt(HD)
    position = lax.broadcasted_iota(jnp.int32, (2 * HEADS, cached), 1)
    wide = (some, 2 * HD)
    diagonal = (lax.broadcasted_iota(jnp.int32, wide, 0) // GROUP) % 2 == (
        lax.broadcasted_iota(jnp.int32, wide, 1) // HD
    )
    first = (lax.broadcasted_iota(jnp.int32, (some, HD), 0) // GROUP) % 2 == 0
    scores = []
    for r in range(block):
        rows = head_rows(q_ref, r)
        parts = []
        for p in range(KVH // 2):
            q = rows[p * some:(p + 1) * some]
            q = jnp.concatenate([q, q], axis=1)
            q = jnp.where(diagonal, q, jnp.zeros_like(q))
            parts.append(
                lax.dot_general(
                    q, kv_ref[r, :, p * 2 * HD:(p + 1) * 2 * HD], (((1,), (1,)), ((), ())),
                    preferred_element_type=jnp.float32,
                )
            )
        one = jnp.concatenate(parts, axis=0) * scale
        length = len_ref[start + pl.program_id(0) * block + r]
        scores.append(jnp.where(position < length, one, NEG))
    scores = jnp.concatenate(scores, axis=0)
    top = jnp.max(scores, axis=1, keepdims=True)
    expo = jnp.exp(scores - top)
    total = jnp.sum(expo, axis=1, keepdims=True)
    lse = top + jnp.log(total)
    inverse = 1.0 / total
    expo = expo.astype(jnp.bfloat16)
    for r in range(block):
        base = r * 2 * HEADS
        parts = []
        for p in range(KVH // 2):
            out = jnp.dot(
                expo[base + p * some:base + (p + 1) * some],
                kv_ref[r, :, KEYS + p * 2 * HD:KEYS + (p + 1) * 2 * HD],
                preferred_element_type=jnp.float32,
            )
            parts.append(jnp.where(first, out[:, :HD], out[:, HD:]))
        o_ref[r] = jnp.concatenate(parts, axis=0) * inverse[base:base + 2 * HEADS]
        lse_ref[r] = lse[base:base + 2 * HEADS]


def attend_cache(lengths, q, kv_cache, start, count, before, cost, gates):
    rows = q.shape[1]
    cached, width = kv_cache.shape[1:]
    block = min(8, count)
    skip = start // block
    any_spec = pl.BlockSpec(memory_space=pltpu.HBM)
    return pl.pallas_call(
        functools.partial(cache_body, start),
        grid=(count // block,),
        in_specs=[
            pl.BlockSpec(memory_space=pltpu.SMEM),
            pl.BlockSpec((2, block, HEADS, HD), lambda i: (0, i + skip, 0, 0)),
            pl.BlockSpec((block, cached, width), lambda i: (i + skip, 0, 0)),
            *[any_spec for _ in (*before, *gates)],
        ],
        out_specs=(
            pl.BlockSpec((block, 2 * HEADS, HD), lambda i: (i + skip, 0, 0)),
            pl.BlockSpec((block, 2 * HEADS, 1), lambda i: (i + skip, 0, 0)),
            any_spec,
        ),
        out_shape=(
            pltpu.HBM((rows, 2 * HEADS, HD), jnp.float32),
            pltpu.HBM((rows, 2 * HEADS, 1), jnp.float32),
            FLAG,
        ),
        input_output_aliases={3 + i: i for i in range(len(before))},
        cost_estimate=cost,
        compiler_params=pltpu.CompilerParams(vmem_limit_bytes=ATTEND_VMEM),
        name="attend_cache",
    )(lengths, *in_hbm(q, kv_cache, *before, *gates))


def weigh_body(q_ref, o_ref, lse_ref, keys_ref, prob_ref, out_ref):
    block = q_ref.shape[1]
    shape = (2 * HEADS, 2 * KVH)
    row = lax.broadcasted_iota(jnp.int32, shape, 0)
    col = lax.broadcasted_iota(jnp.int32, shape, 1)
    head = row // (4 * GROUP) * 2 + (row // GROUP) % 2
    step = (row // (2 * GROUP)) % 2
    live = (head == col % KVH) & (col // KVH <= step)
    scale = 1.0 / math.sqrt(HD)
    scores = []
    for r in range(block):
        keys = jnp.concatenate([keys_ref[s, r] for s in range(2)], axis=0).astype(jnp.bfloat16)
        one = lax.dot_general(
            head_rows(q_ref, r), keys, (((1,), (1,)), ((), ())), preferred_element_type=jnp.float32
        ) * scale
        scores.append(jnp.where(live, one, NEG))
    scores = jnp.concatenate(scores, axis=0)
    lse = lse_ref[...].reshape(block * 2 * HEADS, 1)
    top = jnp.maximum(jnp.max(scores, axis=1, keepdims=True), lse)
    expo = jnp.exp(scores - top)
    before = jnp.exp(lse - top)
    inverse = 1.0 / (before + jnp.sum(expo, axis=1, keepdims=True))
    before = before * inverse
    prob_ref[...] = (expo * inverse).astype(jnp.bfloat16).reshape(prob_ref.shape)
    for r in range(block):
        out_ref[r] = o_ref[r] * before[r * 2 * HEADS:(r + 1) * 2 * HEADS]


def weigh_new(q, o, lse, keys):
    rows = q.shape[1]
    block = min(8, rows)
    half = pl.BlockSpec((block, 2 * HEADS, HD), lambda i: (i, 0, 0))
    return pl.pallas_call(
        weigh_body,
        grid=(rows // block,),
        in_specs=[
            pl.BlockSpec((2, block, HEADS, HD), lambda i: (0, i, 0, 0)),
            half,
            pl.BlockSpec((block, 2 * HEADS, 1), lambda i: (i, 0, 0)),
            pl.BlockSpec((2, block, KVH, HD), lambda i: (0, i, 0, 0)),
        ],
        out_specs=(pl.BlockSpec((block, 2 * HEADS, 2 * KVH), lambda i: (i, 0, 0)), half),
        out_shape=(
            pltpu.VMEM((rows, 2 * HEADS, 2 * KVH), jnp.bfloat16),
            pltpu.VMEM(o.shape, jnp.float32),
        ),
        cost_estimate=LIGHT,
        compiler_params=pltpu.CompilerParams(vmem_limit_bytes=ATTEND_VMEM),
        name="weigh_new",
    )(*in_hbm(q, o, lse), keys)


def add_body(prob_ref, o_ref, vals_ref, out_ref, sum_ref):
    block = o_ref.shape[0]
    for r in range(block):
        vals = jnp.concatenate([vals_ref[s, r] for s in range(2)], axis=0).astype(jnp.bfloat16)
        sum_ref[r * 2 * HEADS:(r + 1) * 2 * HEADS, :] = o_ref[r] + jnp.dot(
            prob_ref[r], vals, preferred_element_type=jnp.float32
        )
    some = 2 * GROUP
    for at in range(2 * HEADS):
        pair, step, head = at // (2 * some), (at // some) % 2, at % some
        column = (pair * some + head) * HD
        out_ref[step, :, column:column + HD] = sum_ref[
            pl.ds(at, block, stride=2 * HEADS), :
        ].astype(jnp.bfloat16)


def add_new(probs, o, vals):
    rows = o.shape[0]
    block = min(16, rows)
    return pl.pallas_call(
        add_body,
        grid=(rows // block,),
        in_specs=[
            pl.BlockSpec((block, 2 * HEADS, 2 * KVH), lambda i: (i, 0, 0)),
            pl.BlockSpec((block, 2 * HEADS, HD), lambda i: (i, 0, 0)),
            pl.BlockSpec((2, block, KVH, HD), lambda i: (0, i, 0, 0)),
        ],
        out_specs=pl.BlockSpec((2, block, HEADS * HD), lambda i: (0, i, 0)),
        out_shape=jax.ShapeDtypeStruct((2, rows, HEADS * HD), jnp.bfloat16),
        scratch_shapes=[pltpu.VMEM((block * 2 * HEADS, HD), jnp.float32)],
        cost_estimate=LIGHT,
        compiler_params=pltpu.CompilerParams(vmem_limit_bytes=ATTEND_VMEM),
        name="add_new",
    )(*in_vmem(probs, o), vals)


def marker_body(*refs):
    del refs


def marker(flag):
    any_spec = pl.BlockSpec(memory_space=pltpu.HBM)
    return pl.pallas_call(
        marker_body,
        in_specs=[any_spec],
        out_specs=any_spec,
        out_shape=FLAG,
        cost_estimate=COVER,
        compiler_params=pltpu.CompilerParams(vmem_limit_bytes=1 << 20),
        name="marker",
    )(*in_hbm(flag))


def tie(*values):
    return lax.optimization_barrier(values)


def halves(terms):
    half = terms[0].shape[0] // 2
    return [
        sum(term[begin:begin + half].astype(jnp.float32) for term in terms).astype(jnp.bfloat16)
        for begin in (0, half)
    ]


def sum_of(terms):
    return sum(term.astype(jnp.float32) for term in terms).astype(jnp.bfloat16)


def cross(value, tensor, mask):
    return lax.ppermute(value, "tensor", [(i, i ^ mask) for i in range(tensor)])


def local(
    replicas,
    tensor,
    hidden,
    base_weight,
    delta_values,
    delta_scales,
    tenant_slot,
    seg_tenant,
    seg_length,
    queries,
    kv_cache,
    cache_length,
):
    def swap(value, mask):
        return lax.ppermute(value, "replica", [(i, i ^ mask) for i in range(replicas)])

    rows = hidden.shape[1]
    columns = base_weight.shape[1]
    shard_rows = rows // tensor
    half = columns // 2
    masks = [1 << i for i in range(tensor.bit_length() - 1)]
    flat = hidden.reshape(2 * rows, hidden.shape[2])
    piece = shard_rows // 2
    masks_far = list(range(2, replicas, 2))

    place = jnp.stack([lax.axis_index("replica") * SLOTS, lax.axis_index("tensor")]).astype(jnp.int32)
    far = [swap(flat, mask) for mask in masks_far]
    sibling = swap(flat, 1)
    meta = jnp.concatenate([seg_tenant, seg_length], axis=1)
    meta = jnp.concatenate([meta, swap(meta, 1)], axis=0)
    far_meta = [swap(meta, mask) for mask in masks_far]

    def cached(at, before, flag):
        return attend_cache(cache_length, q, kv_cache, at * piece, piece, before, LIGHT, [flag])

    own, other, flag = delta_rows(
        place, tenant_slot, meta, flat, sibling, delta_values, delta_scales, tensor, base_weight
    )
    back = swap(other, 1)
    queries, flag = tie(queries, flag)
    q, flag = tie(queries.reshape(2, shard_rows, HEADS, HD), flag)
    flag = marker(flag)
    back, flag = tie(back, flag)
    sent, kept = halves([own, back])
    sent, far, flag = tie(sent, far, flag)
    theirs_in = [swap(rows_in, 1) for rows_in in far]
    near = [kept, cross(sent, tensor, masks[0])]

    flying = []
    for mask, pair, far_rows, far_sibling in zip(masks_far, far_meta, far, theirs_in):
        for start in (0, half):
            mine, theirs, flag = delta_rows(
                place, tenant_slot, pair, far_rows, far_sibling, delta_values, delta_scales,
                tensor, None, start, half, [flag],
            )
            back = swap(theirs, 1)
            if flying:
                flying[-1], flag = tie(flying[-1], flag)
                flying[-1] = swap(sum_of(flying[-1]), flying_mask)
            else:
                near, flag = tie(near, flag)
                near = sum_of(near)
            flag = marker(flag)
            back, flag = tie(back, flag)
            sent, kept = halves([mine, back])
            sent, flag = tie(sent, flag)
            flying.append([kept, cross(sent, tensor, masks[0])])
            flying_mask = mask

    *done, flag = cached(0, (), flag)
    flying, flag = tie(flying, flag)
    last = sum_of(flying[-1])
    values = [[near[:, start:start + half], *flying[at::2]] for at, start in enumerate((0, half))]
    sent, kept = halves(values[0])
    last, sent, flag = tie(last, sent, flag)
    values[1][-1] = swap(last, flying_mask)
    values[0] = [kept, cross(sent, tensor, masks[1])]
    *done, flag = cached(1, done, flag)
    values, done = tie(values, done)
    finals = []
    for at, value in enumerate(values):
        for mask in masks[2 - at:]:
            sent, kept = halves(value)
            value = [kept, cross(sent, tensor, mask)]
        finals.append(value)

    def by_head(value):
        return value.astype(jnp.float32).reshape(2, shard_rows, KVH, HD)

    keys = sum_of(finals[0]).reshape(2, shard_rows, half)
    probs, weighed = weigh_new(q, *done, by_head(keys))
    last, probs = tie(finals[1], probs)
    vals = sum_of(last).reshape(2, shard_rows, half)
    attention = add_new(probs, weighed, by_head(vals))
    return (jnp.concatenate([keys, vals], axis=2), attention)


def solution(mesh):
    placed = (
        P(None, ("groups", "replica"), "tensor"),
        P("tensor", None),
        P(("groups", "replica"), "tensor", None),
        P(("groups", "replica"), "tensor", None),
        P(),
        P(("groups", "replica"), None),
        P(("groups", "replica"), None),
        P(None, ("groups", "replica", "tensor"), None),
        P(("groups", "replica", "tensor"), None, None),
        P(("groups", "replica", "tensor")),
    )
    return jax.shard_map(
        functools.partial(local, mesh.shape["replica"], mesh.shape["tensor"]),
        mesh=mesh,
        in_specs=placed,
        out_specs=(
            P(None, ("groups", "replica", "tensor"), None),
            P(None, ("groups", "replica", "tensor"), None),
        ),
        check_vma=False,
    )
```

time: 108 us -> 84.8 us (0.79)
  waiting for transfers between devices: 25.5 us -> 14.8 us
  local copies, waits for them, and re-layouts: 7.38 us -> 2.67 us
  starting transfers between devices: 19.7 us -> 16.5 us
  Pallas kernels: 49.3 us -> 46.3 us
  other arithmetic: 5.06 us -> 3.52 us
    ppermute x6 -> x5, waiting for transfers between devices: 19.8 us -> 5.12 us  [cross(): return lax.ppermute(value, 'tensor', [(i, i ^ mask) for i in range(tensor)])]
    ppermute x12 -> x10, waiting for transfers between devices: 5.69 us -> 9.66 us  [swap(): lax.ppermute(value, 'replica', [(i, i ^ mask) for i in range(replicas)])]
    pallas_call x4 -> x2, Pallas kernels: 15.4 us -> 11.6 us  [attend_cache(): pl.pallas_call(functools.partial(cache_body, start), grid=(count // block...]
    slice x2, local copies, waits for them, and re-layouts: 3.77 us -> 0.01 us  [local(): near[:, start:start + half]]
    ppermute x6 -> x5, starting transfers between devices: 10.4 us -> 8.24 us  [cross(): return lax.ppermute(value, 'tensor', [(i, i ^ mask) for i in range(tensor)])]
    convert_element_type x9 -> x8, other arithmetic: 3.14 us -> 1.17 us  [the longest x5 0.91 us: halves(): sum((term[begin:begin + half].astype(jnp.float32) for term in terms))]
    reshape x1 -> x0, local copies, waits for them, and re-layouts: 1.27 us -> none  [local(): return (new_kv, attention.reshape(2, shard_rows, HEADS * HD))]
    ppermute x12 -> x10, starting transfers between devices: 9.23 us -> 8.23 us  [swap(): lax.ppermute(value, 'replica', [(i, i ^ mask) for i in range(replicas)])]
  transfers between devices with their start and end apart: 18 -> 15, of which waited for: 7 -> 10; matrix products, arithmetic and copies ran while one was open for 7% -> 4% of each run, Pallas kernels for 40% -> 52%
where the time goes in v3:
time: 84.8 us; the launch traced here: 84.6 us
  Pallas kernels  46.3 us (55%)
  starting transfers between devices  16.5 us (19%)
  waiting for transfers between devices  14.8 us (17%)
  other arithmetic  3.52 us (4%)
  local copies, waits for them, and re-layouts  2.67 us (3%)
    pallas_call x3, Pallas kernels, delta_rows(): pl.pallas_call(functools.partial(delta_body, base is not None, tensor, st...  26.3 us
    pallas_call x2, Pallas kernels, attend_cache(): pl.pallas_call(functools.partial(cache_body, start), grid=(count // block...  11.6 us
    ppermute x10, waiting for transfers between devices, swap(): lax.ppermute(value, 'replica', [(i, i ^ mask) for i in range(replicas)])  9.66 us
    ppermute x5, starting transfers between devices, cross(): return lax.ppermute(value, 'tensor', [(i, i ^ mask) for i in range(tensor)])  8.24 us
    ppermute x10, starting transfers between devices, swap(): lax.ppermute(value, 'replica', [(i, i ^ mask) for i in range(replicas)])  8.23 us
    pallas_call x1, Pallas kernels, weigh_new(): pl.pallas_call(weigh_body, grid=(rows // block,), in_specs=[pl.BlockSpec(...  5.75 us
    ppermute x5, waiting for transfers between devices, cross(): return lax.ppermute(value, 'tensor', [(i, i ^ mask) for i in range(tensor)])  5.12 us
    pallas_call x1, Pallas kernels, add_new(): pl.pallas_call(add_body, grid=(rows // block,), in_specs=[pl.BlockSpec((b...  2.71 us
  transfers between devices with their start and end apart: 15, of which 10 were waited for; matrix products, arithmetic and copies ran while one was open for 4% of the time, Pallas kernels for 52%

profile of v3, /device:TPU:0, one launch (start us, length us, event | category | flops | bytes accessed | tf_op | source)
XLA Modules:
  0.0 84.6 jit_solution(6990588857176727772)
XLA Ops:
  1.1 2.6 %collective-permute-start.3 = (bf16[256,2048]{1,0:T(8,128)(2,1)}, bf16[256,2048]{1,0:T(8,128)(2,1)S(1)}, u32[]{:S(2)}, u32[]{:S(2)}) collective-permute-start(bf16[256,2048]{1,0:T(8,128)(2,1)} %bitcast.18), channel_id=1, source_target_pairs={{0,2},{1,3},{2,0},{3,1},{4,6},{5,7},{6,4},{7,5},{8,10},{9,11},{10,... | collective-permute-start | bytes 3145736 | tf_op jit(solution)/shard_map/ppermute | solution.py:391
  4.7 0.9 %collective-permute-done = s32[1,8]{1,0:T(1,128)S(1)} collective-permute-done((s32[1,8]{1,0:T(1,128)S(1)}, s32[1,8]{1,0:T(1,128)S(1)}, u32[]{:S(2)}, u32[]{:S(2)}) %collective-permute-start) | collective-permute-done | bytes 64 | tf_op jit(solution)/shard_map/ppermute | solution.py:391
  6.3 1.2 %copy-done = bf16[2,128,2048]{2,1,0:T(8,128)(2,1)S(1)} copy-done((bf16[2,128,2048]{2,1,0:T(8,128)(2,1)S(1)}, bf16[2,128,2048]{2,1,0:T(8,128)(2,1)}, u32[]{:S(2)}) %copy-start) | copy-done | bytes 1048600
  7.6 13.6 %delta_rows.3 = (bf16[256,2048]{1,0:T(8,128)(2,1)}, bf16[256,2048]{1,0:T(8,128)(2,1)}, f32[8,128]{1,0:T(8,128)}) custom-call(s32[2]{0:T(128)S(1)} %pad_add_fusion.1.refs_0_, s32[8]{0:T(128)} %refs_1_.5, s32[2,8]{1,0:T(2,128)S(1)} %pad_add_fusion.refs_2_, bf16[256,2048]{1,0:T(8,128)(2,1)S(1)} %bitcast.19, ...), custom_call_target="tpu_custom_call" | custom-call | flops 1 | bytes 1 | tf_op jit(solution)/shard_map/delta_rows/pallas_call | solution.py:149
  21.2 1.3 %copy.14 = bf16[8,8,64,128]{3,2,1,0:T(8,128)(2,1)} copy(bf16[8,8,64,128]{3,1,2,0:T(8,128)(2,1)S(1)} %bitcast.25) | data formatting | bytes 2097152
  22.7 2.5 %collective-permute-done.2 = bf16[256,2048]{1,0:T(8,128)(2,1)S(1)} collective-permute-done((bf16[256,2048]{1,0:T(8,128)(2,1)S(1)}, bf16[256,2048]{1,0:T(8,128)(2,1)S(1)}, u32[]{:S(2)}, u32[]{:S(2)}) %collective-permute-start.2) | collective-permute-done | bytes 1048608 | tf_op jit(solution)/shard_map/ppermute | solution.py:391
  25.6 2.1 %collective-permute-done.3.refs_3_ = bf16[256,2048]{1,0:T(8,128)(2,1)S(1)} collective-permute-done((bf16[256,2048]{1,0:T(8,128)(2,1)}, bf16[256,2048]{1,0:T(8,128)(2,1)S(1)}, u32[]{:S(2)}, u32[]{:S(2)}) %collective-permute-start.3) | collective-permute-done | bytes 1048608 | tf_op jit(solution)/shard_map/ppermute | solution.py:391
  27.7 1.8 %collective-permute-start.4 = (bf16[128,2048]{1,0:T(8,128)(2,1)S(1)}, bf16[128,2048]{1,0:T(8,128)(2,1)S(1)}, u32[]{:S(2)}, u32[]{:S(2)}) collective-permute-start(bf16[128,2048]{1,0:T(8,128)(2,1)S(1)} %get-tuple-element.65), channel_id=1, source_target_pairs={{0,4},{4,0},{8,12},{12,8},{1,5},{5,1},{9,13},{13,9},{2,6},{6,2},{1... | collective-permute-start | bytes 1572872 | tf_op jit(solution)/shard_map/ppermute | solution.py:373
  29.5 1.5 %collective-permute-start.5 = (s32[2,8]{1,0:T(2,128)S(1)}, s32[2,8]{1,0:T(2,128)S(1)}, u32[]{:S(2)}, u32[]{:S(2)}) collective-permute-start(s32[2,8]{1,0:T(2,128)S(1)} %pad_add_fusion.refs_2_), channel_id=1, source_target_pairs={{0,2},{1,3},{2,0},{3,1},{4,6},{5,7},{6,4},{7,5},{8,10},{9,11},{10,... | collective-permute-start | bytes 200 | tf_op jit(solution)/shard_map/ppermute | solution.py:391
  31.0 2.1 %collective-permute-done.5.refs_2_ = s32[2,8]{1,0:T(2,128)S(1)} collective-permute-done((s32[2,8]{1,0:T(2,128)S(1)}, s32[2,8]{1,0:T(2,128)S(1)}, u32[]{:S(2)}, u32[]{:S(2)}) %collective-permute-start.5) | collective-permute-done | bytes 96 | tf_op jit(solution)/shard_map/ppermute | solution.py:391
  33.1 6.3 %delta_rows.4 = (bf16[256,1024]{1,0:T(8,128)(2,1)}, bf16[256,1024]{1,0:T(8,128)(2,1)}, f32[8,128]{1,0:T(8,128)}) custom-call(s32[2]{0:T(128)S(1)} %pad_add_fusion.1.refs_0_, s32[8]{0:T(128)} %refs_1_.5, s32[2,8]{1,0:T(2,128)S(1)} %collective-permute-done.5.refs_2_, bf16[256,2048]{1,0:T(8,128)(2,1)S(1)} %collective-permute-done.3.refs_3_, ...), custom_call_target="tpu_custom_call" | custom-call | flops 1 | bytes 1 | tf_op jit(solution)/shard_map/delta_rows/pallas_call | solution.py:149
  39.4 2.7 %collective-permute-done.4 = bf16[128,2048]{1,0:T(8,128)(2,1)S(1)} collective-permute-done((bf16[128,2048]{1,0:T(8,128)(2,1)S(1)}, bf16[128,2048]{1,0:T(8,128)(2,1)S(1)}, u32[]{:S(2)}, u32[]{:S(2)}) %collective-permute-start.4) | collective-permute-done | bytes 524320 | tf_op jit(solution)/shard_map/ppermute | solution.py:373
  42.1 2.1 %collective-permute-done.7 = bf16[256,1024]{1,0:T(8,128)(2,1)S(1)} collective-permute-done((bf16[256,1024]{1,0:T(8,128)(2,1)}, bf16[256,1024]{1,0:T(8,128)(2,1)S(1)}, u32[]{:S(2)}, u32[]{:S(2)}) %collective-permute-start.7) | collective-permute-done | bytes 524320 | tf_op jit(solution)/shard_map/ppermute | solution.py:391
  44.4 1.8 %collective-permute-start.8 = (bf16[128,1024]{1,0:T(8,128)(2,1)S(1)}, bf16[128,1024]{1,0:T(8,128)(2,1)S(1)}, u32[]{:S(2)}, u32[]{:S(2)}) collective-permute-start(bf16[128,1024]{1,0:T(8,128)(2,1)S(1)} %get-tuple-element.76), channel_id=1, source_target_pairs={{0,4},{4,0},{8,12},{12,8},{1,5},{5,1},{9,13},{13,9},{2,6},{6,2},{1... | collective-permute-start | bytes 786440 | tf_op jit(solution)/shard_map/ppermute | solution.py:373
  46.2 6.3 %delta_rows.5 = (bf16[256,1024]{1,0:T(8,128)(2,1)}, bf16[256,1024]{1,0:T(8,128)(2,1)}, f32[8,128]{1,0:T(8,128)}) custom-call(s32[2]{0:T(128)S(1)} %pad_add_fusion.1.refs_0_, s32[8]{0:T(128)} %refs_1_.5, s32[2,8]{1,0:T(2,128)S(1)} %collective-permute-done.5.refs_2_, bf16[256,2048]{1,0:T(8,128)(2,1)S(1)} %collective-permute-done.3.refs_3_, ...), custom_call_target="tpu_custom_call" | custom-call | flops 1 | bytes 1 | tf_op jit(solution)/shard_map/delta_rows/pallas_call | solution.py:149
  52.9 1.7 %collective-permute-start.9 = (bf16[128,1024]{1,0:T(8,128)(2,1)S(1)}, bf16[128,1024]{1,0:T(8,128)(2,1)S(1)}, u32[]{:S(2)}, u32[]{:S(2)}) collective-permute-start(bf16[128,1024]{1,0:T(8,128)(2,1)S(1)} %add_convert_fusion.6), channel_id=1, source_target_pairs={{0,2},{1,3},{2,0},{3,1},{4,6},{5,7},{6,4},{7,5},{8,10},{9,11},{10,... | collective-permute-start | bytes 786440 | tf_op jit(solution)/shard_map/ppermute | solution.py:391
  54.9 1.6 %collective-permute-start.11 = (bf16[128,1024]{1,0:T(8,128)(2,1)S(1)}, bf16[128,1024]{1,0:T(8,128)(2,1)S(1)}, u32[]{:S(2)}, u32[]{:S(2)}) collective-permute-start(bf16[128,1024]{1,0:T(8,128)(2,1)S(1)} %get-tuple-element.86), channel_id=1, source_target_pairs={{0,4},{4,0},{8,12},{12,8},{1,5},{5,1},{9,13},{13,9},{2,6},{6,2},{1... | collective-permute-start | bytes 786440 | tf_op jit(solution)/shard_map/ppermute | solution.py:373
  56.6 5.8 %attend_cache.2 = (f32[32,128,128]{2,1,0:T(8,128)}, f32[32,128,1]{2,1,0:T(8,128)}, f32[8,128]{1,0:T(8,128)}) custom-call(s32[32]{0:T(128)S(1)} %copy-done.1, bf16[2,32,64,128]{3,2,1,0:T(8,128)(2,1)} %bitcast.22, bf16[32,128,2048]{2,1,0:T(8,128)(2,1)} %kv_ref.3, f32[8,128]{1,0:T(8,128)} %marker.5.refs_0_), custom_call_target="tpu_custom_call" | custom-call | flops 1 | bytes 1 | tf_op jit(solution)/shard_map/attend_cache/pallas_call | solution.py:225
  63.4 1.6 %collective-permute-start.13 = (bf16[128,1024]{1,0:T(8,128)(2,1)S(1)}, bf16[128,1024]{1,0:T(8,128)(2,1)S(1)}, u32[]{:S(2)}, u32[]{:S(2)}) collective-permute-start(bf16[128,1024]{1,0:T(8,128)(2,1)S(1)} %add_convert_fusion.3), channel_id=1, source_target_pairs={{0,2},{1,3},{2,0},{3,1},{4,6},{5,7},{6,4},{7,5},{8,10},{9,11},{10,... | collective-permute-start | bytes 786440 | tf_op jit(solution)/shard_map/ppermute | solution.py:391
  65.0 2.6 %collective-permute-start.12 = (bf16[64,1024]{1,0:T(8,128)(2,1)S(1)}, bf16[64,1024]{1,0:T(8,128)(2,1)S(1)}, u32[]{:S(2)}, u32[]{:S(2)}) collective-permute-start(bf16[64,1024]{1,0:T(8,128)(2,1)S(1)} %get-tuple-element.94), channel_id=1, source_target_pairs={{0,8},{4,12},{8,0},{12,4},{1,9},{5,13},{9,1},{13,5},{2,10},{6,14},... | collective-permute-start | bytes 393224 | tf_op jit(solution)/shard_map/ppermute | solution.py:373
  67.6 5.7 %attend_cache.3 = (f32[32,128,128]{2,1,0:T(8,128)}, f32[32,128,1]{2,1,0:T(8,128)}, f32[8,128]{1,0:T(8,128)}) custom-call(s32[32]{0:T(128)S(1)} %copy-done.1, bf16[2,32,64,128]{3,2,1,0:T(8,128)(2,1)} %bitcast.23, bf16[32,128,2048]{2,1,0:T(8,128)(2,1)} %kv_ref.3, ...), custom_call_target="tpu_custom_call", output_to_operand_aliasing={{0}: (3, {}), {1}: (4, {})} | custom-call | flops 1 | bytes 1 | tf_op jit(solution)/shard_map/attend_cache/pallas_call | solution.py:225
  73.9 5.7 %weigh_new.1 = (bf16[32,128,16]{2,1,0:T(8,128)(2,1)S(1)}, f32[32,128,128]{2,1,0:T(8,128)S(1)}) custom-call(bf16[2,32,64,128]{3,2,1,0:T(8,128)(2,1)} %bitcast.24, f32[32,128,128]{2,1,0:T(8,128)} %get-tuple-element.105.o_ref, f32[32,128,1]{2,1,0:T(8,128)} %get-tuple-element.106.lse_ref, f32[2,32,8,128]{3,2,1,0:T(8,128)S(1)} %bitcast.21), custom_call_target="tpu_custom_call" | custom-call | flops 1 | bytes 1 | tf_op jit(solution)/shard_map/weigh_new/pallas_call | solution.py:283
  79.7 1.4 %collective-permute-done.14 = bf16[64,1024]{1,0:T(8,128)(2,1)S(1)} collective-permute-done((bf16[64,1024]{1,0:T(8,128)(2,1)S(1)}, bf16[64,1024]{1,0:T(8,128)(2,1)S(1)}, u32[]{:S(2)}, u32[]{:S(2)}) %collective-permute-start.14) | collective-permute-done | bytes 131104 | tf_op jit(solution)/shard_map/ppermute | solution.py:373
  81.9 2.7 %add_new.1 = bf16[2,32,8192]{2,1,0:T(8,128)(2,1)} custom-call(bf16[32,128,16]{2,1,0:T(8,128)(2,1)S(1)} %get-tuple-element.110.prob_ref, f32[32,128,128]{2,1,0:T(8,128)S(1)} %get-tuple-element.111.o_ref, f32[2,32,8,128]{3,2,1,0:T(8,128)S(1)} %bitcast.20), custom_call_target="tpu_custom_call" | custom-call | flops 1 | bytes 1 | tf_op jit(solution)/shard_map/add_new/pallas_call | solution.py:322
  (51 shorter events, 6.1 us)
Async XLA Ops:
  0.6 5.7 %collective-permute-start.1 = (bf16[256,2048]{1,0:T(8,128)(2,1)}, bf16[256,2048]{1,0:T(8,128)(2,1)S(1)}, u32[]{:S(2)}, u32[]{:S(2)}) collective-permute-start(bf16[256,2048]{1,0:T(8,128)(2,1)} %bitcast.17), channel_id=1, source_target_pairs={{0,1},{1,0},{2,3},{3,2},{4,5},{5,4},{6,7},{7,6},{8,9},{9,8},{10,11... | collective-permute-start | bytes 3145736 | tf_op jit(solution)/shard_map/ppermute | solution.py:391
  1.1 26.5 %collective-permute-start.3 = (bf16[256,2048]{1,0:T(8,128)(2,1)}, bf16[256,2048]{1,0:T(8,128)(2,1)S(1)}, u32[]{:S(2)}, u32[]{:S(2)}) collective-permute-start(bf16[256,2048]{1,0:T(8,128)(2,1)} %bitcast.18), channel_id=1, source_target_pairs={{0,2},{1,3},{2,0},{3,1},{4,6},{5,7},{6,4},{7,5},{8,10},{9,11},{10,... | collective-permute-start | bytes 3145736 | tf_op jit(solution)/shard_map/ppermute | solution.py:391
  4.5 1.1 %collective-permute-start = (s32[1,8]{1,0:T(1,128)S(1)}, s32[1,8]{1,0:T(1,128)S(1)}, u32[]{:S(2)}, u32[]{:S(2)}) collective-permute-start(s32[1,8]{1,0:T(1,128)S(1)} %pad_add_fusion.2), channel_id=1, source_target_pairs={{0,1},{1,0},{2,3},{3,2},{4,5},{5,4},{6,7},{7,6},{8,9},{9,8},{10,11... | collective-permute-start | bytes 104 | tf_op jit(solution)/shard_map/ppermute | solution.py:391
  6.3 1.2 %copy-start = (bf16[2,128,2048]{2,1,0:T(8,128)(2,1)S(1)}, bf16[2,128,2048]{2,1,0:T(8,128)(2,1)}, u32[]{:S(2)}) copy-start(bf16[2,128,2048]{2,1,0:T(8,128)(2,1)} %param.10) | copy-start | bytes 3145732
  7.6 13.6 %copy-start.4 = (bf16[2,32,8192]{2,1,0:T(8,128)(2,1)S(1)}, bf16[2,32,8192]{2,1,0:T(8,128)(2,1)}, u32[]{:S(2)}) copy-start(bf16[2,32,8192]{2,1,0:T(8,128)(2,1)} %param.17) | copy-start | bytes 3145732
  21.2 1.3 %copy-start.7 = (bf16[256,2048]{1,0:T(8,128)(2,1)S(1)}, bf16[256,2048]{1,0:T(8,128)(2,1)}, u32[]{:S(2)}) copy-start(bf16[256,2048]{1,0:T(8,128)(2,1)} %get-tuple-element.58) | copy-start | bytes 3145732
  22.5 2.7 %copy-start.3 = (bf16[256,2048]{1,0:T(8,128)(2,1)S(1)}, bf16[256,2048]{1,0:T(8,128)(2,1)}, u32[]{:S(2)}) copy-start(bf16[256,2048]{1,0:T(8,128)(2,1)} %get-tuple-element.57) | copy-start | bytes 3145732
  22.5 2.7 %collective-permute-start.2 = (bf16[256,2048]{1,0:T(8,128)(2,1)S(1)}, bf16[256,2048]{1,0:T(8,128)(2,1)S(1)}, u32[]{:S(2)}, u32[]{:S(2)}) collective-permute-start(bf16[256,2048]{1,0:T(8,128)(2,1)S(1)} %copy-done.7), channel_id=1, source_target_pairs={{0,1},{1,0},{2,3},{3,2},{4,5},{5,4},{6,7},{7,6},{8,9},{9,8},{10,11... | collective-permute-start | bytes 3145736 | tf_op jit(solution)/shard_map/ppermute | solution.py:391
  27.7 5.4 %collective-permute-start.6 = (bf16[256,2048]{1,0:T(8,128)(2,1)S(1)}, bf16[256,2048]{1,0:T(8,128)(2,1)S(1)}, u32[]{:S(2)}, u32[]{:S(2)}) collective-permute-start(bf16[256,2048]{1,0:T(8,128)(2,1)S(1)} %collective-permute-done.3.refs_3_), channel_id=1, source_target_pairs={{0,1},{1,0},{2,3},{3,2},{4,5},{5,4},{6,7},{7,6},{8,9},{9,8},{10,11... | collective-permute-start | bytes 3145736 | tf_op jit(solution)/shard_map/ppermute | solution.py:391
  27.7 14.4 %collective-permute-start.4 = (bf16[128,2048]{1,0:T(8,128)(2,1)S(1)}, bf16[128,2048]{1,0:T(8,128)(2,1)S(1)}, u32[]{:S(2)}, u32[]{:S(2)}) collective-permute-start(bf16[128,2048]{1,0:T(8,128)(2,1)S(1)} %get-tuple-element.65), channel_id=1, source_target_pairs={{0,4},{4,0},{8,12},{12,8},{1,5},{5,1},{9,13},{13,9},{2,6},{6,2},{1... | collective-permute-start | bytes 1572872 | tf_op jit(solution)/shard_map/ppermute | solution.py:373
  29.5 3.6 %collective-permute-start.5 = (s32[2,8]{1,0:T(2,128)S(1)}, s32[2,8]{1,0:T(2,128)S(1)}, u32[]{:S(2)}, u32[]{:S(2)}) collective-permute-start(s32[2,8]{1,0:T(2,128)S(1)} %pad_add_fusion.refs_2_), channel_id=1, source_target_pairs={{0,2},{1,3},{2,0},{3,1},{4,6},{5,7},{6,4},{7,5},{8,10},{9,11},{10,... | collective-permute-start | bytes 200 | tf_op jit(solution)/shard_map/ppermute | solution.py:391
  42.1 2.1 %copy-start.6 = (bf16[256,1024]{1,0:T(8,128)(2,1)S(1)}, bf16[256,1024]{1,0:T(8,128)(2,1)}, u32[]{:S(2)}) copy-start(bf16[256,1024]{1,0:T(8,128)(2,1)} %get-tuple-element.71) | copy-start | bytes 1572868
  42.1 2.1 %collective-permute-start.7 = (bf16[256,1024]{1,0:T(8,128)(2,1)}, bf16[256,1024]{1,0:T(8,128)(2,1)S(1)}, u32[]{:S(2)}, u32[]{:S(2)}) collective-permute-start(bf16[256,1024]{1,0:T(8,128)(2,1)} %get-tuple-element.72), channel_id=1, source_target_pairs={{0,1},{1,0},{2,3},{3,2},{4,5},{5,4},{6,7},{7,6},{8,9},{9,8},{10,11... | collective-permute-start | bytes 1572872 | tf_op jit(solution)/shard_map/ppermute | solution.py:391
  44.4 8.4 %collective-permute-start.8 = (bf16[128,1024]{1,0:T(8,128)(2,1)S(1)}, bf16[128,1024]{1,0:T(8,128)(2,1)S(1)}, u32[]{:S(2)}, u32[]{:S(2)}) collective-permute-start(bf16[128,1024]{1,0:T(8,128)(2,1)S(1)} %get-tuple-element.76), channel_id=1, source_target_pairs={{0,4},{4,0},{8,12},{12,8},{1,5},{5,1},{9,13},{13,9},{2,6},{6,2},{1... | collective-permute-start | bytes 786440 | tf_op jit(solution)/shard_map/ppermute | solution.py:373
  52.6 2.1 %collective-permute-start.10 = (bf16[256,1024]{1,0:T(8,128)(2,1)}, bf16[256,1024]{1,0:T(8,128)(2,1)S(1)}, u32[]{:S(2)}, u32[]{:S(2)}) collective-permute-start(bf16[256,1024]{1,0:T(8,128)(2,1)} %get-tuple-element.82), channel_id=1, source_target_pairs={{0,1},{1,0},{2,3},{3,2},{4,5},{5,4},{6,7},{7,6},{8,9},{9,8},{10,11... | collective-permute-start | bytes 1572872 | tf_op jit(solution)/shard_map/ppermute | solution.py:391
  52.9 1.9 %copy-start.5 = (bf16[256,1024]{1,0:T(8,128)(2,1)S(1)}, bf16[256,1024]{1,0:T(8,128)(2,1)}, u32[]{:S(2)}) copy-start(bf16[256,1024]{1,0:T(8,128)(2,1)} %get-tuple-element.81) | copy-start | bytes 1572868
  52.9 3.8 %copy-start.1 = (s32[32]{0:T(128)S(1)}, s32[32]{0:T(128)}, u32[]{:S(2)}) copy-start(s32[32]{0:T(128)} %len_ref.3) | copy-start | bytes 388
  52.9 9.6 %collective-permute-start.9 = (bf16[128,1024]{1,0:T(8,128)(2,1)S(1)}, bf16[128,1024]{1,0:T(8,128)(2,1)S(1)}, u32[]{:S(2)}, u32[]{:S(2)}) collective-permute-start(bf16[128,1024]{1,0:T(8,128)(2,1)S(1)} %add_convert_fusion.6), channel_id=1, source_target_pairs={{0,2},{1,3},{2,0},{3,1},{4,6},{5,7},{6,4},{7,5},{8,10},{9,11},{10,... | collective-permute-start | bytes 786440 | tf_op jit(solution)/shard_map/ppermute | solution.py:391
  54.9 8.4 %collective-permute-start.11 = (bf16[128,1024]{1,0:T(8,128)(2,1)S(1)}, bf16[128,1024]{1,0:T(8,128)(2,1)S(1)}, u32[]{:S(2)}, u32[]{:S(2)}) collective-permute-start(bf16[128,1024]{1,0:T(8,128)(2,1)S(1)} %get-tuple-element.86), channel_id=1, source_target_pairs={{0,4},{4,0},{8,12},{12,8},{1,5},{5,1},{9,13},{13,9},{2,6},{6,2},{1... | collective-permute-start | bytes 786440 | tf_op jit(solution)/shard_map/ppermute | solution.py:373
  56.6 11.0 %copy-start.2 = (bf16[128,2048]{1,0:T(8,128)(2,1)}, bf16[128,2048]{1,0:T(8,128)(2,1)S(1)}, u32[]{:S(2)}) copy-start(bf16[128,2048]{1,0:T(8,128)(2,1)S(1)} %add_convert_fusion) | copy-start | bytes 1572868
  63.4 9.9 %collective-permute-start.13 = (bf16[128,1024]{1,0:T(8,128)(2,1)S(1)}, bf16[128,1024]{1,0:T(8,128)(2,1)S(1)}, u32[]{:S(2)}, u32[]{:S(2)}) collective-permute-start(bf16[128,1024]{1,0:T(8,128)(2,1)S(1)} %add_convert_fusion.3), channel_id=1, source_target_pairs={{0,2},{1,3},{2,0},{3,1},{4,6},{5,7},{6,4},{7,5},{8,10},{9,11},{10,... | collective-permute-start | bytes 786440 | tf_op jit(solution)/shard_map/ppermute | solution.py:391
  65.0 8.3 %collective-permute-start.12 = (bf16[64,1024]{1,0:T(8,128)(2,1)S(1)}, bf16[64,1024]{1,0:T(8,128)(2,1)S(1)}, u32[]{:S(2)}, u32[]{:S(2)}) collective-permute-start(bf16[64,1024]{1,0:T(8,128)(2,1)S(1)} %get-tuple-element.94), channel_id=1, source_target_pairs={{0,8},{4,12},{8,0},{12,4},{1,9},{5,13},{9,1},{13,5},{2,10},{6,14},... | collective-permute-start | bytes 393224 | tf_op jit(solution)/shard_map/ppermute | solution.py:373
  67.6 5.8 %slice-start = ((bf16[128,2048]{1,0:T(8,128)(2,1)}), bf16[128,1024]{1,0:T(8,128)(2,1)S(1)}, s32[]{:S(2)}) async-start(bf16[128,2048]{1,0:T(8,128)(2,1)} %copy-done.2), calls=%async_computation | async-start | bytes 524288 | tf_op jit(solution)/shard_map/slice | solution.py:449
  73.4 7.6 %collective-permute-start.14 = (bf16[64,1024]{1,0:T(8,128)(2,1)S(1)}, bf16[64,1024]{1,0:T(8,128)(2,1)S(1)}, u32[]{:S(2)}, u32[]{:S(2)}) collective-permute-start(bf16[64,1024]{1,0:T(8,128)(2,1)S(1)} %get-tuple-element.124), channel_id=1, source_target_pairs={{0,8},{4,12},{8,0},{12,4},{1,9},{5,13},{9,1},{13,5},{2,10},{6,14},... | collective-permute-start | bytes 393224 | tf_op jit(solution)/shard_map/ppermute | solution.py:373

commit v4 on v3

--- a/solution.py
+++ b/solution.py
@@ -16,6 +16,7 @@
 BLOCK = 128
 SEG_MOST = 40
 SLOTS = 2
+QUARTERS = 4
 NEG = -1e30
 DELTA_VMEM = 50 * 1024 * 1024
 ATTEND_VMEM = 50 * 1024 * 1024
@@ -63,16 +64,16 @@
     return place
 
 
-def delta_body(with_base, tensor, steps, rows, *refs):
-    place_ref, slot_ref, meta_ref, xa_ref, xb_ref, val_ref, sc_ref, base_ref = refs[:8]
+def delta_body(with_base, tensor, steps, rows, chunks, *refs):
+    place_ref, slot_ref, meta_ref, xa_ref = refs[:4]
+    xb_refs = refs[4:4 + chunks]
+    val_ref, sc_ref, base_ref = refs[4 + chunks:7 + chunks]
     if with_base:
-        da_ref, db_ref, _, xc_ref, scatter_ref, xo_ref = refs[-6:]
+        da_ref, *db_refs, _, xc_ref, scatter_ref, xo_ref = refs[-5 - QUARTERS:]
     else:
-        da_ref, db_ref, _, xc_ref, scatter_ref = refs[-5:]
-    width = val_ref.shape[1]
+        da_ref, *db_refs, _, xc_ref, scatter_ref = refs[-4 - QUARTERS:]
     half = steps * rows
     taken = SLOTS * 2 * steps * SEG_MOST
-    per_slot = taken // SLOTS
 
     @pl.when(pl.program_id(0) == 0)
     def _():
@@ -81,7 +82,8 @@
         along = row_positions(meta_ref, slot_ref, first, steps, rows, flat // half, flat % half)
         picks = (lax.broadcasted_iota(jnp.int32, (taken, 2 * half), 0) == along).astype(jnp.bfloat16)
         got = jnp.dot(picks[:, :half], xa_ref[...], preferred_element_type=jnp.float32)
-        got += jnp.dot(picks[:, half:], xb_ref[...], preferred_element_type=jnp.float32)
+        xb = jnp.concatenate([ref[...] for ref in xb_refs], axis=0)
+        got += jnp.dot(picks[:, half:], xb, preferred_element_type=jnp.float32)
         xc_ref[...] = got.astype(jnp.bfloat16)
         order = scatter_order(me, tensor, steps, rows, (1, 2 * half), 1)
         along = row_positions(meta_ref, slot_ref, first, steps, rows, flat // half, order)
@@ -94,6 +96,23 @@
                 preferred_element_type=jnp.float32,
             ).astype(jnp.bfloat16)
 
+    spread = spread_products(xc_ref, scatter_ref, val_ref, sc_ref)
+    own = spread[:half]
+    if with_base:
+        own = own + jnp.dot(xo_ref[...], base_ref[...], preferred_element_type=jnp.float32)
+    da_ref[...] = own.astype(da_ref.dtype)
+    put_quarters(db_refs, spread[half:])
+
+
+def put_quarters(refs, value):
+    rows = value.shape[0] // QUARTERS
+    for at, ref in enumerate(refs):
+        ref[...] = value[at * rows:(at + 1) * rows].astype(ref.dtype)
+
+
+def spread_products(xc_ref, scatter_ref, val_ref, sc_ref):
+    width = val_ref.shape[1]
+    per_slot = xc_ref.shape[0] // SLOTS
     parts = []
     for slot in range(SLOTS):
         scaled = [
@@ -107,14 +126,44 @@
                 preferred_element_type=jnp.float32,
             ).astype(jnp.bfloat16)
         )
-    spread = jnp.dot(
+    return jnp.dot(
         scatter_ref[...], jnp.concatenate(parts, axis=0), preferred_element_type=jnp.float32
     )
-    own = spread[:half]
-    if with_base:
-        own = own + jnp.dot(xo_ref[...], base_ref[...], preferred_element_type=jnp.float32)
-    da_ref[...] = own.astype(da_ref.dtype)
-    db_ref[...] = spread[half:].astype(db_ref.dtype)
+
+
+def more_body(xc_ref, scatter_ref, val_ref, sc_ref, *refs):
+    da_ref, *db_refs, _ = refs[-2 - QUARTERS:]
+    half = da_ref.shape[0]
+    spread = spread_products(xc_ref, scatter_ref, val_ref, sc_ref)
+    da_ref[...] = spread[:half].astype(da_ref.dtype)
+    put_quarters(db_refs, spread[half:])
+
+
+def more_delta_rows(gathered, scatter, values, scales, start, columns, gates):
+    width = values.shape[1]
+    half = scatter.shape[0] // 2
+    tile = min(512, columns)
+    skip = start // tile
+    out = pl.BlockSpec((half, tile), lambda i: (0, i))
+    shape = pltpu.VMEM((half, columns), jnp.bfloat16)
+    quarters = [pl.BlockSpec((half // QUARTERS, tile), lambda i: (0, i))] * QUARTERS
+    quarter_shapes = [pltpu.VMEM((half // QUARTERS, columns), jnp.bfloat16)] * QUARTERS
+    return pl.pallas_call(
+        more_body,
+        grid=(columns // tile,),
+        in_specs=[
+            pl.BlockSpec(gathered.shape, lambda i: (0, 0)),
+            pl.BlockSpec(scatter.shape, lambda i: (0, 0)),
+            pl.BlockSpec((SLOTS, width, tile), lambda i: (0, 0, i + skip)),
+            pl.BlockSpec((SLOTS, width // BLOCK, tile), lambda i: (0, 0, i + skip)),
+            *[pl.BlockSpec(memory_space=pltpu.HBM) for _ in gates],
+        ],
+        out_specs=(out, *quarters, pl.BlockSpec(memory_space=pltpu.HBM)),
+        out_shape=(shape, *quarter_shapes, FLAG),
+        cost_estimate=LIGHT,
+        compiler_params=pltpu.CompilerParams(vmem_limit_bytes=DELTA_VMEM),
+        name="more_delta_rows",
+    )(*in_vmem(gathered, scatter), *in_hbm(values, scales, *gates))
 
 
 def delta_rows(place, slots, meta, xa, xb, values, scales, tensor, base=None, start=0, columns=None, gates=()):
@@ -127,11 +176,11 @@
     smem = pl.BlockSpec(memory_space=pltpu.SMEM)
     whole = pl.BlockSpec(xa.shape, lambda i: (0, 0))
     in_specs = [
-        smem, smem, smem, whole, whole,
+        smem, smem, smem, whole, *[pl.BlockSpec(x.shape, lambda i: (0, 0)) for x in xb],
         pl.BlockSpec((SLOTS, width, tile), lambda i: (0, 0, i + skip)),
         pl.BlockSpec((SLOTS, width // BLOCK, tile), lambda i: (0, 0, i + skip)),
     ]
-    args = [place, *in_hbm(slots), meta, *in_vmem(xa, xb), *in_hbm(values, scales)]
+    args = [place, *in_hbm(slots), meta, *in_vmem(xa, *xb), *in_hbm(values, scales)]
     if base is not None:
         in_specs.append(pl.BlockSpec((width, tile), lambda i: (0, i + skip)))
         args += in_hbm(base)
@@ -139,19 +188,24 @@
     args += in_hbm(*gates)
     taken = SLOTS * 2 * steps * SEG_MOST
     out = pl.BlockSpec((steps * rows, tile), lambda i: (0, i))
-    shape = pltpu.HBM((steps * rows, columns), jnp.bfloat16)
-    scratch = [
-        pltpu.VMEM((taken, width), jnp.bfloat16),
-        pltpu.VMEM((2 * steps * rows, taken), jnp.bfloat16),
-    ]
+    shape = pltpu.VMEM((steps * rows, columns), jnp.bfloat16)
+    quarter = steps * rows // QUARTERS
+    quarters = [pl.BlockSpec((quarter, tile), lambda i: (0, i))] * QUARTERS
+    quarter_shapes = [pltpu.VMEM((quarter, columns), jnp.bfloat16)] * QUARTERS
+    gathered = (taken, width), (2 * steps * rows, taken)
     if base is not None:
-        scratch.append(pltpu.VMEM((steps * rows, width), jnp.bfloat16))
+        scratch = [pltpu.VMEM(dims, jnp.bfloat16) for dims in (*gathered, xa.shape)]
+        kept_specs, kept_shapes = (), ()
+    else:
+        scratch = []
+        kept_specs = tuple(pl.BlockSpec(dims, lambda i: (0, 0)) for dims in gathered)
+        kept_shapes = tuple(pltpu.VMEM(dims, jnp.bfloat16) for dims in gathered)
     return pl.pallas_call(
-        functools.partial(delta_body, base is not None, tensor, steps, rows),
+        functools.partial(delta_body, base is not None, tensor, steps, rows, len(xb)),
         grid=(columns // tile,),
         in_specs=in_specs,
-        out_specs=(out, out, pl.BlockSpec(memory_space=pltpu.HBM)),
-        out_shape=(shape, shape, FLAG),
+        out_specs=(out, *quarters, pl.BlockSpec(memory_space=pltpu.HBM), *kept_specs),
+        out_shape=(shape, *quarter_shapes, FLAG, *kept_shapes),
         scratch_shapes=scratch,
         cost_estimate=LIGHT,
         compiler_params=pltpu.CompilerParams(vmem_limit_bytes=DELTA_VMEM),
@@ -159,19 +213,27 @@
     )(*args)
 
 
-def head_rows(ref, r):
-    some = 2 * GROUP
-    return jnp.concatenate(
-        [ref[s, r, p * some:(p + 1) * some, :] for p in range(KVH // 2) for s in range(2)], axis=0
-    )
-
-
-def cache_body(start, len_ref, q_ref, kv_ref, *refs):
-    o_ref, lse_ref, _ = refs[-3:]
-    block = q_ref.shape[1]
+def cache_body(start, count, len_ref, q_ref, kv_ref, *refs):
+    o_ref, lse_ref, rows_ref, _, sorted_ref = refs[-5:]
+    block = rows_ref.shape[0]
     cached = kv_ref.shape[1]
     some = 4 * GROUP
     scale = 1.0 / math.sqrt(HD)
+
+    @pl.when(pl.program_id(0) == 0)
+    def _():
+        low = start // 16 * 16
+        high = min(-(-(start + count) // 16) * 16, q_ref.shape[1])
+        for at in range(2 * HEADS):
+            pair, step, head = at // some, at // (some // 2) % 2, at % (some // 2)
+            column = (pair * some // 2 + head) * HD
+            value = q_ref[step, low:high, column:column + HD].astype(jnp.float32)
+            value = value[start - low:start - low + count]
+            if count > 1:
+                sorted_ref[pl.ds(at, count, stride=2 * HEADS), :] = value
+            else:
+                sorted_ref[at:at + 1, :] = value
+
     position = lax.broadcasted_iota(jnp.int32, (2 * HEADS, cached), 1)
     wide = (some, 2 * HD)
     diagonal = (lax.broadcasted_iota(jnp.int32, wide, 0) // GROUP) % 2 == (
@@ -180,7 +242,9 @@
     first = (lax.broadcasted_iota(jnp.int32, (some, HD), 0) // GROUP) % 2 == 0
     scores = []
     for r in range(block):
-        rows = head_rows(q_ref, r)
+        at = pl.multiple_of((pl.program_id(0) * block + r) * 2 * HEADS, 2 * HEADS)
+        rows = sorted_ref[pl.ds(at, 2 * HEADS), :].astype(jnp.bfloat16)
+        rows_ref[r] = rows
         parts = []
         for p in range(KVH // 2):
             q = rows[p * some:(p + 1) * some]
@@ -216,40 +280,43 @@
         lse_ref[r] = lse[base:base + 2 * HEADS]
 
 
-def attend_cache(lengths, q, kv_cache, start, count, before, cost, gates):
-    rows = q.shape[1]
+def attend_cache(lengths, queries, kv_cache, start, count, before, cost, gates):
+    rows = queries.shape[1]
     cached, width = kv_cache.shape[1:]
-    block = min(8, count)
+    block = max(1, min(8, count // 2))
     skip = start // block
-    any_spec = pl.BlockSpec(memory_space=pltpu.HBM)
+    in_place = pl.BlockSpec(memory_space=pltpu.HBM)
     return pl.pallas_call(
-        functools.partial(cache_body, start),
+        functools.partial(cache_body, start, count),
         grid=(count // block,),
         in_specs=[
             pl.BlockSpec(memory_space=pltpu.SMEM),
-            pl.BlockSpec((2, block, HEADS, HD), lambda i: (0, i + skip, 0, 0)),
+            pl.BlockSpec(queries.shape, lambda i: (0, 0, 0)),
             pl.BlockSpec((block, cached, width), lambda i: (i + skip, 0, 0)),
-            *[any_spec for _ in (*before, *gates)],
+            *[in_place for _ in (*before, *gates)],
         ],
         out_specs=(
             pl.BlockSpec((block, 2 * HEADS, HD), lambda i: (i + skip, 0, 0)),
             pl.BlockSpec((block, 2 * HEADS, 1), lambda i: (i + skip, 0, 0)),
-            any_spec,
+            pl.BlockSpec((block, 2 * HEADS, HD), lambda i: (i + skip, 0, 0)),
+            in_place,
         ),
         out_shape=(
             pltpu.HBM((rows, 2 * HEADS, HD), jnp.float32),
             pltpu.HBM((rows, 2 * HEADS, 1), jnp.float32),
+            pltpu.HBM((rows, 2 * HEADS, HD), jnp.bfloat16),
             FLAG,
         ),
+        scratch_shapes=[pltpu.VMEM((count * 2 * HEADS, HD), jnp.float32)],
         input_output_aliases={3 + i: i for i in range(len(before))},
         cost_estimate=cost,
         compiler_params=pltpu.CompilerParams(vmem_limit_bytes=ATTEND_VMEM),
         name="attend_cache",
-    )(lengths, *in_hbm(q, kv_cache, *before, *gates))
-
-
-def weigh_body(q_ref, o_ref, lse_ref, keys_ref, prob_ref, out_ref):
-    block = q_ref.shape[1]
+    )(lengths, *in_hbm(queries, kv_cache, *before, *gates))
+
+
+def weigh_body(o_ref, lse_ref, rows_ref, keys_ref, prob_ref, out_ref):
+    block = o_ref.shape[0]
     shape = (2 * HEADS, 2 * KVH)
     row = lax.broadcasted_iota(jnp.int32, shape, 0)
     col = lax.broadcasted_iota(jnp.int32, shape, 1)
@@ -261,7 +328,7 @@
     for r in range(block):
         keys = jnp.concatenate([keys_ref[s, r] for s in range(2)], axis=0).astype(jnp.bfloat16)
         one = lax.dot_general(
-            head_rows(q_ref, r), keys, (((1,), (1,)), ((), ())), preferred_element_type=jnp.float32
+            rows_ref[r], keys, (((1,), (1,)), ((), ())), preferred_element_type=jnp.float32
         ) * scale
         scores.append(jnp.where(live, one, NEG))
     scores = jnp.concatenate(scores, axis=0)
@@ -276,17 +343,17 @@
         out_ref[r] = o_ref[r] * before[r * 2 * HEADS:(r + 1) * 2 * HEADS]
 
 
-def weigh_new(q, o, lse, keys):
-    rows = q.shape[1]
+def weigh_new(o, lse, queries, keys):
+    rows = o.shape[0]
     block = min(8, rows)
     half = pl.BlockSpec((block, 2 * HEADS, HD), lambda i: (i, 0, 0))
     return pl.pallas_call(
         weigh_body,
         grid=(rows // block,),
         in_specs=[
-            pl.BlockSpec((2, block, HEADS, HD), lambda i: (0, i, 0, 0)),
             half,
             pl.BlockSpec((block, 2 * HEADS, 1), lambda i: (i, 0, 0)),
+            half,
             pl.BlockSpec((2, block, KVH, HD), lambda i: (0, i, 0, 0)),
         ],
         out_specs=(pl.BlockSpec((block, 2 * HEADS, 2 * KVH), lambda i: (i, 0, 0)), half),
@@ -297,10 +364,13 @@
         cost_estimate=LIGHT,
         compiler_params=pltpu.CompilerParams(vmem_limit_bytes=ATTEND_VMEM),
         name="weigh_new",
-    )(*in_hbm(q, o, lse), keys)
-
-
-def add_body(prob_ref, o_ref, vals_ref, out_ref, sum_ref):
+    )(*in_hbm(o, lse, queries), keys)
+
+
+def add_body(prob_ref, o_ref, keys_ref, flat_ref, vals_ref, out_ref, new_ref, sum_ref):
+    half = keys_ref.shape[2]
+    new_ref[:, :, :half] = keys_ref[...]
+    new_ref[:, :, half:] = flat_ref[...]
     block = o_ref.shape[0]
     for r in range(block):
         vals = jnp.concatenate([vals_ref[s, r] for s in range(2)], axis=0).astype(jnp.bfloat16)
@@ -316,7 +386,7 @@
         ].astype(jnp.bfloat16)
 
 
-def add_new(probs, o, vals):
+def add_new(probs, o, keys, flat, vals):
     rows = o.shape[0]
     block = min(16, rows)
     return pl.pallas_call(
@@ -325,29 +395,37 @@
         in_specs=[
             pl.BlockSpec((block, 2 * HEADS, 2 * KVH), lambda i: (i, 0, 0)),
             pl.BlockSpec((block, 2 * HEADS, HD), lambda i: (i, 0, 0)),
+            pl.BlockSpec((2, block, KEYS), lambda i: (0, i, 0)),
+            pl.BlockSpec((2, block, KEYS), lambda i: (0, i, 0)),
             pl.BlockSpec((2, block, KVH, HD), lambda i: (0, i, 0, 0)),
         ],
-        out_specs=pl.BlockSpec((2, block, HEADS * HD), lambda i: (0, i, 0)),
-        out_shape=jax.ShapeDtypeStruct((2, rows, HEADS * HD), jnp.bfloat16),
+        out_specs=(
+            pl.BlockSpec((2, block, HEADS * HD), lambda i: (0, i, 0)),
+            pl.BlockSpec((2, block, 2 * KEYS), lambda i: (0, i, 0)),
+        ),
+        out_shape=(
+            jax.ShapeDtypeStruct((2, rows, HEADS * HD), jnp.bfloat16),
+            jax.ShapeDtypeStruct((2, rows, 2 * KEYS), jnp.bfloat16),
+        ),
         scratch_shapes=[pltpu.VMEM((block * 2 * HEADS, HD), jnp.float32)],
         cost_estimate=LIGHT,
         compiler_params=pltpu.CompilerParams(vmem_limit_bytes=ATTEND_VMEM),
         name="add_new",
-    )(*in_vmem(probs, o), vals)
+    )(*in_vmem(probs, o), keys, flat, vals)
 
 
 def marker_body(*refs):
     del refs
 
 
-def marker(flag):
+def marker(flag, cost):
     any_spec = pl.BlockSpec(memory_space=pltpu.HBM)
     return pl.pallas_call(
         marker_body,
         in_specs=[any_spec],
         out_specs=any_spec,
         out_shape=FLAG,
-        cost_estimate=COVER,
+        cost_estimate=cost,
         compiler_params=pltpu.CompilerParams(vmem_limit_bytes=1 << 20),
         name="marker",
     )(*in_hbm(flag))
@@ -396,7 +474,7 @@
     half = columns // 2
     masks = [1 << i for i in range(tensor.bit_length() - 1)]
     flat = hidden.reshape(2 * rows, hidden.shape[2])
-    piece = shard_rows // 2
+    piece = shard_rows // 4
     masks_far = list(range(2, replicas, 2))
 
     place = jnp.stack([lax.axis_index("replica") * SLOTS, lax.axis_index("tensor")]).astype(jnp.int32)
@@ -406,44 +484,55 @@
     meta = jnp.concatenate([meta, swap(meta, 1)], axis=0)
     far_meta = [swap(meta, mask) for mask in masks_far]
 
-    def cached(at, before, flag):
-        return attend_cache(cache_length, q, kv_cache, at * piece, piece, before, LIGHT, [flag])
-
-    own, other, flag = delta_rows(
-        place, tenant_slot, meta, flat, sibling, delta_values, delta_scales, tensor, base_weight
+    def cached(at, count, before, cost, flag):
+        return attend_cache(
+            cache_length, queries, kv_cache, at * piece, count * piece, before, cost, [flag]
+        )
+
+    own, *other, flag = delta_rows(
+        place, tenant_slot, meta, flat, [sibling], delta_values, delta_scales, tensor, base_weight
     )
-    back = swap(other, 1)
-    queries, flag = tie(queries, flag)
-    q, flag = tie(queries.reshape(2, shard_rows, HEADS, HD), flag)
-    flag = marker(flag)
+    back = [swap(part, 1) for part in other]
+    flag = marker(flag, COVER)
     back, flag = tie(back, flag)
-    sent, kept = halves([own, back])
-    sent, far, flag = tie(sent, far, flag)
-    theirs_in = [swap(rows_in, 1) for rows_in in far]
+    sent, kept = halves([own, jnp.concatenate(back, axis=0)])
+    sent, flag = tie(sent, flag)
     near = [kept, cross(sent, tensor, masks[0])]
+    *done, flag = cached(0, 1, (), LIGHT, flag)
+    far, far_meta, flag = tie(far, far_meta, flag)
+    quarter = rows // 2
+    theirs_in = [
+        [swap(rows_in[at:at + quarter], 1) for at in range(0, 2 * rows, quarter)] for rows_in in far
+    ]
 
     flying = []
     for mask, pair, far_rows, far_sibling in zip(masks_far, far_meta, far, theirs_in):
         for start in (0, half):
-            mine, theirs, flag = delta_rows(
-                place, tenant_slot, pair, far_rows, far_sibling, delta_values, delta_scales,
-                tensor, None, start, half, [flag],
-            )
-            back = swap(theirs, 1)
+            if start == 0:
+                mine, *theirs, flag, gathered, spread = delta_rows(
+                    place, tenant_slot, pair, far_rows, far_sibling, delta_values, delta_scales,
+                    tensor, None, start, half, [flag],
+                )
+            else:
+                mine, *theirs, flag = more_delta_rows(
+                    gathered, spread, delta_values, delta_scales, start, half, [flag]
+                )
+            back = [swap(part, 1) for part in theirs]
             if flying:
                 flying[-1], flag = tie(flying[-1], flag)
                 flying[-1] = swap(sum_of(flying[-1]), flying_mask)
+                flag = marker(flag, COVER)
             else:
                 near, flag = tie(near, flag)
                 near = sum_of(near)
-            flag = marker(flag)
+                flag = marker(flag, LIGHT)
             back, flag = tie(back, flag)
-            sent, kept = halves([mine, back])
+            sent, kept = halves([mine, jnp.concatenate(back, axis=0)])
             sent, flag = tie(sent, flag)
             flying.append([kept, cross(sent, tensor, masks[0])])
             flying_mask = mask
 
-    *done, flag = cached(0, (), flag)
+    *done, flag = cached(1, 2, done, LIGHT, flag)
     flying, flag = tie(flying, flag)
     last = sum_of(flying[-1])
     values = [[near[:, start:start + half], *flying[at::2]] for at, start in enumerate((0, half))]
@@ -451,24 +540,25 @@
     last, sent, flag = tie(last, sent, flag)
     values[1][-1] = swap(last, flying_mask)
     values[0] = [kept, cross(sent, tensor, masks[1])]
-    *done, flag = cached(1, done, flag)
-    values, done = tie(values, done)
-    finals = []
-    for at, value in enumerate(values):
-        for mask in masks[2 - at:]:
-            sent, kept = halves(value)
-            value = [kept, cross(sent, tensor, mask)]
-        finals.append(value)
+    *done, flag = cached(3, 1, done, LIGHT, flag)
+    values[1], done = tie(values[1], done)
+    for mask in masks[1:]:
+        sent, kept = halves(values[1])
+        values[1] = [kept, cross(sent, tensor, mask)]
+    values[0], sent = tie(values[0], sent)
+    for mask in masks[2:]:
+        sent, kept = halves(values[0])
+        values[0] = [kept, cross(sent, tensor, mask)]
 
     def by_head(value):
         return value.astype(jnp.float32).reshape(2, shard_rows, KVH, HD)
 
-    keys = sum_of(finals[0]).reshape(2, shard_rows, half)
-    probs, weighed = weigh_new(q, *done, by_head(keys))
-    last, probs = tie(finals[1], probs)
+    keys = sum_of(values[0]).reshape(2, shard_rows, half)
+    probs, weighed = weigh_new(*done, by_head(keys))
+    last, probs = tie(values[1], probs)
     vals = sum_of(last).reshape(2, shard_rows, half)
-    attention = add_new(probs, weighed, by_head(vals))
-    return (jnp.concatenate([keys, vals], axis=2), attention)
+    attention, new_kv = add_new(probs, weighed, keys, vals, by_head(vals))
+    return (new_kv, attention)
 
 
 def solution(mesh):

time: 84.8 us -> 78.4 us (0.925)
  waiting for transfers between devices: 14.8 us -> 6.05 us
  starting transfers between devices: 16.5 us -> 18.1 us
  Pallas kernels: 46.3 us -> 47.6 us
  local copies, waits for them, and re-layouts: 2.67 us -> 1.58 us
    pallas_call x3 -> x5, Pallas kernels: 17.3 us -> 26.4 us  [the longest x3 15.8 us: attend_cache(): pl.pallas_call(functools.partial(cache_body, start, count), grid=(count /...]
    pallas_call x3 -> x2, Pallas kernels: 26.3 us -> 18.4 us  [delta_rows(): pl.pallas_call(functools.partial(delta_body, base is not None, tensor, st...]
    ppermute x10 -> x22, waiting for transfers between devices: 9.66 us -> 3.86 us  [swap(): lax.ppermute(value, 'replica', [(i, i ^ mask) for i in range(replicas)])]
    ppermute x5, waiting for transfers between devices: 5.12 us -> 2.2 us  [cross(): return lax.ppermute(value, 'tensor', [(i, i ^ mask) for i in range(tensor)])]
    ppermute x10 -> x22, starting transfers between devices: 8.23 us -> 10.6 us  [swap(): lax.ppermute(value, 'replica', [(i, i ^ mask) for i in range(replicas)])]
    unnamed x19 -> x12, local copies, waits for them, and re-layouts: 2.66 us -> 1.5 us
  transfers between devices with their start and end apart: 15 -> 27, of which waited for: 10 -> 13; matrix products, arithmetic and copies ran while one was open for 4% -> 5% of each run, Pallas kernels for 52% -> 57%
where the time goes in v4:
time: 78.4 us; the launch traced here: 78.1 us
  Pallas kernels  47.6 us (61%)
  starting transfers between devices  18.1 us (23%)
  waiting for transfers between devices  6.05 us (8%)
  other arithmetic  3.94 us (5%)
  local copies, waits for them, and re-layouts  1.58 us (2%)
  between operations  0.85 us (1%)
    pallas_call x2, Pallas kernels, delta_rows(): pl.pallas_call(functools.partial(delta_body, base is not None, tensor, st...  18.4 us
    pallas_call x3, Pallas kernels, attend_cache(): pl.pallas_call(functools.partial(cache_body, start, count), grid=(count /...  15.8 us
    ppermute x22, starting transfers between devices, swap(): lax.ppermute(value, 'replica', [(i, i ^ mask) for i in range(replicas)])  10.6 us
    ppermute x5, starting transfers between devices, cross(): return lax.ppermute(value, 'tensor', [(i, i ^ mask) for i in range(tensor)])  7.55 us
    pallas_call x1, Pallas kernels, weigh_new(): pl.pallas_call(weigh_body, grid=(rows // block,), in_specs=[half, pl.Bloc...  5.73 us
    pallas_call x1, Pallas kernels, more_delta_rows(): pl.pallas_call(more_body, grid=(columns // tile,), in_specs=[pl.BlockSpec...  4.8 us
    ppermute x22, waiting for transfers between devices, swap(): lax.ppermute(value, 'replica', [(i, i ^ mask) for i in range(replicas)])  3.86 us
    pallas_call x1, Pallas kernels, add_new(): pl.pallas_call(add_body, grid=(rows // block,), in_specs=[pl.BlockSpec((b...  2.81 us
  transfers between devices with their start and end apart: 27, of which 13 were waited for; matrix products, arithmetic and copies ran while one was open for 5% of the time, Pallas kernels for 57%

profile of v4, /device:TPU:0, one launch (start us, length us, event | category | flops | bytes accessed | tf_op | source)
XLA Modules:
  0.0 78.1 jit_solution(3271153869318100028)
XLA Ops:
  0.6 0.5 collective-permute-start.1
  1.1 2.6 %collective-permute-start.7 = (bf16[256,2048]{1,0:T(8,128)(2,1)}, bf16[256,2048]{1,0:T(8,128)(2,1)S(1)}, u32[]{:S(2)}, u32[]{:S(2)}) collective-permute-start(bf16[256,2048]{1,0:T(8,128)(2,1)} %bitcast.15), channel_id=1, source_target_pairs={{0,2},{1,3},{2,0},{3,1},{4,6},{5,7},{6,4},{7,5},{8,10},{9,11},{10,... | collective-permute-start | bytes 3145736 | tf_op jit(solution)/shard_map/ppermute | solution.py:469
  3.7 0.7 pad_add_fusion.2
  4.6 0.7 pad_add_fusion.1.refs_0_
  5.6 1.3 %pad_add_fusion.refs_2_ = s32[2,8]{1,0:T(2,128)} fusion(s32[1,8]{1,0:T(1,128)S(1)} %collective-permute-done, s32[1,4]{1,0:T(1,128)} %param.16, s32[1,4]{1,0:T(1,128)} %param.15), kind=kLoop, calls=%fused_computation.17 | loop fusion | flops 32 | bytes 128 | tf_op jit(solution)/shard_map/concatenate | solution.py:484
  6.9 1.2 %copy-done = bf16[2,128,2048]{2,1,0:T(8,128)(2,1)S(1)} copy-done((bf16[2,128,2048]{2,1,0:T(8,128)(2,1)S(1)}, bf16[2,128,2048]{2,1,0:T(8,128)(2,1)}, u32[]{:S(2)}) %copy-start) | copy-done | bytes 1048600
  8.1 12.7 %delta_rows.2 = (bf16[256,2048]{1,0:T(8,128)(2,1)S(1)}, bf16[64,2048]{1,0:T(8,128)(2,1)S(1)}, bf16[64,2048]{1,0:T(8,128)(2,1)S(1)}, bf16[64,2048]{1,0:T(8,128)(2...) custom-call(s32[2]{0:T(128)} %pad_add_fusion.1.refs_0_, s32[8]{0:T(128)} %refs_1_.3, ...), custom_call_target="tpu_custom_call" | custom-call | flops 1 | bytes 1 | tf_op jit(solution)/shard_map/delta_rows/pallas_call | solution.py:203
  22.6 0.7 collective-permute-start.8
  23.9 1.6 %collective-permute-start.6 = (bf16[128,2048]{1,0:T(8,128)(2,1)S(1)}, bf16[128,2048]{1,0:T(8,128)(2,1)S(1)}, u32[]{:S(2)}, u32[]{:S(2)}) collective-permute-start(bf16[128,2048]{1,0:T(8,128)(2,1)S(1)} %get-tuple-element.95), channel_id=1, source_target_pairs={{0,4},{4,0},{8,12},{12,8},{1,5},{5,1},{9,13},{13,9},{2,6},{6,2},{1... | collective-permute-start | bytes 1572872 | tf_op jit(solution)/shard_map/ppermute | solution.py:451
  25.6 4.5 %attend_cache.3 = (f32[32,128,128]{2,1,0:T(8,128)}, f32[32,128,1]{2,1,0:T(8,128)}, bf16[32,128,128]{2,1,0:T(8,128)(2,1)}, f32[8,128]{1,0:T(8,128)}) custom-call(s32[32]{0:T(128)S(1)} %copy-done.1, bf16[2,32,8192]{2,1,0:T(8,128)(2,1)} %q_ref.5, bf16[32,128,2048]{2,1,0:T(8,128)(2,1)} %kv_ref.5, f32[8,128]{1,0:T(8,128)} %marker.3.refs_0_), custom_call_target="tpu_custom_call" | custom-call | flops 1 | bytes 1 | tf_op jit(solution)/shard_map/attend_cache/pallas_call | solution.py:289
  31.3 0.5 collective-permute-done.12.refs_7_
  32.9 5.7 %delta_rows.3 = (bf16[256,1024]{1,0:T(8,128)(2,1)S(1)}, bf16[64,1024]{1,0:T(8,128)(2,1)S(1)}, bf16[64,1024]{1,0:T(8,128)(2,1)S(1)}, bf16[64,1024]{1,0:T(8,128)(2...) custom-call(s32[2]{0:T(128)} %pad_add_fusion.1.refs_0_, ...), custom_call_target="tpu_custom_call" | custom-call | flops 1 | bytes 1 | tf_op jit(solution)/shard_map/delta_rows/pallas_call | solution.py:203
  40.9 0.5 collective-permute-start.17
  41.4 4.8 %more_delta_rows.1 = (bf16[256,1024]{1,0:T(8,128)(2,1)S(1)}, bf16[64,1024]{1,0:T(8,128)(2,1)S(1)}, bf16[64,1024]{1,0:T(8,128)(2,1)S(1)}, bf16[64,1024]{1,0:T(8,1...) custom-call(bf16[320,2048]{1,0:T(8,128)(2,1)S(1)} %get-tuple-element.116.xc_ref, ...), custom_call_target="tpu_custom_call" | custom-call | flops 1 | bytes 1 | tf_op jit(solution)/shard_map/more_delta_rows/pallas_call | solution.py:151
  47.3 2.2 %collective-permute-done.17 = bf16[128,1024]{1,0:T(8,128)(2,1)S(1)} collective-permute-done((bf16[128,1024]{1,0:T(8,128)(2,1)S(1)}, bf16[128,1024]{1,0:T(8,128)(2,1)S(1)}, u32[]{:S(2)}, u32[]{:S(2)}) %collective-permute-start.17) | collective-permute-done | bytes 262176 | tf_op jit(solution)/shard_map/ppermute | solution.py:451
  49.7 0.5 collective-permute-start.23
  50.3 1.1 %collective-permute-start.18 = (bf16[128,1024]{1,0:T(8,128)(2,1)S(1)}, bf16[128,1024]{1,0:T(8,128)(2,1)S(1)}, u32[]{:S(2)}, u32[]{:S(2)}) collective-permute-start(bf16[128,1024]{1,0:T(8,128)(2,1)S(1)} %add_convert_fusion.6), channel_id=1, source_target_pairs={{0,2},{1,3},{2,0},{3,1},{4,6},{5,7},{6,4},{7,5},{8,10},{9,11},{10,... | collective-permute-start | bytes 786440 | tf_op jit(solution)/shard_map/ppermute | solution.py:469
  51.6 6.9 %attend_cache.4 = (f32[32,128,128]{2,1,0:T(8,128)}, f32[32,128,1]{2,1,0:T(8,128)}, bf16[32,128,128]{2,1,0:T(8,128)(2,1)}, f32[8,128]{1,0:T(8,128)}) custom-call(s32[32]{0:T(128)S(1)} %copy-done.1, bf16[2,32,8192]{2,1,0:T(8,128)(2,1)} %q_ref.5, bf16[32,128,2048]{2,1,0:T(8,128)(2,1)} %kv_ref.5, ...), custom_call_target="tpu_custom_call", output_to_operand_aliasing={{0}: (3, {}), {1}: (4, {}), {2}: (5, {})} | custom-call | flops 1 | bytes 1 | tf_op jit(solution)/shard_map/attend_cache/pallas_call | solution.py:289
  58.7 1.1 %collective-permute-start.24 = (bf16[128,1024]{1,0:T(8,128)(2,1)S(1)}, bf16[128,1024]{1,0:T(8,128)(2,1)S(1)}, u32[]{:S(2)}, u32[]{:S(2)}) collective-permute-start(bf16[128,1024]{1,0:T(8,128)(2,1)S(1)} %add_convert_fusion.3), channel_id=1, source_target_pairs={{0,2},{1,3},{2,0},{3,1},{4,6},{5,7},{6,4},{7,5},{8,10},{9,11},{10,... | collective-permute-start | bytes 786440 | tf_op jit(solution)/shard_map/ppermute | solution.py:469
  59.9 2.6 %collective-permute-start.26 = (bf16[64,1024]{1,0:T(8,128)(2,1)S(1)}, bf16[64,1024]{1,0:T(8,128)(2,1)S(1)}, u32[]{:S(2)}, u32[]{:S(2)}) collective-permute-start(bf16[64,1024]{1,0:T(8,128)(2,1)S(1)} %get-tuple-element.156), channel_id=1, source_target_pairs={{0,8},{4,12},{8,0},{12,4},{1,9},{5,13},{9,1},{13,5},{2,10},{6,14},... | collective-permute-start | bytes 393224 | tf_op jit(solution)/shard_map/ppermute | solution.py:451
  62.5 4.5 %attend_cache.5 = (f32[32,128,128]{2,1,0:T(8,128)}, f32[32,128,1]{2,1,0:T(8,128)}, bf16[32,128,128]{2,1,0:T(8,128)(2,1)}, f32[8,128]{1,0:T(8,128)}) custom-call(s32[32]{0:T(128)S(1)} %copy-done.1, bf16[2,32,8192]{2,1,0:T(8,128)(2,1)} %q_ref.5, bf16[32,128,2048]{2,1,0:T(8,128)(2,1)} %kv_ref.5, ...), custom_call_target="tpu_custom_call", output_to_operand_aliasing={{0}: (3, {}), {1}: (4, {}), {2}: (5, {})} | custom-call | flops 1 | bytes 1 | tf_op jit(solution)/shard_map/attend_cache/pallas_call | solution.py:289
  67.1 2.3 %collective-permute-start.25 = (bf16[64,1024]{1,0:T(8,128)(2,1)S(1)}, bf16[64,1024]{1,0:T(8,128)(2,1)S(1)}, u32[]{:S(2)}, u32[]{:S(2)}) collective-permute-start(bf16[64,1024]{1,0:T(8,128)(2,1)S(1)} %get-tuple-element.178), channel_id=1, source_target_pairs={{0,8},{4,12},{8,0},{12,4},{1,9},{5,13},{9,1},{13,5},{2,10},{6,14},... | collective-permute-start | bytes 393224 | tf_op jit(solution)/shard_map/ppermute | solution.py:451
  69.4 5.7 %weigh_new.1 = (bf16[32,128,16]{2,1,0:T(8,128)(2,1)S(1)}, f32[32,128,128]{2,1,0:T(8,128)S(1)}) custom-call(f32[32,128,128]{2,1,0:T(8,128)} %get-tuple-element.153.o_ref, f32[32,128,1]{2,1,0:T(8,128)} %get-tuple-element.154.lse_ref, bf16[32,128,128]{2,1,0:T(8,128)(2,1)} %get-tuple-element.155.rows_ref, f32[2,32,8,128]{3,2,1,0:T(8,128)S(1)} %bitcast.17), custom_call_target="tpu_custom_call" | custom-call | flops 1 | bytes 1 | tf_op jit(solution)/shard_map/weigh_new/pallas_call | solution.py:350
  75.3 2.8 %add_new.1 = (bf16[2,32,8192]{2,1,0:T(8,128)(2,1)}, bf16[2,32,2048]{2,1,0:T(8,128)(2,1)}) custom-call(bf16[32,128,16]{2,1,0:T(8,128)(2,1)S(1)} %get-tuple-element.160.prob_ref, f32[32,128,128]{2,1,0:T(8,128)S(1)} %get-tuple-element.161.o_ref, bf16[2,32,1024]{2,1,0:T(8,128)(2,1)S(1)} %bitcast.18, bf16[2,32,1024]{2,1,0:T(8,128)(2,1)S(1)} %bitcast.19, ...), custom_call_target="tpu_custom_call" | custom-call | flops 1 | bytes 1 | tf_op jit(solution)/shard_map/add_new/pallas_call | solution.py:392
  (69 shorter events, 9.4 us)
Async XLA Ops:
  0.6 6.3 %collective-permute-start.1 = (bf16[256,2048]{1,0:T(8,128)(2,1)}, bf16[256,2048]{1,0:T(8,128)(2,1)S(1)}, u32[]{:S(2)}, u32[]{:S(2)}) collective-permute-start(bf16[256,2048]{1,0:T(8,128)(2,1)} %bitcast.14), channel_id=1, source_target_pairs={{0,1},{1,0},{2,3},{3,2},{4,5},{5,4},{6,7},{7,6},{8,9},{9,8},{10,11... | collective-permute-start | bytes 3145736 | tf_op jit(solution)/shard_map/ppermute | solution.py:469
  1.1 28.9 %collective-permute-start.7 = (bf16[256,2048]{1,0:T(8,128)(2,1)}, bf16[256,2048]{1,0:T(8,128)(2,1)S(1)}, u32[]{:S(2)}, u32[]{:S(2)}) collective-permute-start(bf16[256,2048]{1,0:T(8,128)(2,1)} %bitcast.15), channel_id=1, source_target_pairs={{0,2},{1,3},{2,0},{3,1},{4,6},{5,7},{6,4},{7,5},{8,10},{9,11},{10,... | collective-permute-start | bytes 3145736 | tf_op jit(solution)/shard_map/ppermute | solution.py:469
  20.8 1.6 %collective-permute-start.2 = (bf16[64,2048]{1,0:T(8,128)(2,1)S(1)}, bf16[64,2048]{1,0:T(8,128)(2,1)S(1)}, u32[]{:S(2)}, u32[]{:S(2)}) collective-permute-start(bf16[64,2048]{1,0:T(8,128)(2,1)S(1)} %get-tuple-element.85), channel_id=1, source_target_pairs={{0,1},{1,0},{2,3},{3,2},{4,5},{5,4},{6,7},{7,6},{8,9},{9,8},{10,11... | collective-permute-start | bytes 786440 | tf_op jit(solution)/shard_map/ppermute | solution.py:469
  21.1 2.2 %collective-permute-start.3 = (bf16[64,2048]{1,0:T(8,128)(2,1)S(1)}, bf16[64,2048]{1,0:T(8,128)(2,1)S(1)}, u32[]{:S(2)}, u32[]{:S(2)}) collective-permute-start(bf16[64,2048]{1,0:T(8,128)(2,1)S(1)} %get-tuple-element.86), channel_id=1, source_target_pairs={{0,1},{1,0},{2,3},{3,2},{4,5},{5,4},{6,7},{7,6},{8,9},{9,8},{10,11... | collective-permute-start | bytes 786440 | tf_op jit(solution)/shard_map/ppermute | solution.py:469
  21.4 1.9 %collective-permute-start.4 = (bf16[64,2048]{1,0:T(8,128)(2,1)S(1)}, bf16[64,2048]{1,0:T(8,128)(2,1)S(1)}, u32[]{:S(2)}, u32[]{:S(2)}) collective-permute-start(bf16[64,2048]{1,0:T(8,128)(2,1)S(1)} %get-tuple-element.87), channel_id=1, source_target_pairs={{0,1},{1,0},{2,3},{3,2},{4,5},{5,4},{6,7},{7,6},{8,9},{9,8},{10,11... | collective-permute-start | bytes 786440 | tf_op jit(solution)/shard_map/ppermute | solution.py:469
  21.6 1.9 %collective-permute-start.5 = (bf16[64,2048]{1,0:T(8,128)(2,1)S(1)}, bf16[64,2048]{1,0:T(8,128)(2,1)S(1)}, u32[]{:S(2)}, u32[]{:S(2)}) collective-permute-start(bf16[64,2048]{1,0:T(8,128)(2,1)S(1)} %get-tuple-element.88), channel_id=1, source_target_pairs={{0,1},{1,0},{2,3},{3,2},{4,5},{5,4},{6,7},{7,6},{8,9},{9,8},{10,11... | collective-permute-start | bytes 786440 | tf_op jit(solution)/shard_map/ppermute | solution.py:469
  22.6 7.5 %collective-permute-start.8 = (s32[2,8]{1,0:T(2,128)S(1)}, s32[2,8]{1,0:T(2,128)S(1)}, u32[]{:S(2)}, u32[]{:S(2)}) collective-permute-start(s32[2,8]{1,0:T(2,128)S(1)} %copy-done.3), channel_id=1, source_target_pairs={{0,2},{1,3},{2,0},{3,1},{4,6},{5,7},{6,4},{7,5},{8,10},{9,11},{10,... | collective-permute-start | bytes 200 | tf_op jit(solution)/shard_map/ppermute | solution.py:469
  23.9 15.7 %collective-permute-start.6 = (bf16[128,2048]{1,0:T(8,128)(2,1)S(1)}, bf16[128,2048]{1,0:T(8,128)(2,1)S(1)}, u32[]{:S(2)}, u32[]{:S(2)}) collective-permute-start(bf16[128,2048]{1,0:T(8,128)(2,1)S(1)} %get-tuple-element.95), channel_id=1, source_target_pairs={{0,4},{4,0},{8,12},{12,8},{1,5},{5,1},{9,13},{13,9},{2,6},{6,2},{1... | collective-permute-start | bytes 1572872 | tf_op jit(solution)/shard_map/ppermute | solution.py:451
  30.2 1.6 %collective-permute-start.12 = (bf16[64,2048]{1,0:T(8,128)(2,1)S(1)}, bf16[64,2048]{1,0:T(8,128)(2,1)S(1)}, u32[]{:S(2)}, u32[]{:S(2)}) collective-permute-start(bf16[64,2048]{1,0:T(8,128)(2,1)S(1)} %get-tuple-element.170), channel_id=1, source_target_pairs={{0,1},{1,0},{2,3},{3,2},{4,5},{5,4},{6,7},{7,6},{8,9},{9,8},{10,11... | collective-permute-start | bytes 786440 | tf_op jit(solution)/shard_map/ppermute | solution.py:469
  30.2 1.9 %collective-permute-start.11 = (bf16[64,2048]{1,0:T(8,128)(2,1)S(1)}, bf16[64,2048]{1,0:T(8,128)(2,1)S(1)}, u32[]{:S(2)}, u32[]{:S(2)}) collective-permute-start(bf16[64,2048]{1,0:T(8,128)(2,1)S(1)} %get-tuple-element.171), channel_id=1, source_target_pairs={{0,1},{1,0},{2,3},{3,2},{4,5},{5,4},{6,7},{7,6},{8,9},{9,8},{10,11... | collective-permute-start | bytes 786440 | tf_op jit(solution)/shard_map/ppermute | solution.py:469
  30.7 1.8 %collective-permute-start.10 = (bf16[64,2048]{1,0:T(8,128)(2,1)S(1)}, bf16[64,2048]{1,0:T(8,128)(2,1)S(1)}, u32[]{:S(2)}, u32[]{:S(2)}) collective-permute-start(bf16[64,2048]{1,0:T(8,128)(2,1)S(1)} %get-tuple-element.172), channel_id=1, source_target_pairs={{0,1},{1,0},{2,3},{3,2},{4,5},{5,4},{6,7},{7,6},{8,9},{9,8},{10,11... | collective-permute-start | bytes 786440 | tf_op jit(solution)/shard_map/ppermute | solution.py:469
  30.8 2.1 %collective-permute-start.9 = (bf16[64,2048]{1,0:T(8,128)(2,1)S(1)}, bf16[64,2048]{1,0:T(8,128)(2,1)S(1)}, u32[]{:S(2)}, u32[]{:S(2)}) collective-permute-start(bf16[64,2048]{1,0:T(8,128)(2,1)S(1)} %get-tuple-element.173), channel_id=1, source_target_pairs={{0,1},{1,0},{2,3},{3,2},{4,5},{5,4},{6,7},{7,6},{8,9},{9,8},{10,11... | collective-permute-start | bytes 786440 | tf_op jit(solution)/shard_map/ppermute | solution.py:469
  38.6 1.4 %collective-permute-start.13 = (bf16[64,1024]{1,0:T(8,128)(2,1)S(1)}, bf16[64,1024]{1,0:T(8,128)(2,1)S(1)}, u32[]{:S(2)}, u32[]{:S(2)}) collective-permute-start(bf16[64,1024]{1,0:T(8,128)(2,1)S(1)} %get-tuple-element.105), channel_id=1, source_target_pairs={{0,1},{1,0},{2,3},{3,2},{4,5},{5,4},{6,7},{7,6},{8,9},{9,8},{10,11... | collective-permute-start | bytes 393224 | tf_op jit(solution)/shard_map/ppermute | solution.py:469
  39.3 1.4 %collective-permute-start.16 = (bf16[64,1024]{1,0:T(8,128)(2,1)S(1)}, bf16[64,1024]{1,0:T(8,128)(2,1)S(1)}, u32[]{:S(2)}, u32[]{:S(2)}) collective-permute-start(bf16[64,1024]{1,0:T(8,128)(2,1)S(1)} %get-tuple-element.108), channel_id=1, source_target_pairs={{0,1},{1,0},{2,3},{3,2},{4,5},{5,4},{6,7},{7,6},{8,9},{9,8},{10,11... | collective-permute-start | bytes 393224 | tf_op jit(solution)/shard_map/ppermute | solution.py:469
  40.9 8.6 %collective-permute-start.17 = (bf16[128,1024]{1,0:T(8,128)(2,1)S(1)}, bf16[128,1024]{1,0:T(8,128)(2,1)S(1)}, u32[]{:S(2)}, u32[]{:S(2)}) collective-permute-start(bf16[128,1024]{1,0:T(8,128)(2,1)S(1)} %get-tuple-element.115), channel_id=1, source_target_pairs={{0,4},{4,0},{8,12},{12,8},{1,5},{5,1},{9,13},{13,9},{2,6},{6,2},{1... | collective-permute-start | bytes 786440 | tf_op jit(solution)/shard_map/ppermute | solution.py:451
  46.2 3.3 %collective-permute-start.19 = (bf16[64,1024]{1,0:T(8,128)(2,1)S(1)}, bf16[64,1024]{1,0:T(8,128)(2,1)S(1)}, u32[]{:S(2)}, u32[]{:S(2)}) collective-permute-start(bf16[64,1024]{1,0:T(8,128)(2,1)S(1)} %get-tuple-element.123), channel_id=1, source_target_pairs={{0,1},{1,0},{2,3},{3,2},{4,5},{5,4},{6,7},{7,6},{8,9},{9,8},{10,11... | collective-permute-start | bytes 393224 | tf_op jit(solution)/shard_map/ppermute | solution.py:469
  46.3 3.2 %collective-permute-start.20 = (bf16[64,1024]{1,0:T(8,128)(2,1)S(1)}, bf16[64,1024]{1,0:T(8,128)(2,1)S(1)}, u32[]{:S(2)}, u32[]{:S(2)}) collective-permute-start(bf16[64,1024]{1,0:T(8,128)(2,1)S(1)} %get-tuple-element.124), channel_id=1, source_target_pairs={{0,1},{1,0},{2,3},{3,2},{4,5},{5,4},{6,7},{7,6},{8,9},{9,8},{10,11... | collective-permute-start | bytes 393224 | tf_op jit(solution)/shard_map/ppermute | solution.py:469
  46.8 2.7 %collective-permute-start.21 = (bf16[64,1024]{1,0:T(8,128)(2,1)S(1)}, bf16[64,1024]{1,0:T(8,128)(2,1)S(1)}, u32[]{:S(2)}, u32[]{:S(2)}) collective-permute-start(bf16[64,1024]{1,0:T(8,128)(2,1)S(1)} %get-tuple-element.125), channel_id=1, source_target_pairs={{0,1},{1,0},{2,3},{3,2},{4,5},{5,4},{6,7},{7,6},{8,9},{9,8},{10,11... | collective-permute-start | bytes 393224 | tf_op jit(solution)/shard_map/ppermute | solution.py:469
  46.9 2.6 %collective-permute-start.22 = (bf16[64,1024]{1,0:T(8,128)(2,1)S(1)}, bf16[64,1024]{1,0:T(8,128)(2,1)S(1)}, u32[]{:S(2)}, u32[]{:S(2)}) collective-permute-start(bf16[64,1024]{1,0:T(8,128)(2,1)S(1)} %get-tuple-element.126), channel_id=1, source_target_pairs={{0,1},{1,0},{2,3},{3,2},{4,5},{5,4},{6,7},{7,6},{8,9},{9,8},{10,11... | collective-permute-start | bytes 393224 | tf_op jit(solution)/shard_map/ppermute | solution.py:469
  49.7 8.7 %collective-permute-start.23 = (bf16[128,1024]{1,0:T(8,128)(2,1)S(1)}, bf16[128,1024]{1,0:T(8,128)(2,1)S(1)}, u32[]{:S(2)}, u32[]{:S(2)}) collective-permute-start(bf16[128,1024]{1,0:T(8,128)(2,1)S(1)} %get-tuple-element.133), channel_id=1, source_target_pairs={{0,4},{4,0},{8,12},{12,8},{1,5},{5,1},{9,13},{13,9},{2,6},{6,2},{1... | collective-permute-start | bytes 786440 | tf_op jit(solution)/shard_map/ppermute | solution.py:451
  50.3 8.3 %collective-permute-start.18 = (bf16[128,1024]{1,0:T(8,128)(2,1)S(1)}, bf16[128,1024]{1,0:T(8,128)(2,1)S(1)}, u32[]{:S(2)}, u32[]{:S(2)}) collective-permute-start(bf16[128,1024]{1,0:T(8,128)(2,1)S(1)} %add_convert_fusion.6), channel_id=1, source_target_pairs={{0,2},{1,3},{2,0},{3,1},{4,6},{5,7},{6,4},{7,5},{8,10},{9,11},{10,... | collective-permute-start | bytes 786440 | tf_op jit(solution)/shard_map/ppermute | solution.py:469
  58.7 8.3 %collective-permute-start.24 = (bf16[128,1024]{1,0:T(8,128)(2,1)S(1)}, bf16[128,1024]{1,0:T(8,128)(2,1)S(1)}, u32[]{:S(2)}, u32[]{:S(2)}) collective-permute-start(bf16[128,1024]{1,0:T(8,128)(2,1)S(1)} %add_convert_fusion.3), channel_id=1, source_target_pairs={{0,2},{1,3},{2,0},{3,1},{4,6},{5,7},{6,4},{7,5},{8,10},{9,11},{10,... | collective-permute-start | bytes 786440 | tf_op jit(solution)/shard_map/ppermute | solution.py:469
  59.9 9.5 %collective-permute-start.26 = (bf16[64,1024]{1,0:T(8,128)(2,1)S(1)}, bf16[64,1024]{1,0:T(8,128)(2,1)S(1)}, u32[]{:S(2)}, u32[]{:S(2)}) collective-permute-start(bf16[64,1024]{1,0:T(8,128)(2,1)S(1)} %get-tuple-element.156), channel_id=1, source_target_pairs={{0,8},{4,12},{8,0},{12,4},{1,9},{5,13},{9,1},{13,5},{2,10},{6,14},... | collective-permute-start | bytes 393224 | tf_op jit(solution)/shard_map/ppermute | solution.py:451
  67.1 8.1 %collective-permute-start.25 = (bf16[64,1024]{1,0:T(8,128)(2,1)S(1)}, bf16[64,1024]{1,0:T(8,128)(2,1)S(1)}, u32[]{:S(2)}, u32[]{:S(2)}) collective-permute-start(bf16[64,1024]{1,0:T(8,128)(2,1)S(1)} %get-tuple-element.178), channel_id=1, source_target_pairs={{0,8},{4,12},{8,0},{12,4},{1,9},{5,13},{9,1},{13,5},{2,10},{6,14},... | collective-permute-start | bytes 393224 | tf_op jit(solution)/shard_map/ppermute | solution.py:451
  (9 other events, 25.1 us)

commit v5 on v4

v5 whole, which is shorter than its diff:
```python
import functools
import math

import jax
import jax.numpy as jnp
from jax import lax
from jax.experimental import pallas as pl
from jax.experimental.pallas import tpu as pltpu
from jax.sharding import PartitionSpec as P

HEADS = 64
KVH = 8
HD = 128
GROUP = HEADS // KVH
KEYS = KVH * HD
BLOCK = 128
SEG_MOST = 40
SLOTS = 2
QUARTERS = 4
NEG = -1e30
LIGHT = pl.CostEstimate(flops=1, bytes_accessed=1, transcendentals=0)
FLAG = pltpu.HBM((8, 128), jnp.float32)
SMEM = pl.BlockSpec(memory_space=pltpu.SMEM)
VMEM = pl.BlockSpec(memory_space=pltpu.VMEM)
HBM = pl.BlockSpec(memory_space=pltpu.HBM)
KERNEL_VMEM = 28 * 1024 * 1024
COVER = pl.CostEstimate(flops=1 << 34, bytes_accessed=1 << 26, transcendentals=0)


def in_hbm(*values):
    return [pltpu.with_memory_space_constraint(value, pltpu.HBM) for value in values]


def in_vmem(*values):
    return [pltpu.with_memory_space_constraint(value, pltpu.VMEM) for value in values]


def scatter_order(me, tensor, steps, rows, shape, axis):
    out = lax.broadcasted_iota(jnp.int32, shape, axis) % (steps * rows)
    shard = rows // tensor
    turn = tensor - 1 - out // (steps * shard)
    bits = tensor.bit_length() - 1
    apart = jnp.zeros(shape, jnp.int32)
    for bit in range(bits):
        apart = apart | (((turn >> (bits - 1 - bit)) & 1) << bit)
    step = (out // shard) % steps
    return step * rows + (apart ^ me) * shard + out % shard


def row_positions(meta_refs, slot_ref, first, steps, rows, source, index):
    step = index // rows
    row = index % rows
    per_slot = 2 * steps * SEG_MOST
    place = jnp.full(index.shape, -1, jnp.int32)
    for src, meta_ref in enumerate(meta_refs):
        begin = jnp.int32(0)
        for seg in range(meta_ref.shape[1] // 2):
            slot = slot_ref[meta_ref[0, seg]] - first
            length = meta_ref[0, meta_ref.shape[1] // 2 + seg]
            end = begin + length
            held = jnp.logical_and(slot >= 0, slot < SLOTS)
            offset = jnp.where(held, slot * per_slot + src * steps * SEG_MOST - begin, -(1 << 20))
            inside = (source == src) & (row >= begin) & (row < end)
            place = jnp.where(inside, offset + step * SEG_MOST + row, place)
            begin = end
    return place


def place_rows(tensor, steps, rows, slot_ref, meta_refs):
    half = steps * rows
    taken = SLOTS * 2 * steps * SEG_MOST
    first, me = lax.axis_index("replica") * SLOTS, lax.axis_index("tensor")
    flat = lax.broadcasted_iota(jnp.int32, (1, 2 * half), 1)
    order = scatter_order(me, tensor, steps, rows, (1, 2 * half), 1)
    chosen = []
    for index in (flat % half, order):
        along = row_positions(meta_refs, slot_ref, first, steps, rows, flat // half, index)
        chosen.append(lax.broadcasted_iota(jnp.int32, (taken, 2 * half), 0) == along)
    picks = chosen[0].astype(jnp.bfloat16)
    scatter = chosen[1].astype(jnp.float32).T.astype(jnp.bfloat16)
    return picks, scatter, order[:, :half]


def gather_rows(picks, xa, xb):
    half = xa.shape[0]
    got = jnp.dot(picks[:, :half], xa, preferred_element_type=jnp.float32)
    got += jnp.dot(picks[:, half:], xb, preferred_element_type=jnp.float32)
    return got.astype(jnp.bfloat16)


def spread_products(xc_ref, scatter_ref, weight_ref, cols):
    per_slot = xc_ref.shape[0] // SLOTS
    parts = [
        jnp.dot(
            xc_ref[slot * per_slot:(slot + 1) * per_slot, :], weight_ref[slot, :, cols],
            preferred_element_type=jnp.float32,
        ).astype(jnp.bfloat16)
        for slot in range(SLOTS)
    ]
    return jnp.dot(
        scatter_ref[...], jnp.concatenate(parts, axis=0), preferred_element_type=jnp.float32
    )


def first_body(tensor, steps, rows, *refs):
    slot_ref, meta_a, meta_b, xa_hbm, xb_ref, val_hbm, sc_hbm, base_hbm = refs[:8]
    da_ref, *db_refs = refs[8:9 + QUARTERS]
    weight_ref, _, xa_ref, sc_ref, base_ref, xc_ref, scatter_ref, xo_ref, sems = refs[9 + QUARTERS:]
    half = steps * rows
    width, columns = base_ref.shape
    tile = min(512, columns)
    tiles = [slice(at, at + tile) for at in range(0, columns, tile)]

    def copy(source, target, at):
        started = pltpu.make_async_copy(source, target, sems.at[at])
        started.start()
        return started

    rows_here = copy(xa_hbm, xa_ref, 0)
    scales = copy(sc_hbm, sc_ref, 1)
    coming = [
        (
            copy(val_hbm.at[:, :, cols], weight_ref.at[:, :, cols], 2 + 2 * at),
            copy(base_hbm.at[:, cols], base_ref.at[:, cols], 3 + 2 * at),
        )
        for at, cols in enumerate(tiles)
    ]
    picks, scatter, order = place_rows(tensor, steps, rows, slot_ref, (meta_a, meta_b))
    scatter_ref[...] = scatter
    turned = lax.broadcasted_iota(jnp.int32, (half, half), 0) == order
    turned = turned.astype(jnp.float32).T.astype(jnp.bfloat16)
    rows_here.wait()
    xc_ref[...] = gather_rows(picks, xa_ref[...], xb_ref[...])
    xo_ref[...] = jnp.dot(
        turned, xa_ref[...], preferred_element_type=jnp.float32
    ).astype(jnp.bfloat16)
    scales.wait()
    for cols, (values, base) in zip(tiles, coming):
        values.wait()
        for slot in range(SLOTS):
            for b in range(width // BLOCK):
                held = slice(b * BLOCK, (b + 1) * BLOCK)
                weight_ref[slot, held, cols] = (
                    weight_ref[slot, held, cols] * sc_ref[slot, b:b + 1, cols]
                )
        spread = spread_products(xc_ref, scatter_ref, weight_ref, cols)
        base.wait()
        own = spread[:half] + jnp.dot(
            xo_ref[...], base_ref[:, cols], preferred_element_type=jnp.float32
        )
        da_ref[:, cols] = own.astype(da_ref.dtype)
        put_quarters(db_refs, spread[half:], cols)


def far_body(tensor, steps, rows, start, chunks, *refs):
    slot_ref, meta_a, meta_b, xa_ref = refs[:4]
    xb_refs = refs[4:4 + chunks]
    weight_ref = refs[4 + chunks]
    da_ref, *db_refs, _, xc_ref, scatter_ref = refs[-4 - QUARTERS:]
    picks, scatter, _ = place_rows(tensor, steps, rows, slot_ref, (meta_a, meta_b))
    scatter_ref[...] = scatter
    xb = jnp.concatenate([ref[...] for ref in xb_refs], axis=0)
    xc_ref[...] = gather_rows(picks, xa_ref[...], xb)
    far_columns(start, xc_ref, scatter_ref, weight_ref, da_ref, db_refs)


def more_body(start, xc_ref, scatter_ref, weight_ref, *refs):
    da_ref, *db_refs, _ = refs[-2 - QUARTERS:]
    far_columns(start, xc_ref, scatter_ref, weight_ref, da_ref, db_refs)


def far_columns(start, xc_ref, scatter_ref, weight_ref, da_ref, db_refs):
    half, columns = da_ref.shape
    tile = min(512, columns)
    for at in range(0, columns, tile):
        spread = spread_products(
            xc_ref, scatter_ref, weight_ref, slice(start + at, start + at + tile)
        )
        cols = slice(at, at + tile)
        da_ref[:, cols] = spread[:half].astype(da_ref.dtype)
        put_quarters(db_refs, spread[half:], cols)


def put_quarters(refs, value, cols):
    rows = value.shape[0] // QUARTERS
    for at, ref in enumerate(refs):
        ref[:, cols] = value[at * rows:(at + 1) * rows].astype(ref.dtype)


def sums_shapes(half, columns):
    quarter = pltpu.VMEM((half // QUARTERS, columns), jnp.bfloat16)
    return [pltpu.VMEM((half, columns), jnp.bfloat16)] + [quarter] * QUARTERS


def first_delta(slots, metas, xa, xb, values, scales, base, tensor):
    steps = 2
    half, width = xa.shape
    rows = half // steps
    columns = base.shape[1]
    taken = SLOTS * 2 * steps * SEG_MOST
    outs = [*sums_shapes(half, columns), pltpu.VMEM(values.shape, jnp.bfloat16), FLAG]
    return pl.pallas_call(
        functools.partial(first_body, tensor, steps, rows),
        in_specs=[SMEM, SMEM, SMEM, HBM, VMEM, HBM, HBM, HBM],
        out_specs=[VMEM] * (len(outs) - 1) + [HBM],
        out_shape=outs,
        scratch_shapes=[
            pltpu.VMEM(xa.shape, jnp.bfloat16),
            pltpu.VMEM(scales.shape, jnp.bfloat16),
            pltpu.VMEM(base.shape, jnp.bfloat16),
            pltpu.VMEM((taken, width), jnp.bfloat16),
            pltpu.VMEM((2 * half, taken), jnp.bfloat16),
            pltpu.VMEM(xa.shape, jnp.bfloat16),
            pltpu.SemaphoreType.DMA((2 + 2 * max(1, columns // 512),)),
        ],
        cost_estimate=LIGHT,
        compiler_params=pltpu.CompilerParams(vmem_limit_bytes=22 << 20),
        name="first_delta",
    )(*in_hbm(slots), *metas, *in_hbm(xa), *in_vmem(xb), *in_hbm(values, scales, base))


def far_delta(slots, metas, xa, xb, weights, tensor, start, columns, gates):
    steps = 2
    half, width = xa.shape
    taken = SLOTS * 2 * steps * SEG_MOST
    kept = [pltpu.VMEM((taken, width), jnp.bfloat16), pltpu.VMEM((2 * half, taken), jnp.bfloat16)]
    outs = [*sums_shapes(half, columns), FLAG, *kept]
    return pl.pallas_call(
        functools.partial(far_body, tensor, steps, half // steps, start, len(xb)),
        in_specs=[SMEM, SMEM, SMEM] + [VMEM] * (2 + len(xb)) + [HBM] * len(gates),
        out_specs=[VMEM] * (1 + QUARTERS) + [HBM, VMEM, VMEM],
        out_shape=outs,
        cost_estimate=LIGHT,
        compiler_params=pltpu.CompilerParams(vmem_limit_bytes=12 << 20),
        name="far_delta",
    )(*in_hbm(slots), *metas, *in_vmem(xa, *xb, weights), *in_hbm(*gates))


def more_delta(gathered, scatter, weights, start, columns, gates):
    outs = [*sums_shapes(scatter.shape[0] // 2, columns), FLAG]
    return pl.pallas_call(
        functools.partial(more_body, start),
        in_specs=[VMEM] * 3 + [HBM] * len(gates),
        out_specs=[VMEM] * (1 + QUARTERS) + [HBM],
        out_shape=outs,
        cost_estimate=LIGHT,
        compiler_params=pltpu.CompilerParams(vmem_limit_bytes=8 << 20),
        name="more_delta",
    )(*in_vmem(gathered, scatter, weights), *in_hbm(*gates))


def add_quarters_body(value_ref, *refs):
    quarters, halves_out = refs[:QUARTERS], refs[QUARTERS:]
    rows = value_ref.shape[0] // QUARTERS
    for at, quarter in enumerate(quarters):
        target = halves_out[2 * at // QUARTERS]
        begin = at * rows % target.shape[0]
        target[begin:begin + rows, :] = (
            value_ref[at * rows:(at + 1) * rows, :].astype(jnp.float32)
            + quarter[...].astype(jnp.float32)
        ).astype(jnp.bfloat16)


def add_quarters(value, quarters):
    half = pltpu.VMEM((value.shape[0] // 2, value.shape[1]), jnp.bfloat16)
    return pl.pallas_call(
        add_quarters_body,
        in_specs=[VMEM] * (1 + QUARTERS),
        out_specs=[VMEM] * 2,
        out_shape=[half] * 2,
        cost_estimate=LIGHT,
        compiler_params=pltpu.CompilerParams(vmem_limit_bytes=4 << 20),
        name="add_quarters",
    )(*in_vmem(value, *quarters))


def cut_body(value_ref, *refs):
    rows = refs[0].shape[0]
    for at, ref in enumerate(refs):
        ref[...] = value_ref[at * rows:(at + 1) * rows, :]


def cut(value):
    quarter = pltpu.VMEM((value.shape[0] // QUARTERS, value.shape[1]), value.dtype)
    return pl.pallas_call(
        cut_body,
        in_specs=[VMEM],
        out_specs=[VMEM] * QUARTERS,
        out_shape=[quarter] * QUARTERS,
        cost_estimate=LIGHT,
        compiler_params=pltpu.CompilerParams(vmem_limit_bytes=4 << 20),
        name="cut",
    )(*in_vmem(value))


def cache_body(start, count, len_ref, q_ref, kv_ref, *refs):
    o_ref, lse_ref, turned_ref, _, sorted_ref = refs[-5:]
    block = o_ref.shape[0]
    cached = kv_ref.shape[1]
    some = 4 * GROUP
    scale = 1.0 / math.sqrt(HD)

    @pl.when(pl.program_id(0) == 0)
    def _():
        low = start // q_ref.shape[1] * q_ref.shape[1]
        for at in range(2 * HEADS):
            pair, step, head = at // some, at // (some // 2) % 2, at % (some // 2)
            column = (pair * some // 2 + head) * HD
            value = q_ref[step, :, column:column + HD].astype(jnp.float32)
            value = value[start - low:start - low + count]
            if count > 1:
                sorted_ref[pl.ds(at, count, stride=2 * HEADS), :] = value
            else:
                sorted_ref[at:at + 1, :] = value

    position = lax.broadcasted_iota(jnp.int32, (cached, 2 * HEADS), 0)
    column = lax.broadcasted_iota(jnp.int32, (HD, 2 * HEADS), 1)
    heads = column // some * 2 + column // GROUP % 2
    first = (lax.broadcasted_iota(jnp.int32, (some, HD), 0) // GROUP) % 2 == 0
    probs = []
    for r in range(block):
        at = pl.multiple_of((pl.program_id(0) * block + r) * 2 * HEADS, 2 * HEADS)
        turned = sorted_ref[pl.ds(at, 2 * HEADS), :].astype(jnp.bfloat16).T
        turned_ref[r] = turned
        wide = jnp.concatenate(
            [jnp.where(heads == k, turned, jnp.zeros_like(turned)) for k in range(KVH)], axis=0
        )
        scores = scale * jnp.dot(kv_ref[r, :, :KEYS], wide, preferred_element_type=jnp.float32)
        length = len_ref[start + pl.program_id(0) * block + r]
        scores = jnp.where(position < length, scores, NEG)
        top = jnp.max(scores, axis=0, keepdims=True)
        expo = jnp.exp(scores - top)
        total = jnp.sum(expo, axis=0, keepdims=True)
        lse_ref[r] = top + jnp.log(total)
        probs.append((expo * (1.0 / total)).astype(jnp.bfloat16).T)
    for r in range(block):
        parts = []
        for p in range(KVH // 2):
            out = jnp.dot(
                probs[r][p * some:(p + 1) * some],
                kv_ref[r, :, KEYS + p * 2 * HD:KEYS + (p + 1) * 2 * HD],
                preferred_element_type=jnp.float32,
            )
            parts.append(jnp.where(first, out[:, :HD], out[:, HD:]))
        o_ref[r] = jnp.concatenate(parts, axis=0)


def attend_cache(lengths, queries, kv_cache, start, count, before, cost, gates):
    rows = queries.shape[1]
    cached, width = kv_cache.shape[1:]
    block = max(1, min(8, count // 2))
    skip = start // block
    together = 16 if rows % 16 == 0 else rows
    in_place = pl.BlockSpec(memory_space=pltpu.HBM)
    return pl.pallas_call(
        functools.partial(cache_body, start, count),
        grid=(count // block,),
        in_specs=[
            pl.BlockSpec(memory_space=pltpu.SMEM),
            pl.BlockSpec((2, together, queries.shape[2]), lambda i: (0, start // together, 0)),
            pl.BlockSpec((block, cached, width), lambda i: (i + skip, 0, 0)),
            *[in_place for _ in (*before, *gates)],
        ],
        out_specs=(
            pl.BlockSpec((block, 2 * HEADS, HD), lambda i: (i + skip, 0, 0)),
            pl.BlockSpec((block, 1, 2 * HEADS), lambda i: (i + skip, 0, 0)),
            pl.BlockSpec((block, HD, 2 * HEADS), lambda i: (i + skip, 0, 0)),
            in_place,
        ),
        out_shape=(
            pltpu.VMEM((rows, 2 * HEADS, HD), jnp.float32),
            pltpu.VMEM((rows, 1, 2 * HEADS), jnp.float32),
            pltpu.VMEM((rows, HD, 2 * HEADS), jnp.bfloat16),
            FLAG,
        ),
        scratch_shapes=[pltpu.VMEM((count * 2 * HEADS, HD), jnp.float32)],
        input_output_aliases={3 + i: i for i in range(len(before))},
        cost_estimate=cost,
        compiler_params=pltpu.CompilerParams(vmem_limit_bytes=22 << 20),
        name="attend_cache",
    )(lengths, *in_hbm(queries, kv_cache), *in_vmem(*before), *in_hbm(*gates))


def weigh_body(o_ref, lse_ref, turned_ref, keys_ref, prob_ref, out_ref):
    rows = o_ref.shape[0]
    block = min(8, rows)
    pairs = 2 * KVH
    shape = (pairs, 2 * HEADS)
    row = lax.broadcasted_iota(jnp.int32, shape, 0)
    col = lax.broadcasted_iota(jnp.int32, shape, 1)
    head = col // (4 * GROUP) * 2 + (col // GROUP) % 2
    step = (col // (2 * GROUP)) % 2
    live = (head == row % KVH) & (row // KVH <= step)
    scale = 1.0 / math.sqrt(HD)

    def some_rows(at, carry):
        for inner in range(block):
            r = at * block + inner
            keys = jnp.concatenate([keys_ref[s, r] for s in range(2)], axis=0).astype(jnp.bfloat16)
            scores = scale * jnp.dot(keys, turned_ref[r], preferred_element_type=jnp.float32)
            scores = jnp.where(live, scores, NEG)
            lse = lse_ref[r]
            top = jnp.maximum(jnp.max(scores, axis=0, keepdims=True), lse)
            expo = jnp.exp(scores - top)
            before = jnp.exp(lse - top)
            inverse = 1.0 / (before + jnp.sum(expo, axis=0, keepdims=True))
            shares = jnp.broadcast_to(before * inverse, shape)
            both = jnp.concatenate([expo * inverse, shares], axis=0).T
            prob_ref[r] = both[:, :pairs].astype(jnp.bfloat16)
            out_ref[r] = o_ref[r] * both[:, pairs:pairs + 1]
        return carry

    lax.fori_loop(0, rows // block, some_rows, 0)


def weigh_new(o, lse, turned, keys):
    rows = o.shape[0]
    return pl.pallas_call(
        weigh_body,
        in_specs=[VMEM] * 4,
        out_specs=[VMEM] * 2,
        out_shape=(
            pltpu.VMEM((rows, 2 * HEADS, 2 * KVH), jnp.bfloat16),
            pltpu.VMEM(o.shape, jnp.float32),
        ),
        cost_estimate=LIGHT,
        compiler_params=pltpu.CompilerParams(vmem_limit_bytes=8 << 20),
        name="weigh_new",
    )(*in_vmem(o, lse, turned, keys))


def add_body(prob_ref, o_ref, keys_ref, flat_ref, vals_ref, out_hbm, new_hbm, out_ref, sum_ref, sems):
    half = keys_ref.shape[2]
    rows = o_ref.shape[0]
    block = min(16, rows)
    some = 2 * GROUP
    copies = [
        pltpu.make_async_copy(keys_ref, new_hbm.at[:, :, :half], sems.at[0]),
        pltpu.make_async_copy(flat_ref, new_hbm.at[:, :, half:], sems.at[1]),
    ]
    for copy in copies:
        copy.start()
    for begin in range(0, rows, block):
        for r in range(block):
            vals = jnp.concatenate([vals_ref[s, begin + r] for s in range(2)], axis=0)
            sum_ref[r * 2 * HEADS:(r + 1) * 2 * HEADS, :] = o_ref[begin + r] + jnp.dot(
                prob_ref[begin + r], vals.astype(jnp.bfloat16), preferred_element_type=jnp.float32
            )
        for at in range(2 * HEADS):
            pair, step, head = at // (2 * some), (at // some) % 2, at % some
            column = (pair * some + head) * HD
            out_ref[step, begin:begin + block, column:column + HD] = sum_ref[
                pl.ds(at, block, stride=2 * HEADS), :
            ].astype(jnp.bfloat16)
        copies.append(
            pltpu.make_async_copy(
                out_ref.at[:, begin:begin + block, :], out_hbm.at[:, begin:begin + block, :],
                sems.at[2 + begin // block],
            )
        )
        copies[-1].start()
    for copy in copies:
        copy.wait()


def add_new(probs, o, keys, flat, vals):
    rows = o.shape[0]
    block = min(16, rows)
    return pl.pallas_call(
        add_body,
        in_specs=[VMEM] * 5,
        out_specs=[HBM, HBM],
        out_shape=(
            jax.ShapeDtypeStruct((2, rows, HEADS * HD), jnp.bfloat16),
            jax.ShapeDtypeStruct((2, rows, 2 * KEYS), jnp.bfloat16),
        ),
        scratch_shapes=[
            pltpu.VMEM((2, rows, HEADS * HD), jnp.bfloat16),
            pltpu.VMEM((block * 2 * HEADS, HD), jnp.float32),
            pltpu.SemaphoreType.DMA((2 + rows // block,)),
        ],
        cost_estimate=LIGHT,
        compiler_params=pltpu.CompilerParams(vmem_limit_bytes=12 << 20),
        name="add_new",
    )(*in_vmem(probs, o, keys, flat, vals))


def marker_body(*refs):
    del refs


def marker(flag, cost):
    any_spec = pl.BlockSpec(memory_space=pltpu.HBM)
    return pl.pallas_call(
        marker_body,
        in_specs=[any_spec],
        out_specs=any_spec,
        out_shape=FLAG,
        cost_estimate=cost,
        compiler_params=pltpu.CompilerParams(vmem_limit_bytes=1 << 20),
        name="marker",
    )(*in_hbm(flag))


def tie(*values):
    return lax.optimization_barrier(values)


def halves(terms):
    half = terms[0].shape[0] // 2
    return [
        sum(term[begin:begin + half].astype(jnp.float32) for term in terms).astype(jnp.bfloat16)
        for begin in (0, half)
    ]


def sum_of(terms):
    return sum(term.astype(jnp.float32) for term in terms).astype(jnp.bfloat16)


def cross(value, tensor, mask):
    return lax.ppermute(value, "tensor", [(i, i ^ mask) for i in range(tensor)])


def local(
    replicas,
    tensor,
    hidden,
    base_weight,
    delta_values,
    delta_scales,
    tenant_slot,
    seg_tenant,
    seg_length,
    queries,
    kv_cache,
    cache_length,
):
    def swap(value, mask):
        return lax.ppermute(value, "replica", [(i, i ^ mask) for i in range(replicas)])

    rows = hidden.shape[1]
    columns = base_weight.shape[1]
    shard_rows = rows // tensor
    half = columns // 2
    masks = [1 << i for i in range(tensor.bit_length() - 1)]
    flat = hidden.reshape(2 * rows, hidden.shape[2])
    piece = shard_rows // 4
    masks_far = list(range(2, replicas, 2))

    far = [swap(flat, mask) for mask in masks_far]
    sibling = swap(flat, 1)
    meta = jnp.concatenate([seg_tenant, seg_length], axis=1)
    metas = [meta, *[swap(meta, mask) for mask in range(1, replicas)]]

    def cached(at, count, before, cost, flag):
        return attend_cache(
            cache_length, queries, kv_cache, at * piece, count * piece, before, cost, [flag]
        )

    own, *other, weights, flag = first_delta(
        tenant_slot, metas[:2], flat, sibling, delta_values, delta_scales, base_weight, tensor
    )
    back = [swap(part, 1) for part in other]
    flag = marker(flag, COVER)
    back, flag = tie(back, flag)
    sent, kept = add_quarters(own, back)
    sent, flag = tie(sent, flag)
    near = [kept, cross(sent, tensor, masks[0])]
    *done, flag = cached(0, 1, (), LIGHT, flag)
    far, far_metas, flag = tie(far, metas[2:], flag)
    theirs_in = [[swap(part, 1) for part in cut(rows_in)] for rows_in in far]

    flying = []
    for mask, far_rows, far_sibling in zip(masks_far, far, theirs_in):
        pair = far_metas[mask - 2:mask]
        for start in (0, half):
            if start == 0:
                mine, *theirs, flag, gathered, spread = far_delta(
                    tenant_slot, pair, far_rows, far_sibling, weights, tensor, start, half, [flag]
                )
            else:
                mine, *theirs, flag = more_delta(gathered, spread, weights, start, half, [flag])
            back = [swap(part, 1) for part in theirs]
            if flying:
                flying[-1], flag = tie(flying[-1], flag)
                flying[-1] = swap(sum_of(flying[-1]), flying_mask)
                flag = marker(flag, COVER)
            else:
                near, flag = tie(near, flag)
                near = sum_of(near)
                flag = marker(flag, LIGHT)
            back, flag = tie(back, flag)
            sent, kept = add_quarters(mine, back)
            sent, flag = tie(sent, flag)
            flying.append([kept, cross(sent, tensor, masks[0])])
            flying_mask = mask

    *done, flag = cached(2, 2, done, LIGHT, flag)
    flying, flag = tie(flying, flag)
    last = sum_of(flying[-1])
    values = [[near[:, start:start + half], *flying[at::2]] for at, start in enumerate((0, half))]
    sent, kept = halves(values[0])
    last, sent, flag = tie(last, sent, flag)
    values[1][-1] = swap(last, flying_mask)
    values[0] = [kept, cross(sent, tensor, masks[1])]
    *done, flag = cached(1, 1, done, LIGHT, flag)
    values[1], done = tie(values[1], done)
    for mask in masks[1:]:
        sent, kept = halves(values[1])
        values[1] = [kept, cross(sent, tensor, mask)]
    values[0], sent = tie(values[0], sent)
    for mask in masks[2:]:
        sent, kept = halves(values[0])
        values[0] = [kept, cross(sent, tensor, mask)]

    def by_head(value):
        return value.astype(jnp.float32).reshape(2, shard_rows, KVH, HD)

    keys = sum_of(values[0]).reshape(2, shard_rows, half)
    probs, weighed = weigh_new(*done, by_head(keys))
    last, probs = tie(values[1], probs)
    vals = sum_of(last).reshape(2, shard_rows, half)
    attention, new_kv = add_new(probs, weighed, keys, vals, by_head(vals))
    return (new_kv, attention)


def solution(mesh):
    placed = (
        P(None, ("groups", "replica"), "tensor"),
        P("tensor", None),
        P(("groups", "replica"), "tensor", None),
        P(("groups", "replica"), "tensor", None),
        P(),
        P(("groups", "replica"), None),
        P(("groups", "replica"), None),
        P(None, ("groups", "replica", "tensor"), None),
        P(("groups", "replica", "tensor"), None, None),
        P(("groups", "replica", "tensor")),
    )
    return jax.shard_map(
        functools.partial(local, mesh.shape["replica"], mesh.shape["tensor"]),
        mesh=mesh,
        in_specs=placed,
        out_specs=(
            P(None, ("groups", "replica", "tensor"), None),
            P(None, ("groups", "replica", "tensor"), None),
        ),
        check_vma=False,
    )
```

time: 78.4 us -> 73 us (0.931)
  Pallas kernels: 47.6 us -> 36.1 us
  waiting for transfers between devices: 6.05 us -> 12.4 us
  starting transfers between devices: 18.1 us -> 22.1 us
  other arithmetic: 3.94 us -> 1.22 us
  local copies, waits for them, and re-layouts: 1.58 us -> 0.11 us
    pallas_call x5 -> x9, Pallas kernels: 31.7 us -> 23.5 us  [the longest x1 11.9 us: first_delta(): pl.pallas_call(functools.partial(first_body, tensor, steps, rows), in_spe...]
    ppermute x5, waiting for transfers between devices: 2.2 us -> 6.21 us  [cross(): return lax.ppermute(value, 'tensor', [(i, i ^ mask) for i in range(tensor)])]
    pallas_call x3, Pallas kernels: 15.8 us -> 12.6 us  [attend_cache(): pl.pallas_call(functools.partial(cache_body, start, count), grid=(count /...]
    ppermute x22 -> x23, waiting for transfers between devices: 3.86 us -> 6.17 us  [swap(): lax.ppermute(value, 'replica', [(i, i ^ mask) for i in range(replicas)])]
    ppermute x5, starting transfers between devices: 7.55 us -> 9.79 us  [cross(): return lax.ppermute(value, 'tensor', [(i, i ^ mask) for i in range(tensor)])]
    ppermute x22 -> x23, starting transfers between devices: 10.6 us -> 12.3 us  [swap(): lax.ppermute(value, 'replica', [(i, i ^ mask) for i in range(replicas)])]
    unnamed x12 -> x6, local copies, waits for them, and re-layouts: 1.5 us -> 0.11 us
    concatenate x1 -> x0, other arithmetic: 1.31 us -> none  [local(): meta = jnp.concatenate([meta, swap(meta, 1)], axis=0)]
  transfers between devices with their start and end apart: 27 -> 28, of which waited for: 13 -> 18; matrix products, arithmetic and copies ran while one was open for 5% -> 2% of each run, Pallas kernels for 57% -> 46%
where the time goes in v5:
time: 73 us; the launch traced here: 72.8 us
  Pallas kernels  36.1 us (49%)
  starting transfers between devices  22.1 us (30%)
  waiting for transfers between devices  12.4 us (17%)
  other arithmetic  1.22 us (2%)
  between operations  0.99 us (1%)
    pallas_call x3, Pallas kernels, attend_cache(): pl.pallas_call(functools.partial(cache_body, start, count), grid=(count /...  12.6 us
    ppermute x23, starting transfers between devices, swap(): lax.ppermute(value, 'replica', [(i, i ^ mask) for i in range(replicas)])  12.3 us
    pallas_call x1, Pallas kernels, first_delta(): pl.pallas_call(functools.partial(first_body, tensor, steps, rows), in_spe...  11.9 us
    ppermute x5, starting transfers between devices, cross(): return lax.ppermute(value, 'tensor', [(i, i ^ mask) for i in range(tensor)])  9.79 us
    ppermute x5, waiting for transfers between devices, cross(): return lax.ppermute(value, 'tensor', [(i, i ^ mask) for i in range(tensor)])  6.21 us
    ppermute x23, waiting for transfers between devices, swap(): lax.ppermute(value, 'replica', [(i, i ^ mask) for i in range(replicas)])  6.17 us
    pallas_call x1, Pallas kernels, far_delta(): pl.pallas_call(functools.partial(far_body, tensor, steps, half // steps,...  3.68 us
    pallas_call x1, Pallas kernels, add_new(): pl.pallas_call(add_body, in_specs=[VMEM] * 5, out_specs=[HBM, HBM], out_s...  2.64 us
  transfers between devices with their start and end apart: 28, of which 18 were waited for; matrix products, arithmetic and copies ran while one was open for 2% of the time, Pallas kernels for 46%

profile of v5, /device:TPU:0, one launch (start us, length us, event | category | flops | bytes accessed | tf_op | source)
XLA Modules:
  0.0 72.8 jit_solution(9149914698413938096)
XLA Ops:
  0.6 0.5 collective-permute-start.1
  1.1 2.6 %collective-permute-start.7 = (bf16[256,2048]{1,0:T(8,128)(2,1)}, bf16[256,2048]{1,0:T(8,128)(2,1)S(1)}, u32[]{:S(2)}, u32[]{:S(2)}) collective-permute-start(bf16[256,2048]{1,0:T(8,128)(2,1)} %bitcast.16), channel_id=1, source_target_pairs={{0,2},{1,3},{2,0},{3,1},{4,6},{5,7},{6,4},{7,5},{8,10},{9,11},{10,... | collective-permute-start | bytes 3145736 | tf_op jit(solution)/shard_map/ppermute | solution.py:540
  3.7 0.7 %pad_add_fusion.refs_1_ = s32[1,8]{1,0:T(1,128)S(1)} fusion(s32[1,4]{1,0:T(1,128)} %param.16, s32[1,4]{1,0:T(1,128)} %param.15), kind=kLoop, calls=%fused_computation.11 | loop fusion | flops 8 | bytes 64 | tf_op jit(solution)/shard_map/concatenate | solution.py:553
  4.6 1.0 %collective-permute-done.refs_2_ = s32[1,8]{1,0:T(1,128)S(1)} collective-permute-done((s32[1,8]{1,0:T(1,128)S(1)}, s32[1,8]{1,0:T(1,128)S(1)}, u32[]{:S(2)}, u32[]{:S(2)}) %collective-permute-start) | collective-permute-done | bytes 64 | tf_op jit(solution)/shard_map/ppermute | solution.py:540
  5.6 11.9 %first_delta.1 = (bf16[256,2048]{1,0:T(8,128)(2,1)S(1)}, bf16[64,2048]{1,0:T(8,128)(2,1)S(1)}, bf16[64,2048]{1,0:T(8,128)(2,1)S(1)}, bf16[64,2048]{1,0:T(8,128)(...) custom-call(s32[8]{0:T(128)} %refs_0_.3, ...), custom_call_target="tpu_custom_call" | custom-call | flops 1 | bytes 1 | tf_op jit(solution)/shard_map/first_delta/pallas_call | solution.py:202
  18.5 0.5 collective-permute-done.2.refs_0_
  20.4 1.6 %collective-permute-start.6 = (bf16[128,2048]{1,0:T(8,128)(2,1)S(1)}, bf16[128,2048]{1,0:T(8,128)(2,1)S(1)}, u32[]{:S(2)}, u32[]{:S(2)}) collective-permute-start(bf16[128,2048]{1,0:T(8,128)(2,1)S(1)} %get-tuple-element.109), channel_id=1, source_target_pairs={{0,4},{4,0},{8,12},{12,8},{1,5},{5,1},{9,13},{13,9},{2,6},{6,2},{1... | collective-permute-start | bytes 1572872 | tf_op jit(solution)/shard_map/ppermute | solution.py:522
  22.4 1.2 %collective-permute-start.8 = (s32[1,8]{1,0:T(1,128)S(1)}, s32[1,8]{1,0:T(1,128)S(1)}, u32[]{:S(2)}, u32[]{:S(2)}) collective-permute-start(s32[1,8]{1,0:T(1,128)S(1)} %pad_add_fusion.refs_1_), channel_id=1, source_target_pairs={{0,2},{1,3},{2,0},{3,1},{4,6},{5,7},{6,4},{7,5},{8,10},{9,11},{10,... | collective-permute-start | bytes 104 | tf_op jit(solution)/shard_map/ppermute | solution.py:540
  23.6 3.5 %attend_cache.3 = (f32[32,128,128]{2,1,0:T(8,128)S(1)}, f32[32,1,128]{2,1,0:T(1,128)S(1)}, bf16[32,128,128]{2,1,0:T(8,128)(2,1)S(1)}, f32[8,128]{1,0:T(8,128)}) custom-call(s32[32]{0:T(128)S(1)} %copy-done, bf16[2,32,8192]{2,1,0:T(8,128)(2,1)} %q_ref.5, bf16[32,128,2048]{2,1,0:T(8,128)(2,1)} %kv_ref.5, f32[8,128]{1,0:T(8,128)} %marker.3.refs_0_), custom_call_target="tpu_custom_call" | custom-call | flops 1 | bytes 1 | tf_op jit(solution)/shard_map/attend_cache/pallas_call | solution.py:355
  28.9 0.5 collective-permute-done.10.refs_4_
  30.6 3.7 %far_delta.1 = (bf16[256,1024]{1,0:T(8,128)(2,1)S(1)}, bf16[64,1024]{1,0:T(8,128)(2,1)S(1)}, bf16[64,1024]{1,0:T(8,128)(2,1)S(1)}, bf16[64,1024]{1,0:T(8,128)(2,...) custom-call(s32[8]{0:T(128)} %refs_0_.3, ...), custom_call_target="tpu_custom_call" | custom-call | flops 1 | bytes 1 | tf_op jit(solution)/shard_map/far_delta/pallas_call | solution.py:228
  36.5 1.9 %collective-permute-start.18 = (bf16[128,1024]{1,0:T(8,128)(2,1)S(1)}, bf16[128,1024]{1,0:T(8,128)(2,1)S(1)}, u32[]{:S(2)}, u32[]{:S(2)}) collective-permute-start(bf16[128,1024]{1,0:T(8,128)(2,1)S(1)} %get-tuple-element.137), channel_id=1, source_target_pairs={{0,4},{4,0},{8,12},{12,8},{1,5},{5,1},{9,13},{13,9},{2,6},{6,2},{1... | collective-permute-start | bytes 786440 | tf_op jit(solution)/shard_map/ppermute | solution.py:522
  38.4 2.3 %more_delta.1 = (bf16[256,1024]{1,0:T(8,128)(2,1)S(1)}, bf16[64,1024]{1,0:T(8,128)(2,1)S(1)}, bf16[64,1024]{1,0:T(8,128)(2,1)S(1)}, bf16[64,1024]{1,0:T(8,128)(2...) custom-call(bf16[320,2048]{1,0:T(8,128)(2,1)S(1)} %get-tuple-element.138.xc_ref, ...), custom_call_target="tpu_custom_call" | custom-call | flops 1 | bytes 1 | tf_op jit(solution)/shard_map/more_delta/pallas_call | solution.py:241
  41.8 3.4 %collective-permute-done.18 = bf16[128,1024]{1,0:T(8,128)(2,1)S(1)} collective-permute-done((bf16[128,1024]{1,0:T(8,128)(2,1)S(1)}, bf16[128,1024]{1,0:T(8,128)(2,1)S(1)}, u32[]{:S(2)}, u32[]{:S(2)}) %collective-permute-start.18) | collective-permute-done | bytes 262176 | tf_op jit(solution)/shard_map/ppermute | solution.py:522
  45.3 1.8 %collective-permute-start.24 = (bf16[128,1024]{1,0:T(8,128)(2,1)S(1)}, bf16[128,1024]{1,0:T(8,128)(2,1)S(1)}, u32[]{:S(2)}, u32[]{:S(2)}) collective-permute-start(bf16[128,1024]{1,0:T(8,128)(2,1)S(1)} %get-tuple-element.157), channel_id=1, source_target_pairs={{0,4},{4,0},{8,12},{12,8},{1,5},{5,1},{9,13},{13,9},{2,6},{6,2},{1... | collective-permute-start | bytes 786440 | tf_op jit(solution)/shard_map/ppermute | solution.py:522
  47.2 1.6 %collective-permute-start.19 = (bf16[128,1024]{1,0:T(8,128)(2,1)S(1)}, bf16[128,1024]{1,0:T(8,128)(2,1)S(1)}, u32[]{:S(2)}, u32[]{:S(2)}) collective-permute-start(bf16[128,1024]{1,0:T(8,128)(2,1)S(1)} %add_convert_fusion.2), channel_id=1, source_target_pairs={{0,2},{1,3},{2,0},{3,1},{4,6},{5,7},{6,4},{7,5},{8,10},{9,11},{10,... | collective-permute-start | bytes 786440 | tf_op jit(solution)/shard_map/ppermute | solution.py:540
  48.9 5.5 %attend_cache.4 = (f32[32,128,128]{2,1,0:T(8,128)S(1)}, f32[32,1,128]{2,1,0:T(1,128)S(1)}, bf16[32,128,128]{2,1,0:T(8,128)(2,1)S(1)}, f32[8,128]{1,0:T(8,128)}) custom-call(s32[32]{0:T(128)S(1)} %copy-done, bf16[2,32,8192]{2,1,0:T(8,128)(2,1)} %q_ref.5, bf16[32,128,2048]{2,1,0:T(8,128)(2,1)} %kv_ref.5, ...), custom_call_target="tpu_custom_call", output_to_operand_aliasing={{0}: (3, {}), {1}: (4, {}), {2}: (5, {})} | custom-call | flops 1 | bytes 1 | tf_op jit(solution)/shard_map/attend_cache/pallas_call | solution.py:355
  54.9 1.6 %collective-permute-start.25 = (bf16[128,1024]{1,0:T(8,128)(2,1)S(1)}, bf16[128,1024]{1,0:T(8,128)(2,1)S(1)}, u32[]{:S(2)}, u32[]{:S(2)}) collective-permute-start(bf16[128,1024]{1,0:T(8,128)(2,1)S(1)} %add_convert_fusion.1), channel_id=1, source_target_pairs={{0,2},{1,3},{2,0},{3,1},{4,6},{5,7},{6,4},{7,5},{8,10},{9,11},{10,... | collective-permute-start | bytes 786440 | tf_op jit(solution)/shard_map/ppermute | solution.py:540
  56.4 2.6 %collective-permute-start.27 = (bf16[64,1024]{1,0:T(8,128)(2,1)S(1)}, bf16[64,1024]{1,0:T(8,128)(2,1)S(1)}, u32[]{:S(2)}, u32[]{:S(2)}) collective-permute-start(bf16[64,1024]{1,0:T(8,128)(2,1)S(1)} %get-tuple-element.180), channel_id=1, source_target_pairs={{0,8},{4,12},{8,0},{12,4},{1,9},{5,13},{9,1},{13,5},{2,10},{6,14},... | collective-permute-start | bytes 393224 | tf_op jit(solution)/shard_map/ppermute | solution.py:522
  59.0 3.6 %attend_cache.5 = (f32[32,128,128]{2,1,0:T(8,128)S(1)}, f32[32,1,128]{2,1,0:T(1,128)S(1)}, bf16[32,128,128]{2,1,0:T(8,128)(2,1)S(1)}, f32[8,128]{1,0:T(8,128)}) custom-call(s32[32]{0:T(128)S(1)} %copy-done, bf16[2,32,8192]{2,1,0:T(8,128)(2,1)} %q_ref.5, bf16[32,128,2048]{2,1,0:T(8,128)(2,1)} %kv_ref.5, ...), custom_call_target="tpu_custom_call", output_to_operand_aliasing={{0}: (3, {}), {1}: (4, {}), {2}: (5, {})} | custom-call | flops 1 | bytes 1 | tf_op jit(solution)/shard_map/attend_cache/pallas_call | solution.py:355
  62.7 1.8 %collective-permute-start.26 = (bf16[64,1024]{1,0:T(8,128)(2,1)S(1)}, bf16[64,1024]{1,0:T(8,128)(2,1)S(1)}, u32[]{:S(2)}, u32[]{:S(2)}) collective-permute-start(bf16[64,1024]{1,0:T(8,128)(2,1)S(1)} %get-tuple-element.196), channel_id=1, source_target_pairs={{0,8},{4,12},{8,0},{12,4},{1,9},{5,13},{9,1},{13,5},{2,10},{6,14},... | collective-permute-start | bytes 393224 | tf_op jit(solution)/shard_map/ppermute | solution.py:522
  64.6 2.5 %weigh_new.1 = (bf16[32,128,16]{2,1,0:T(8,128)(2,1)S(1)}, f32[32,128,128]{2,1,0:T(8,128)S(1)}) custom-call(f32[32,128,128]{2,1,0:T(8,128)S(1)} %get-tuple-element.177.o_ref, f32[32,1,128]{2,1,0:T(1,128)S(1)} %get-tuple-element.178.lse_ref, bf16[32,128,128]{2,1,0:T(8,128)(2,1)S(1)} %get-tuple-element.179.turned_ref, f32[2,32,8,128]{3,2,1,0:T(8,128)S(1)} %bitcast.12), custom_call_target="tpu_custom_call" | custom-call | flops 1 | bytes 1 | tf_op jit(solution)/shard_map/weigh_new/pallas_call | solution.py:418
  67.1 2.8 %collective-permute-done.26 = bf16[64,1024]{1,0:T(8,128)(2,1)S(1)} collective-permute-done((bf16[64,1024]{1,0:T(8,128)(2,1)S(1)}, bf16[64,1024]{1,0:T(8,128)(2,1)S(1)}, u32[]{:S(2)}, u32[]{:S(2)}) %collective-permute-start.26) | collective-permute-done | bytes 131104 | tf_op jit(solution)/shard_map/ppermute | solution.py:522
  70.0 2.6 %add_new.1 = (bf16[2,32,8192]{2,1,0:T(8,128)(2,1)}, bf16[2,32,2048]{2,1,0:T(8,128)(2,1)}) custom-call(bf16[32,128,16]{2,1,0:T(8,128)(2,1)S(1)} %get-tuple-element.184.prob_ref, f32[32,128,128]{2,1,0:T(8,128)S(1)} %get-tuple-element.185.o_ref, bf16[2,32,1024]{2,1,0:T(8,128)(2,1)S(1)} %bitcast.13, bf16[2,32,1024]{2,1,0:T(8,128)(2,1)S(1)} %bitcast.14, ...), custom_call_target="tpu_custom_call" | custom-call | flops 1 | bytes 1 | tf_op jit(solution)/shard_map/add_new/pallas_call | solution.py:469
  (63 shorter events, 10.2 us)
Async XLA Ops:
  0.6 5.0 %collective-permute-start.1 = (bf16[256,2048]{1,0:T(8,128)(2,1)}, bf16[256,2048]{1,0:T(8,128)(2,1)S(1)}, u32[]{:S(2)}, u32[]{:S(2)}) collective-permute-start(bf16[256,2048]{1,0:T(8,128)(2,1)} %bitcast.15), channel_id=1, source_target_pairs={{0,1},{1,0},{2,3},{3,2},{4,5},{5,4},{6,7},{7,6},{8,9},{9,8},{10,11... | collective-permute-start | bytes 3145736 | tf_op jit(solution)/shard_map/ppermute | solution.py:540
  1.1 26.6 %collective-permute-start.7 = (bf16[256,2048]{1,0:T(8,128)(2,1)}, bf16[256,2048]{1,0:T(8,128)(2,1)S(1)}, u32[]{:S(2)}, u32[]{:S(2)}) collective-permute-start(bf16[256,2048]{1,0:T(8,128)(2,1)} %bitcast.16), channel_id=1, source_target_pairs={{0,2},{1,3},{2,0},{3,1},{4,6},{5,7},{6,4},{7,5},{8,10},{9,11},{10,... | collective-permute-start | bytes 3145736 | tf_op jit(solution)/shard_map/ppermute | solution.py:540
  17.5 1.6 %collective-permute-start.2 = (bf16[64,2048]{1,0:T(8,128)(2,1)S(1)}, bf16[64,2048]{1,0:T(8,128)(2,1)S(1)}, u32[]{:S(2)}, u32[]{:S(2)}) collective-permute-start(bf16[64,2048]{1,0:T(8,128)(2,1)S(1)} %get-tuple-element.97), channel_id=1, source_target_pairs={{0,1},{1,0},{2,3},{3,2},{4,5},{5,4},{6,7},{7,6},{8,9},{9,8},{10,11... | collective-permute-start | bytes 786440 | tf_op jit(solution)/shard_map/ppermute | solution.py:540
  17.7 1.7 %collective-permute-start.3 = (bf16[64,2048]{1,0:T(8,128)(2,1)S(1)}, bf16[64,2048]{1,0:T(8,128)(2,1)S(1)}, u32[]{:S(2)}, u32[]{:S(2)}) collective-permute-start(bf16[64,2048]{1,0:T(8,128)(2,1)S(1)} %get-tuple-element.98), channel_id=1, source_target_pairs={{0,1},{1,0},{2,3},{3,2},{4,5},{5,4},{6,7},{7,6},{8,9},{9,8},{10,11... | collective-permute-start | bytes 786440 | tf_op jit(solution)/shard_map/ppermute | solution.py:540
  18.0 1.8 %collective-permute-start.4 = (bf16[64,2048]{1,0:T(8,128)(2,1)S(1)}, bf16[64,2048]{1,0:T(8,128)(2,1)S(1)}, u32[]{:S(2)}, u32[]{:S(2)}) collective-permute-start(bf16[64,2048]{1,0:T(8,128)(2,1)S(1)} %get-tuple-element.99), channel_id=1, source_target_pairs={{0,1},{1,0},{2,3},{3,2},{4,5},{5,4},{6,7},{7,6},{8,9},{9,8},{10,11... | collective-permute-start | bytes 786440 | tf_op jit(solution)/shard_map/ppermute | solution.py:540
  18.2 1.9 %collective-permute-start.5 = (bf16[64,2048]{1,0:T(8,128)(2,1)S(1)}, bf16[64,2048]{1,0:T(8,128)(2,1)S(1)}, u32[]{:S(2)}, u32[]{:S(2)}) collective-permute-start(bf16[64,2048]{1,0:T(8,128)(2,1)S(1)} %get-tuple-element.100), channel_id=1, source_target_pairs={{0,1},{1,0},{2,3},{3,2},{4,5},{5,4},{6,7},{7,6},{8,9},{9,8},{10,11... | collective-permute-start | bytes 786440 | tf_op jit(solution)/shard_map/ppermute | solution.py:540
  20.4 14.9 %collective-permute-start.6 = (bf16[128,2048]{1,0:T(8,128)(2,1)S(1)}, bf16[128,2048]{1,0:T(8,128)(2,1)S(1)}, u32[]{:S(2)}, u32[]{:S(2)}) collective-permute-start(bf16[128,2048]{1,0:T(8,128)(2,1)S(1)} %get-tuple-element.109), channel_id=1, source_target_pairs={{0,4},{4,0},{8,12},{12,8},{1,5},{5,1},{9,13},{13,9},{2,6},{6,2},{1... | collective-permute-start | bytes 1572872 | tf_op jit(solution)/shard_map/ppermute | solution.py:522
  22.1 5.3 %collective-permute-start.9 = (s32[1,8]{1,0:T(1,128)S(1)}, s32[1,8]{1,0:T(1,128)S(1)}, u32[]{:S(2)}, u32[]{:S(2)}) collective-permute-start(s32[1,8]{1,0:T(1,128)S(1)} %pad_add_fusion.refs_1_), channel_id=1, source_target_pairs={{0,3},{1,2},{2,1},{3,0},{4,7},{5,6},{6,5},{7,4},{8,11},{9,10},{10,... | collective-permute-start | bytes 104 | tf_op jit(solution)/shard_map/ppermute | solution.py:540
  22.4 5.3 %collective-permute-start.8 = (s32[1,8]{1,0:T(1,128)S(1)}, s32[1,8]{1,0:T(1,128)S(1)}, u32[]{:S(2)}, u32[]{:S(2)}) collective-permute-start(s32[1,8]{1,0:T(1,128)S(1)} %pad_add_fusion.refs_1_), channel_id=1, source_target_pairs={{0,2},{1,3},{2,0},{3,1},{4,6},{5,7},{6,4},{7,5},{8,10},{9,11},{10,... | collective-permute-start | bytes 104 | tf_op jit(solution)/shard_map/ppermute | solution.py:540
  27.8 1.6 %collective-permute-start.10 = (bf16[64,2048]{1,0:T(8,128)(2,1)S(1)}, bf16[64,2048]{1,0:T(8,128)(2,1)S(1)}, u32[]{:S(2)}, u32[]{:S(2)}) collective-permute-start(bf16[64,2048]{1,0:T(8,128)(2,1)S(1)} %get-tuple-element.115), channel_id=1, source_target_pairs={{0,1},{1,0},{2,3},{3,2},{4,5},{5,4},{6,7},{7,6},{8,9},{9,8},{10,11... | collective-permute-start | bytes 786440 | tf_op jit(solution)/shard_map/ppermute | solution.py:540
  27.9 1.9 %collective-permute-start.11 = (bf16[64,2048]{1,0:T(8,128)(2,1)S(1)}, bf16[64,2048]{1,0:T(8,128)(2,1)S(1)}, u32[]{:S(2)}, u32[]{:S(2)}) collective-permute-start(bf16[64,2048]{1,0:T(8,128)(2,1)S(1)} %get-tuple-element.116), channel_id=1, source_target_pairs={{0,1},{1,0},{2,3},{3,2},{4,5},{5,4},{6,7},{7,6},{8,9},{9,8},{10,11... | collective-permute-start | bytes 786440 | tf_op jit(solution)/shard_map/ppermute | solution.py:540
  28.4 1.8 %collective-permute-start.12 = (bf16[64,2048]{1,0:T(8,128)(2,1)S(1)}, bf16[64,2048]{1,0:T(8,128)(2,1)S(1)}, u32[]{:S(2)}, u32[]{:S(2)}) collective-permute-start(bf16[64,2048]{1,0:T(8,128)(2,1)S(1)} %get-tuple-element.117), channel_id=1, source_target_pairs={{0,1},{1,0},{2,3},{3,2},{4,5},{5,4},{6,7},{7,6},{8,9},{9,8},{10,11... | collective-permute-start | bytes 786440 | tf_op jit(solution)/shard_map/ppermute | solution.py:540
  28.5 2.1 %collective-permute-start.13 = (bf16[64,2048]{1,0:T(8,128)(2,1)S(1)}, bf16[64,2048]{1,0:T(8,128)(2,1)S(1)}, u32[]{:S(2)}, u32[]{:S(2)}) collective-permute-start(bf16[64,2048]{1,0:T(8,128)(2,1)S(1)} %get-tuple-element.118), channel_id=1, source_target_pairs={{0,1},{1,0},{2,3},{3,2},{4,5},{5,4},{6,7},{7,6},{8,9},{9,8},{10,11... | collective-permute-start | bytes 786440 | tf_op jit(solution)/shard_map/ppermute | solution.py:540
  34.2 1.4 %collective-permute-start.14 = (bf16[64,1024]{1,0:T(8,128)(2,1)S(1)}, bf16[64,1024]{1,0:T(8,128)(2,1)S(1)}, u32[]{:S(2)}, u32[]{:S(2)}) collective-permute-start(bf16[64,1024]{1,0:T(8,128)(2,1)S(1)} %get-tuple-element.125), channel_id=1, source_target_pairs={{0,1},{1,0},{2,3},{3,2},{4,5},{5,4},{6,7},{7,6},{8,9},{9,8},{10,11... | collective-permute-start | bytes 393224 | tf_op jit(solution)/shard_map/ppermute | solution.py:540
  36.5 8.7 %collective-permute-start.18 = (bf16[128,1024]{1,0:T(8,128)(2,1)S(1)}, bf16[128,1024]{1,0:T(8,128)(2,1)S(1)}, u32[]{:S(2)}, u32[]{:S(2)}) collective-permute-start(bf16[128,1024]{1,0:T(8,128)(2,1)S(1)} %get-tuple-element.137), channel_id=1, source_target_pairs={{0,4},{4,0},{8,12},{12,8},{1,5},{5,1},{9,13},{13,9},{2,6},{6,2},{1... | collective-permute-start | bytes 786440 | tf_op jit(solution)/shard_map/ppermute | solution.py:522
  40.7 4.5 %collective-permute-start.20 = (bf16[64,1024]{1,0:T(8,128)(2,1)S(1)}, bf16[64,1024]{1,0:T(8,128)(2,1)S(1)}, u32[]{:S(2)}, u32[]{:S(2)}) collective-permute-start(bf16[64,1024]{1,0:T(8,128)(2,1)S(1)} %get-tuple-element.145), channel_id=1, source_target_pairs={{0,1},{1,0},{2,3},{3,2},{4,5},{5,4},{6,7},{7,6},{8,9},{9,8},{10,11... | collective-permute-start | bytes 393224 | tf_op jit(solution)/shard_map/ppermute | solution.py:540
  40.8 4.4 %collective-permute-start.21 = (bf16[64,1024]{1,0:T(8,128)(2,1)S(1)}, bf16[64,1024]{1,0:T(8,128)(2,1)S(1)}, u32[]{:S(2)}, u32[]{:S(2)}) collective-permute-start(bf16[64,1024]{1,0:T(8,128)(2,1)S(1)} %get-tuple-element.146), channel_id=1, source_target_pairs={{0,1},{1,0},{2,3},{3,2},{4,5},{5,4},{6,7},{7,6},{8,9},{9,8},{10,11... | collective-permute-start | bytes 393224 | tf_op jit(solution)/shard_map/ppermute | solution.py:540
  41.3 3.9 %collective-permute-start.22 = (bf16[64,1024]{1,0:T(8,128)(2,1)S(1)}, bf16[64,1024]{1,0:T(8,128)(2,1)S(1)}, u32[]{:S(2)}, u32[]{:S(2)}) collective-permute-start(bf16[64,1024]{1,0:T(8,128)(2,1)S(1)} %get-tuple-element.147), channel_id=1, source_target_pairs={{0,1},{1,0},{2,3},{3,2},{4,5},{5,4},{6,7},{7,6},{8,9},{9,8},{10,11... | collective-permute-start | bytes 393224 | tf_op jit(solution)/shard_map/ppermute | solution.py:540
  41.3 3.9 %collective-permute-start.23 = (bf16[64,1024]{1,0:T(8,128)(2,1)S(1)}, bf16[64,1024]{1,0:T(8,128)(2,1)S(1)}, u32[]{:S(2)}, u32[]{:S(2)}) collective-permute-start(bf16[64,1024]{1,0:T(8,128)(2,1)S(1)} %get-tuple-element.148), channel_id=1, source_target_pairs={{0,1},{1,0},{2,3},{3,2},{4,5},{5,4},{6,7},{7,6},{8,9},{9,8},{10,11... | collective-permute-start | bytes 393224 | tf_op jit(solution)/shard_map/ppermute | solution.py:540
  45.3 9.1 %collective-permute-start.24 = (bf16[128,1024]{1,0:T(8,128)(2,1)S(1)}, bf16[128,1024]{1,0:T(8,128)(2,1)S(1)}, u32[]{:S(2)}, u32[]{:S(2)}) collective-permute-start(bf16[128,1024]{1,0:T(8,128)(2,1)S(1)} %get-tuple-element.157), channel_id=1, source_target_pairs={{0,4},{4,0},{8,12},{12,8},{1,5},{5,1},{9,13},{13,9},{2,6},{6,2},{1... | collective-permute-start | bytes 786440 | tf_op jit(solution)/shard_map/ppermute | solution.py:522
  47.2 7.5 %collective-permute-start.19 = (bf16[128,1024]{1,0:T(8,128)(2,1)S(1)}, bf16[128,1024]{1,0:T(8,128)(2,1)S(1)}, u32[]{:S(2)}, u32[]{:S(2)}) collective-permute-start(bf16[128,1024]{1,0:T(8,128)(2,1)S(1)} %add_convert_fusion.2), channel_id=1, source_target_pairs={{0,2},{1,3},{2,0},{3,1},{4,6},{5,7},{6,4},{7,5},{8,10},{9,11},{10,... | collective-permute-start | bytes 786440 | tf_op jit(solution)/shard_map/ppermute | solution.py:540
  54.9 7.7 %collective-permute-start.25 = (bf16[128,1024]{1,0:T(8,128)(2,1)S(1)}, bf16[128,1024]{1,0:T(8,128)(2,1)S(1)}, u32[]{:S(2)}, u32[]{:S(2)}) collective-permute-start(bf16[128,1024]{1,0:T(8,128)(2,1)S(1)} %add_convert_fusion.1), channel_id=1, source_target_pairs={{0,2},{1,3},{2,0},{3,1},{4,6},{5,7},{6,4},{7,5},{8,10},{9,11},{10,... | collective-permute-start | bytes 786440 | tf_op jit(solution)/shard_map/ppermute | solution.py:540
  56.4 8.1 %collective-permute-start.27 = (bf16[64,1024]{1,0:T(8,128)(2,1)S(1)}, bf16[64,1024]{1,0:T(8,128)(2,1)S(1)}, u32[]{:S(2)}, u32[]{:S(2)}) collective-permute-start(bf16[64,1024]{1,0:T(8,128)(2,1)S(1)} %get-tuple-element.180), channel_id=1, source_target_pairs={{0,8},{4,12},{8,0},{12,4},{1,9},{5,13},{9,1},{13,5},{2,10},{6,14},... | collective-permute-start | bytes 393224 | tf_op jit(solution)/shard_map/ppermute | solution.py:522
  62.7 7.2 %collective-permute-start.26 = (bf16[64,1024]{1,0:T(8,128)(2,1)S(1)}, bf16[64,1024]{1,0:T(8,128)(2,1)S(1)}, u32[]{:S(2)}, u32[]{:S(2)}) collective-permute-start(bf16[64,1024]{1,0:T(8,128)(2,1)S(1)} %get-tuple-element.196), channel_id=1, source_target_pairs={{0,8},{4,12},{8,0},{12,4},{1,9},{5,13},{9,1},{13,5},{2,10},{6,14},... | collective-permute-start | bytes 393224 | tf_op jit(solution)/shard_map/ppermute | solution.py:522
  (7 other events, 21.5 us)

commit v6 on v5

--- a/solution.py
+++ b/solution.py
@@ -381,11 +381,10 @@
     )(lengths, *in_hbm(queries, kv_cache), *in_vmem(*before), *in_hbm(*gates))
 
 
-def weigh_body(o_ref, lse_ref, turned_ref, keys_ref, prob_ref, out_ref):
-    rows = o_ref.shape[0]
+def weigh_body(lse_ref, turned_ref, keys_ref, o_ref, share_ref, early_ref):
+    rows = lse_ref.shape[0]
     block = min(8, rows)
-    pairs = 2 * KVH
-    shape = (pairs, 2 * HEADS)
+    shape = (2 * KVH, 2 * HEADS)
     row = lax.broadcasted_iota(jnp.int32, shape, 0)
     col = lax.broadcasted_iota(jnp.int32, shape, 1)
     head = col // (4 * GROUP) * 2 + (col // GROUP) % 2
@@ -403,72 +402,89 @@
             top = jnp.maximum(jnp.max(scores, axis=0, keepdims=True), lse)
             expo = jnp.exp(scores - top)
             before = jnp.exp(lse - top)
-            inverse = 1.0 / (before + jnp.sum(expo, axis=0, keepdims=True))
-            shares = jnp.broadcast_to(before * inverse, shape)
-            both = jnp.concatenate([expo * inverse, shares], axis=0).T
-            prob_ref[r] = both[:, :pairs].astype(jnp.bfloat16)
-            out_ref[r] = o_ref[r] * both[:, pairs:pairs + 1]
+            parts = [jnp.sum(expo[s * KVH:(s + 1) * KVH], axis=0, keepdims=True) for s in range(2)]
+            inverse = 1.0 / (before + parts[0] + parts[1])
+            for place, part in enumerate((before, *parts)):
+                share_ref[place, pl.ds(r, 1), :] = part * inverse
         return carry
 
     lax.fori_loop(0, rows // block, some_rows, 0)
-
-
-def weigh_new(o, lse, turned, keys):
+    some = 4 * GROUP
+
+    def one_pair(pair, carry):
+        back = (2 * HEADS - some * pair) % (2 * HEADS)
+        share = pltpu.roll(share_ref[0], back, 1)
+        for inner in range(some):
+            value = o_ref[pl.ds(pair * some + inner, rows, stride=2 * HEADS), :]
+            column = pl.multiple_of((pair * (some // 2) + inner % (some // 2)) * HD, HD)
+            early_ref[inner // (some // 2), :, pl.ds(column, HD)] = value * share[:, inner:inner + 1]
+        return carry
+
+    lax.fori_loop(0, KVH // 2, one_pair, 0)
+
+
+def weigh_new(lse, turned, keys, o):
     rows = o.shape[0]
     return pl.pallas_call(
         weigh_body,
         in_specs=[VMEM] * 4,
         out_specs=[VMEM] * 2,
         out_shape=(
-            pltpu.VMEM((rows, 2 * HEADS, 2 * KVH), jnp.bfloat16),
-            pltpu.VMEM(o.shape, jnp.float32),
+            pltpu.VMEM((3, rows, 2 * HEADS), jnp.float32),
+            pltpu.VMEM((2, rows, HEADS * HD), jnp.float32),
         ),
         cost_estimate=LIGHT,
         compiler_params=pltpu.CompilerParams(vmem_limit_bytes=8 << 20),
         name="weigh_new",
-    )(*in_vmem(o, lse, turned, keys))
-
-
-def add_body(prob_ref, o_ref, keys_ref, flat_ref, vals_ref, out_hbm, new_hbm, out_ref, sum_ref, sems):
+    )(*in_vmem(lse, turned, keys, o.reshape(rows * 2 * HEADS, HD)))
+
+
+def add_body(share_ref, early_ref, keys_ref, vals_ref, out_hbm, new_hbm, out_ref, sems):
     half = keys_ref.shape[2]
-    rows = o_ref.shape[0]
-    block = min(16, rows)
-    some = 2 * GROUP
-    copies = [
-        pltpu.make_async_copy(keys_ref, new_hbm.at[:, :, :half], sems.at[0]),
-        pltpu.make_async_copy(flat_ref, new_hbm.at[:, :, half:], sems.at[1]),
-    ]
-    for copy in copies:
-        copy.start()
-    for begin in range(0, rows, block):
-        for r in range(block):
-            vals = jnp.concatenate([vals_ref[s, begin + r] for s in range(2)], axis=0)
-            sum_ref[r * 2 * HEADS:(r + 1) * 2 * HEADS, :] = o_ref[begin + r] + jnp.dot(
-                prob_ref[begin + r], vals.astype(jnp.bfloat16), preferred_element_type=jnp.float32
-            )
-        for at in range(2 * HEADS):
-            pair, step, head = at // (2 * some), (at // some) % 2, at % some
-            column = (pair * some + head) * HD
-            out_ref[step, begin:begin + block, column:column + HD] = sum_ref[
-                pl.ds(at, block, stride=2 * HEADS), :
-            ].astype(jnp.bfloat16)
-        copies.append(
-            pltpu.make_async_copy(
-                out_ref.at[:, begin:begin + block, :], out_hbm.at[:, begin:begin + block, :],
-                sems.at[2 + begin // block],
-            )
+    rows = keys_ref.shape[1]
+    some = 4 * GROUP
+    wide = some // 2 * HD
+
+    def piece(pair):
+        cols = pl.ds(pl.multiple_of(pair * wide, wide), wide)
+        return pltpu.make_async_copy(
+            out_ref.at[:, :, cols], out_hbm.at[:, :, cols], sems.at[2 + pair]
         )
-        copies[-1].start()
-    for copy in copies:
-        copy.wait()
-
-
-def add_new(probs, o, keys, flat, vals):
-    rows = o.shape[0]
-    block = min(16, rows)
+
+    first = pltpu.make_async_copy(keys_ref, new_hbm.at[:, :, :half], sems.at[0])
+    second = pltpu.make_async_copy(vals_ref, new_hbm.at[:, :, half:], sems.at[1])
+    first.start()
+    second.start()
+
+    def one_pair(pair, carry):
+        back = (2 * HEADS - some * pair) % (2 * HEADS)
+        shares = [pltpu.roll(share_ref[1 + s], back, 1) for s in range(2)]
+        for head in range(2):
+            at = pl.multiple_of((2 * pair + head) * HD, HD)
+            vals = [vals_ref[s, :, pl.ds(at, HD)].astype(jnp.float32) for s in range(2)]
+            for step in range(2):
+                for member in range(GROUP):
+                    inner = step * some // 2 + head * GROUP + member
+                    column = pl.multiple_of(pair * wide + (head * GROUP + member) * HD, HD)
+                    value = early_ref[step, :, pl.ds(column, HD)]
+                    for s in range(step + 1):
+                        value = value + vals[s] * shares[s][:, inner:inner + 1]
+                    out_ref[step, :, pl.ds(column, HD)] = value.astype(jnp.bfloat16)
+        piece(pair).start()
+        return carry
+
+    lax.fori_loop(0, KVH // 2, one_pair, 0)
+    for pair in range(KVH // 2):
+        piece(pair).wait()
+    first.wait()
+    second.wait()
+
+
+def add_new(shares, early, keys, vals):
+    rows = keys.shape[1]
     return pl.pallas_call(
         add_body,
-        in_specs=[VMEM] * 5,
+        in_specs=[VMEM] * 4,
         out_specs=[HBM, HBM],
         out_shape=(
             jax.ShapeDtypeStruct((2, rows, HEADS * HD), jnp.bfloat16),
@@ -476,13 +492,12 @@
         ),
         scratch_shapes=[
             pltpu.VMEM((2, rows, HEADS * HD), jnp.bfloat16),
-            pltpu.VMEM((block * 2 * HEADS, HD), jnp.float32),
-            pltpu.SemaphoreType.DMA((2 + rows // block,)),
+            pltpu.SemaphoreType.DMA((2 + KVH // 2,)),
         ],
         cost_estimate=LIGHT,
         compiler_params=pltpu.CompilerParams(vmem_limit_bytes=12 << 20),
         name="add_new",
-    )(*in_vmem(probs, o, keys, flat, vals))
+    )(*in_vmem(shares, early, keys, vals))
 
 
 def marker_body(*refs):
@@ -582,27 +597,28 @@
             else:
                 mine, *theirs, flag = more_delta(gathered, spread, weights, start, half, [flag])
             back = [swap(part, 1) for part in theirs]
-            if flying:
-                flying[-1], flag = tie(flying[-1], flag)
-                flying[-1] = swap(sum_of(flying[-1]), flying_mask)
-                flag = marker(flag, COVER)
-            else:
+            if not flying:
                 near, flag = tie(near, flag)
                 near = sum_of(near)
-                flag = marker(flag, LIGHT)
+            flag = marker(flag, LIGHT)
             back, flag = tie(back, flag)
             sent, kept = add_quarters(mine, back)
             sent, flag = tie(sent, flag)
             flying.append([kept, cross(sent, tensor, masks[0])])
+            if len(flying) > 1:
+                flying[-2], flag = tie(flying[-2], flag)
+                early, flag = tie(sum_of(flying[-2]), flag)
+                flying[-2] = swap(early, flying_mask)
             flying_mask = mask
 
     *done, flag = cached(2, 2, done, LIGHT, flag)
-    flying, flag = tie(flying, flag)
-    last = sum_of(flying[-1])
+    flying[-1], flag = tie(flying[-1], flag)
+    last, flag = tie(sum_of(flying[-1]), flag)
+    flying[-1] = swap(last, flying_mask)
+    flying[:-1], flag = tie(flying[:-1], flag)
     values = [[near[:, start:start + half], *flying[at::2]] for at, start in enumerate((0, half))]
     sent, kept = halves(values[0])
-    last, sent, flag = tie(last, sent, flag)
-    values[1][-1] = swap(last, flying_mask)
+    sent, flag = tie(sent, flag)
     values[0] = [kept, cross(sent, tensor, masks[1])]
     *done, flag = cached(1, 1, done, LIGHT, flag)
     values[1], done = tie(values[1], done)
@@ -618,10 +634,11 @@
         return value.astype(jnp.float32).reshape(2, shard_rows, KVH, HD)
 
     keys = sum_of(values[0]).reshape(2, shard_rows, half)
-    probs, weighed = weigh_new(*done, by_head(keys))
-    last, probs = tie(values[1], probs)
+    o, lse, turned = done
+    shares, early = weigh_new(lse, turned, by_head(keys), o)
+    last, shares = tie(values[1], shares)
     vals = sum_of(last).reshape(2, shard_rows, half)
-    attention, new_kv = add_new(probs, weighed, keys, vals, by_head(vals))
+    attention, new_kv = add_new(shares, early, keys, vals)
     return (new_kv, attention)
 
 

time: 73 us -> 70.5 us (0.966)
  starting transfers between devices: 22.1 us -> 20.8 us
    ppermute x5, waiting for transfers between devices: 6.21 us -> 4.58 us  [cross(): return lax.ppermute(value, 'tensor', [(i, i ^ mask) for i in range(tensor)])]
    ppermute x23, waiting for transfers between devices: 6.17 us -> 7.15 us  [swap(): lax.ppermute(value, 'replica', [(i, i ^ mask) for i in range(replicas)])]
  transfers between devices with their start and end apart: 28 -> 28, of which waited for: 18 -> 22; matrix products, arithmetic and copies ran while one was open for 2% -> 2% of each run, Pallas kernels for 46% -> 47%
where the time goes in v6:
time: 70.5 us; the launch traced here: 70.4 us
  Pallas kernels  35.6 us (50%)
  starting transfers between devices  20.8 us (30%)
  waiting for transfers between devices  11.7 us (17%)
  other arithmetic  1.21 us (2%)
  between operations  0.96 us (1%)
    pallas_call x3, Pallas kernels, attend_cache(): pl.pallas_call(functools.partial(cache_body, start, count), grid=(count /...  12.3 us
    pallas_call x1, Pallas kernels, first_delta(): pl.pallas_call(functools.partial(first_body, tensor, steps, rows), in_spe...  11.9 us
    ppermute x23, starting transfers between devices, swap(): lax.ppermute(value, 'replica', [(i, i ^ mask) for i in range(replicas)])  11.7 us
    ppermute x5, starting transfers between devices, cross(): return lax.ppermute(value, 'tensor', [(i, i ^ mask) for i in range(tensor)])  9.1 us
    ppermute x23, waiting for transfers between devices, swap(): lax.ppermute(value, 'replica', [(i, i ^ mask) for i in range(replicas)])  7.15 us
    ppermute x5, waiting for transfers between devices, cross(): return lax.ppermute(value, 'tensor', [(i, i ^ mask) for i in range(tensor)])  4.58 us
    pallas_call x1, Pallas kernels, far_delta(): pl.pallas_call(functools.partial(far_body, tensor, steps, half // steps,...  3.68 us
    pallas_call x1, Pallas kernels, weigh_new(): pl.pallas_call(weigh_body, in_specs=[VMEM] * 4, out_specs=[VMEM] * 2, out...  2.54 us
  transfers between devices with their start and end apart: 28, of which 22 were waited for; matrix products, arithmetic and copies ran while one was open for 2% of the time, Pallas kernels for 47%

profile of v6, /device:TPU:0, one launch (start us, length us, event | category | flops | bytes accessed | tf_op | source)
XLA Modules:
  0.0 70.4 jit_solution(10451677230549308103)
XLA Ops:
  0.6 0.5 collective-permute-start.1
  1.1 2.6 %collective-permute-start.7 = (bf16[256,2048]{1,0:T(8,128)(2,1)}, bf16[256,2048]{1,0:T(8,128)(2,1)S(1)}, u32[]{:S(2)}, u32[]{:S(2)}) collective-permute-start(bf16[256,2048]{1,0:T(8,128)(2,1)} %bitcast.13), channel_id=1, source_target_pairs={{0,2},{1,3},{2,0},{3,1},{4,6},{5,7},{6,4},{7,5},{8,10},{9,11},{10,... | collective-permute-start | bytes 3145736 | tf_op jit(solution)/shard_map/ppermute | solution.py:555
  3.7 0.7 %pad_add_fusion.refs_1_ = s32[1,8]{1,0:T(1,128)S(1)} fusion(s32[1,4]{1,0:T(1,128)} %param.16, s32[1,4]{1,0:T(1,128)} %param.15), kind=kLoop, calls=%fused_computation.10 | loop fusion | flops 8 | bytes 64 | tf_op jit(solution)/shard_map/concatenate | solution.py:568
  4.6 1.0 %collective-permute-done.refs_2_ = s32[1,8]{1,0:T(1,128)S(1)} collective-permute-done((s32[1,8]{1,0:T(1,128)S(1)}, s32[1,8]{1,0:T(1,128)S(1)}, u32[]{:S(2)}, u32[]{:S(2)}) %collective-permute-start) | collective-permute-done | bytes 64 | tf_op jit(solution)/shard_map/ppermute | solution.py:555
  5.6 11.9 %first_delta.1 = (bf16[256,2048]{1,0:T(8,128)(2,1)S(1)}, bf16[64,2048]{1,0:T(8,128)(2,1)S(1)}, bf16[64,2048]{1,0:T(8,128)(2,1)S(1)}, bf16[64,2048]{1,0:T(8,128)(...) custom-call(s32[8]{0:T(128)} %refs_0_.3, ...), custom_call_target="tpu_custom_call" | custom-call | flops 1 | bytes 1 | tf_op jit(solution)/shard_map/first_delta/pallas_call | solution.py:202
  18.5 0.5 collective-permute-done.2.refs_0_
  20.4 1.6 %collective-permute-start.6 = (bf16[128,2048]{1,0:T(8,128)(2,1)S(1)}, bf16[128,2048]{1,0:T(8,128)(2,1)S(1)}, u32[]{:S(2)}, u32[]{:S(2)}) collective-permute-start(bf16[128,2048]{1,0:T(8,128)(2,1)S(1)} %get-tuple-element.113), channel_id=1, source_target_pairs={{0,4},{4,0},{8,12},{12,8},{1,5},{5,1},{9,13},{13,9},{2,6},{6,2},{1... | collective-permute-start | bytes 1572872 | tf_op jit(solution)/shard_map/ppermute | solution.py:537
  22.4 1.2 %collective-permute-start.8 = (s32[1,8]{1,0:T(1,128)S(1)}, s32[1,8]{1,0:T(1,128)S(1)}, u32[]{:S(2)}, u32[]{:S(2)}) collective-permute-start(s32[1,8]{1,0:T(1,128)S(1)} %pad_add_fusion.refs_1_), channel_id=1, source_target_pairs={{0,2},{1,3},{2,0},{3,1},{4,6},{5,7},{6,4},{7,5},{8,10},{9,11},{10,... | collective-permute-start | bytes 104 | tf_op jit(solution)/shard_map/ppermute | solution.py:555
  23.6 3.5 %attend_cache.3 = (f32[32,128,128]{2,1,0:T(8,128)S(1)}, f32[32,1,128]{2,1,0:T(1,128)S(1)}, bf16[32,128,128]{2,1,0:T(8,128)(2,1)S(1)}, f32[8,128]{1,0:T(8,128)}) custom-call(s32[32]{0:T(128)S(1)} %copy-done, bf16[2,32,8192]{2,1,0:T(8,128)(2,1)} %q_ref.5, bf16[32,128,2048]{2,1,0:T(8,128)(2,1)} %kv_ref.5, f32[8,128]{1,0:T(8,128)} %marker.3.refs_0_), custom_call_target="tpu_custom_call" | custom-call | flops 1 | bytes 1 | tf_op jit(solution)/shard_map/attend_cache/pallas_call | solution.py:355
  27.9 0.5 collective-permute-start.11
  28.9 0.5 collective-permute-done.10.refs_4_
  30.6 3.7 %far_delta.1 = (bf16[256,1024]{1,0:T(8,128)(2,1)S(1)}, bf16[64,1024]{1,0:T(8,128)(2,1)S(1)}, bf16[64,1024]{1,0:T(8,128)(2,1)S(1)}, bf16[64,1024]{1,0:T(8,128)(2,...) custom-call(s32[8]{0:T(128)} %refs_0_.3, ...), custom_call_target="tpu_custom_call" | custom-call | flops 1 | bytes 1 | tf_op jit(solution)/shard_map/far_delta/pallas_call | solution.py:228
  36.5 1.9 %collective-permute-start.23 = (bf16[128,1024]{1,0:T(8,128)(2,1)S(1)}, bf16[128,1024]{1,0:T(8,128)(2,1)S(1)}, u32[]{:S(2)}, u32[]{:S(2)}) collective-permute-start(bf16[128,1024]{1,0:T(8,128)(2,1)S(1)} %get-tuple-element.161), channel_id=1, source_target_pairs={{0,4},{4,0},{8,12},{12,8},{1,5},{5,1},{9,13},{13,9},{2,6},{6,2},{1... | collective-permute-start | bytes 786440 | tf_op jit(solution)/shard_map/ppermute | solution.py:537
  38.4 2.3 %more_delta.1 = (bf16[256,1024]{1,0:T(8,128)(2,1)S(1)}, bf16[64,1024]{1,0:T(8,128)(2,1)S(1)}, bf16[64,1024]{1,0:T(8,128)(2,1)S(1)}, bf16[64,1024]{1,0:T(8,128)(2...) custom-call(bf16[320,2048]{1,0:T(8,128)(2,1)S(1)} %get-tuple-element.128.xc_ref, ...), custom_call_target="tpu_custom_call" | custom-call | flops 1 | bytes 1 | tf_op jit(solution)/shard_map/more_delta/pallas_call | solution.py:241
  43.2 2.0 %collective-permute-done.23 = bf16[128,1024]{1,0:T(8,128)(2,1)S(1)} collective-permute-done((bf16[128,1024]{1,0:T(8,128)(2,1)S(1)}, bf16[128,1024]{1,0:T(8,128)(2,1)S(1)}, u32[]{:S(2)}, u32[]{:S(2)}) %collective-permute-start.23) | collective-permute-done | bytes 262176 | tf_op jit(solution)/shard_map/ppermute | solution.py:537
  45.3 1.7 %collective-permute-start.25 = (bf16[128,1024]{1,0:T(8,128)(2,1)S(1)}, bf16[128,1024]{1,0:T(8,128)(2,1)S(1)}, u32[]{:S(2)}, u32[]{:S(2)}) collective-permute-start(bf16[128,1024]{1,0:T(8,128)(2,1)S(1)} %add_convert_fusion.2), channel_id=1, source_target_pairs={{0,2},{1,3},{2,0},{3,1},{4,6},{5,7},{6,4},{7,5},{8,10},{9,11},{10,... | collective-permute-start | bytes 786440 | tf_op jit(solution)/shard_map/ppermute | solution.py:555
  47.0 5.3 %attend_cache.4 = (f32[32,128,128]{2,1,0:T(8,128)S(1)}, f32[32,1,128]{2,1,0:T(1,128)S(1)}, bf16[32,128,128]{2,1,0:T(8,128)(2,1)S(1)}, f32[8,128]{1,0:T(8,128)}) custom-call(s32[32]{0:T(128)S(1)} %copy-done, bf16[2,32,8192]{2,1,0:T(8,128)(2,1)} %q_ref.5, bf16[32,128,2048]{2,1,0:T(8,128)(2,1)} %kv_ref.5, ...), custom_call_target="tpu_custom_call", output_to_operand_aliasing={{0}: (3, {}), {1}: (4, {}), {2}: (5, {})} | custom-call | flops 1 | bytes 1 | tf_op jit(solution)/shard_map/attend_cache/pallas_call | solution.py:355
  52.4 0.8 %collective-permute-start.24 = (bf16[128,1024]{1,0:T(8,128)(2,1)S(1)}, bf16[128,1024]{1,0:T(8,128)(2,1)S(1)}, u32[]{:S(2)}, u32[]{:S(2)}) collective-permute-start(bf16[128,1024]{1,0:T(8,128)(2,1)S(1)} %add_convert_fusion.1), channel_id=1, source_target_pairs={{0,2},{1,3},{2,0},{3,1},{4,6},{5,7},{6,4},{7,5},{8,10},{9,11},{10,... | collective-permute-start | bytes 786440 | tf_op jit(solution)/shard_map/ppermute | solution.py:555
  53.4 2.6 %collective-permute-start.27 = (bf16[64,1024]{1,0:T(8,128)(2,1)S(1)}, bf16[64,1024]{1,0:T(8,128)(2,1)S(1)}, u32[]{:S(2)}, u32[]{:S(2)}) collective-permute-start(bf16[64,1024]{1,0:T(8,128)(2,1)S(1)} %get-tuple-element.187), channel_id=1, source_target_pairs={{0,8},{4,12},{8,0},{12,4},{1,9},{5,13},{9,1},{13,5},{2,10},{6,14},... | collective-permute-start | bytes 393224 | tf_op jit(solution)/shard_map/ppermute | solution.py:537
  56.1 3.5 %attend_cache.5 = (f32[32,128,128]{2,1,0:T(8,128)S(1)}, f32[32,1,128]{2,1,0:T(1,128)S(1)}, bf16[32,128,128]{2,1,0:T(8,128)(2,1)S(1)}, f32[8,128]{1,0:T(8,128)}) custom-call(s32[32]{0:T(128)S(1)} %copy-done, bf16[2,32,8192]{2,1,0:T(8,128)(2,1)} %q_ref.5, bf16[32,128,2048]{2,1,0:T(8,128)(2,1)} %kv_ref.5, ...), custom_call_target="tpu_custom_call", output_to_operand_aliasing={{0}: (3, {}), {1}: (4, {}), {2}: (5, {})} | custom-call | flops 1 | bytes 1 | tf_op jit(solution)/shard_map/attend_cache/pallas_call | solution.py:355
  59.9 2.7 %collective-permute-start.26 = (bf16[64,1024]{1,0:T(8,128)(2,1)S(1)}, bf16[64,1024]{1,0:T(8,128)(2,1)S(1)}, u32[]{:S(2)}, u32[]{:S(2)}) collective-permute-start(bf16[64,1024]{1,0:T(8,128)(2,1)S(1)} %get-tuple-element.202), channel_id=1, source_target_pairs={{0,8},{4,12},{8,0},{12,4},{1,9},{5,13},{9,1},{13,5},{2,10},{6,14},... | collective-permute-start | bytes 393224 | tf_op jit(solution)/shard_map/ppermute | solution.py:537
  62.7 2.5 %weigh_new.1 = (f32[3,32,128]{2,1,0:T(8,128)S(1)}, f32[2,32,8192]{2,1,0:T(8,128)S(1)}) custom-call(f32[32,1,128]{2,1,0:T(1,128)S(1)} %get-tuple-element.185.lse_ref, bf16[32,128,128]{2,1,0:T(8,128)(2,1)S(1)} %get-tuple-element.186.turned_ref, f32[2,32,8,128]{3,2,1,0:T(8,128)S(1)} %bitcast.9, f32[4096,128]{1,0:T(8,128)S(1)} %bitcast.8), custom_call_target="tpu_custom_call" | custom-call | flops 1 | bytes 1 | tf_op jit(solution)/shard_map/weigh_new/pallas_call | solution.py:428
  65.2 2.6 %collective-permute-done.26 = bf16[64,1024]{1,0:T(8,128)(2,1)S(1)} collective-permute-done((bf16[64,1024]{1,0:T(8,128)(2,1)S(1)}, bf16[64,1024]{1,0:T(8,128)(2,1)S(1)}, u32[]{:S(2)}, u32[]{:S(2)}) %collective-permute-start.26) | collective-permute-done | bytes 131104 | tf_op jit(solution)/shard_map/ppermute | solution.py:537
  67.9 2.4 %add_new.1 = (bf16[2,32,8192]{2,1,0:T(8,128)(2,1)}, bf16[2,32,2048]{2,1,0:T(8,128)(2,1)}) custom-call(f32[3,32,128]{2,1,0:T(8,128)S(1)} %get-tuple-element.192.share_ref, f32[2,32,8192]{2,1,0:T(8,128)S(1)} %get-tuple-element.193.early_ref, bf16[2,32,1024]{2,1,0:T(8,128)(2,1)S(1)} %bitcast.10, bf16[2,32,1024]{2,1,0:T(8,128)(2,1)S(1)} %bitcast.11), custom_call_target="tpu_custom_call" | custom-call | flops 1 | bytes 1 | tf_op jit(solution)/shard_map/add_new/pallas_call | solution.py:485
  (59 shorter events, 10.9 us)
Async XLA Ops:
  0.6 5.0 %collective-permute-start.1 = (bf16[256,2048]{1,0:T(8,128)(2,1)}, bf16[256,2048]{1,0:T(8,128)(2,1)S(1)}, u32[]{:S(2)}, u32[]{:S(2)}) collective-permute-start(bf16[256,2048]{1,0:T(8,128)(2,1)} %bitcast.12), channel_id=1, source_target_pairs={{0,1},{1,0},{2,3},{3,2},{4,5},{5,4},{6,7},{7,6},{8,9},{9,8},{10,11... | collective-permute-start | bytes 3145736 | tf_op jit(solution)/shard_map/ppermute | solution.py:555
  1.1 26.6 %collective-permute-start.7 = (bf16[256,2048]{1,0:T(8,128)(2,1)}, bf16[256,2048]{1,0:T(8,128)(2,1)S(1)}, u32[]{:S(2)}, u32[]{:S(2)}) collective-permute-start(bf16[256,2048]{1,0:T(8,128)(2,1)} %bitcast.13), channel_id=1, source_target_pairs={{0,2},{1,3},{2,0},{3,1},{4,6},{5,7},{6,4},{7,5},{8,10},{9,11},{10,... | collective-permute-start | bytes 3145736 | tf_op jit(solution)/shard_map/ppermute | solution.py:555
  17.5 1.6 %collective-permute-start.2 = (bf16[64,2048]{1,0:T(8,128)(2,1)S(1)}, bf16[64,2048]{1,0:T(8,128)(2,1)S(1)}, u32[]{:S(2)}, u32[]{:S(2)}) collective-permute-start(bf16[64,2048]{1,0:T(8,128)(2,1)S(1)} %get-tuple-element.101), channel_id=1, source_target_pairs={{0,1},{1,0},{2,3},{3,2},{4,5},{5,4},{6,7},{7,6},{8,9},{9,8},{10,11... | collective-permute-start | bytes 786440 | tf_op jit(solution)/shard_map/ppermute | solution.py:555
  17.7 1.7 %collective-permute-start.3 = (bf16[64,2048]{1,0:T(8,128)(2,1)S(1)}, bf16[64,2048]{1,0:T(8,128)(2,1)S(1)}, u32[]{:S(2)}, u32[]{:S(2)}) collective-permute-start(bf16[64,2048]{1,0:T(8,128)(2,1)S(1)} %get-tuple-element.102), channel_id=1, source_target_pairs={{0,1},{1,0},{2,3},{3,2},{4,5},{5,4},{6,7},{7,6},{8,9},{9,8},{10,11... | collective-permute-start | bytes 786440 | tf_op jit(solution)/shard_map/ppermute | solution.py:555
  18.0 1.8 %collective-permute-start.4 = (bf16[64,2048]{1,0:T(8,128)(2,1)S(1)}, bf16[64,2048]{1,0:T(8,128)(2,1)S(1)}, u32[]{:S(2)}, u32[]{:S(2)}) collective-permute-start(bf16[64,2048]{1,0:T(8,128)(2,1)S(1)} %get-tuple-element.103), channel_id=1, source_target_pairs={{0,1},{1,0},{2,3},{3,2},{4,5},{5,4},{6,7},{7,6},{8,9},{9,8},{10,11... | collective-permute-start | bytes 786440 | tf_op jit(solution)/shard_map/ppermute | solution.py:555
  18.2 1.9 %collective-permute-start.5 = (bf16[64,2048]{1,0:T(8,128)(2,1)S(1)}, bf16[64,2048]{1,0:T(8,128)(2,1)S(1)}, u32[]{:S(2)}, u32[]{:S(2)}) collective-permute-start(bf16[64,2048]{1,0:T(8,128)(2,1)S(1)} %get-tuple-element.104), channel_id=1, source_target_pairs={{0,1},{1,0},{2,3},{3,2},{4,5},{5,4},{6,7},{7,6},{8,9},{9,8},{10,11... | collective-permute-start | bytes 786440 | tf_op jit(solution)/shard_map/ppermute | solution.py:555
  20.4 14.9 %collective-permute-start.6 = (bf16[128,2048]{1,0:T(8,128)(2,1)S(1)}, bf16[128,2048]{1,0:T(8,128)(2,1)S(1)}, u32[]{:S(2)}, u32[]{:S(2)}) collective-permute-start(bf16[128,2048]{1,0:T(8,128)(2,1)S(1)} %get-tuple-element.113), channel_id=1, source_target_pairs={{0,4},{4,0},{8,12},{12,8},{1,5},{5,1},{9,13},{13,9},{2,6},{6,2},{1... | collective-permute-start | bytes 1572872 | tf_op jit(solution)/shard_map/ppermute | solution.py:537
  22.1 5.3 %collective-permute-start.9 = (s32[1,8]{1,0:T(1,128)S(1)}, s32[1,8]{1,0:T(1,128)S(1)}, u32[]{:S(2)}, u32[]{:S(2)}) collective-permute-start(s32[1,8]{1,0:T(1,128)S(1)} %pad_add_fusion.refs_1_), channel_id=1, source_target_pairs={{0,3},{1,2},{2,1},{3,0},{4,7},{5,6},{6,5},{7,4},{8,11},{9,10},{10,... | collective-permute-start | bytes 104 | tf_op jit(solution)/shard_map/ppermute | solution.py:555
  22.4 5.3 %collective-permute-start.8 = (s32[1,8]{1,0:T(1,128)S(1)}, s32[1,8]{1,0:T(1,128)S(1)}, u32[]{:S(2)}, u32[]{:S(2)}) collective-permute-start(s32[1,8]{1,0:T(1,128)S(1)} %pad_add_fusion.refs_1_), channel_id=1, source_target_pairs={{0,2},{1,3},{2,0},{3,1},{4,6},{5,7},{6,4},{7,5},{8,10},{9,11},{10,... | collective-permute-start | bytes 104 | tf_op jit(solution)/shard_map/ppermute | solution.py:555
  27.8 1.6 %collective-permute-start.10 = (bf16[64,2048]{1,0:T(8,128)(2,1)S(1)}, bf16[64,2048]{1,0:T(8,128)(2,1)S(1)}, u32[]{:S(2)}, u32[]{:S(2)}) collective-permute-start(bf16[64,2048]{1,0:T(8,128)(2,1)S(1)} %get-tuple-element.119), channel_id=1, source_target_pairs={{0,1},{1,0},{2,3},{3,2},{4,5},{5,4},{6,7},{7,6},{8,9},{9,8},{10,11... | collective-permute-start | bytes 786440 | tf_op jit(solution)/shard_map/ppermute | solution.py:555
  27.9 1.9 %collective-permute-start.11 = (bf16[64,2048]{1,0:T(8,128)(2,1)S(1)}, bf16[64,2048]{1,0:T(8,128)(2,1)S(1)}, u32[]{:S(2)}, u32[]{:S(2)}) collective-permute-start(bf16[64,2048]{1,0:T(8,128)(2,1)S(1)} %get-tuple-element.120), channel_id=1, source_target_pairs={{0,1},{1,0},{2,3},{3,2},{4,5},{5,4},{6,7},{7,6},{8,9},{9,8},{10,11... | collective-permute-start | bytes 786440 | tf_op jit(solution)/shard_map/ppermute | solution.py:555
  28.4 1.8 %collective-permute-start.12 = (bf16[64,2048]{1,0:T(8,128)(2,1)S(1)}, bf16[64,2048]{1,0:T(8,128)(2,1)S(1)}, u32[]{:S(2)}, u32[]{:S(2)}) collective-permute-start(bf16[64,2048]{1,0:T(8,128)(2,1)S(1)} %get-tuple-element.121), channel_id=1, source_target_pairs={{0,1},{1,0},{2,3},{3,2},{4,5},{5,4},{6,7},{7,6},{8,9},{9,8},{10,11... | collective-permute-start | bytes 786440 | tf_op jit(solution)/shard_map/ppermute | solution.py:555
  28.5 2.1 %collective-permute-start.13 = (bf16[64,2048]{1,0:T(8,128)(2,1)S(1)}, bf16[64,2048]{1,0:T(8,128)(2,1)S(1)}, u32[]{:S(2)}, u32[]{:S(2)}) collective-permute-start(bf16[64,2048]{1,0:T(8,128)(2,1)S(1)} %get-tuple-element.122), channel_id=1, source_target_pairs={{0,1},{1,0},{2,3},{3,2},{4,5},{5,4},{6,7},{7,6},{8,9},{9,8},{10,11... | collective-permute-start | bytes 786440 | tf_op jit(solution)/shard_map/ppermute | solution.py:555
  34.2 1.4 %collective-permute-start.14 = (bf16[64,1024]{1,0:T(8,128)(2,1)S(1)}, bf16[64,1024]{1,0:T(8,128)(2,1)S(1)}, u32[]{:S(2)}, u32[]{:S(2)}) collective-permute-start(bf16[64,1024]{1,0:T(8,128)(2,1)S(1)} %get-tuple-element.131), channel_id=1, source_target_pairs={{0,1},{1,0},{2,3},{3,2},{4,5},{5,4},{6,7},{7,6},{8,9},{9,8},{10,11... | collective-permute-start | bytes 393224 | tf_op jit(solution)/shard_map/ppermute | solution.py:555
  34.4 1.4 %collective-permute-start.15 = (bf16[64,1024]{1,0:T(8,128)(2,1)S(1)}, bf16[64,1024]{1,0:T(8,128)(2,1)S(1)}, u32[]{:S(2)}, u32[]{:S(2)}) collective-permute-start(bf16[64,1024]{1,0:T(8,128)(2,1)S(1)} %get-tuple-element.132), channel_id=1, source_target_pairs={{0,1},{1,0},{2,3},{3,2},{4,5},{5,4},{6,7},{7,6},{8,9},{9,8},{10,11... | collective-permute-start | bytes 393224 | tf_op jit(solution)/shard_map/ppermute | solution.py:555
  36.5 8.7 %collective-permute-start.23 = (bf16[128,1024]{1,0:T(8,128)(2,1)S(1)}, bf16[128,1024]{1,0:T(8,128)(2,1)S(1)}, u32[]{:S(2)}, u32[]{:S(2)}) collective-permute-start(bf16[128,1024]{1,0:T(8,128)(2,1)S(1)} %get-tuple-element.161), channel_id=1, source_target_pairs={{0,4},{4,0},{8,12},{12,8},{1,5},{5,1},{9,13},{13,9},{2,6},{6,2},{1... | collective-permute-start | bytes 786440 | tf_op jit(solution)/shard_map/ppermute | solution.py:537
  40.7 1.4 %collective-permute-start.18 = (bf16[64,1024]{1,0:T(8,128)(2,1)S(1)}, bf16[64,1024]{1,0:T(8,128)(2,1)S(1)}, u32[]{:S(2)}, u32[]{:S(2)}) collective-permute-start(bf16[64,1024]{1,0:T(8,128)(2,1)S(1)} %get-tuple-element.144), channel_id=1, source_target_pairs={{0,1},{1,0},{2,3},{3,2},{4,5},{5,4},{6,7},{7,6},{8,9},{9,8},{10,11... | collective-permute-start | bytes 393224 | tf_op jit(solution)/shard_map/ppermute | solution.py:555
  40.8 1.5 %collective-permute-start.19 = (bf16[64,1024]{1,0:T(8,128)(2,1)S(1)}, bf16[64,1024]{1,0:T(8,128)(2,1)S(1)}, u32[]{:S(2)}, u32[]{:S(2)}) collective-permute-start(bf16[64,1024]{1,0:T(8,128)(2,1)S(1)} %get-tuple-element.145), channel_id=1, source_target_pairs={{0,1},{1,0},{2,3},{3,2},{4,5},{5,4},{6,7},{7,6},{8,9},{9,8},{10,11... | collective-permute-start | bytes 393224 | tf_op jit(solution)/shard_map/ppermute | solution.py:555
  41.3 1.5 %collective-permute-start.21 = (bf16[64,1024]{1,0:T(8,128)(2,1)S(1)}, bf16[64,1024]{1,0:T(8,128)(2,1)S(1)}, u32[]{:S(2)}, u32[]{:S(2)}) collective-permute-start(bf16[64,1024]{1,0:T(8,128)(2,1)S(1)} %get-tuple-element.147), channel_id=1, source_target_pairs={{0,1},{1,0},{2,3},{3,2},{4,5},{5,4},{6,7},{7,6},{8,9},{9,8},{10,11... | collective-permute-start | bytes 393224 | tf_op jit(solution)/shard_map/ppermute | solution.py:555
  42.9 9.3 %collective-permute-start.22 = (bf16[128,1024]{1,0:T(8,128)(2,1)S(1)}, bf16[128,1024]{1,0:T(8,128)(2,1)S(1)}, u32[]{:S(2)}, u32[]{:S(2)}) collective-permute-start(bf16[128,1024]{1,0:T(8,128)(2,1)S(1)} %get-tuple-element.156), channel_id=1, source_target_pairs={{0,4},{4,0},{8,12},{12,8},{1,5},{5,1},{9,13},{13,9},{2,6},{6,2},{1... | collective-permute-start | bytes 786440 | tf_op jit(solution)/shard_map/ppermute | solution.py:537
  45.3 8.1 %collective-permute-start.25 = (bf16[128,1024]{1,0:T(8,128)(2,1)S(1)}, bf16[128,1024]{1,0:T(8,128)(2,1)S(1)}, u32[]{:S(2)}, u32[]{:S(2)}) collective-permute-start(bf16[128,1024]{1,0:T(8,128)(2,1)S(1)} %add_convert_fusion.2), channel_id=1, source_target_pairs={{0,2},{1,3},{2,0},{3,1},{4,6},{5,7},{6,4},{7,5},{8,10},{9,11},{10,... | collective-permute-start | bytes 786440 | tf_op jit(solution)/shard_map/ppermute | solution.py:555
  52.4 7.5 %collective-permute-start.24 = (bf16[128,1024]{1,0:T(8,128)(2,1)S(1)}, bf16[128,1024]{1,0:T(8,128)(2,1)S(1)}, u32[]{:S(2)}, u32[]{:S(2)}) collective-permute-start(bf16[128,1024]{1,0:T(8,128)(2,1)S(1)} %add_convert_fusion.1), channel_id=1, source_target_pairs={{0,2},{1,3},{2,0},{3,1},{4,6},{5,7},{6,4},{7,5},{8,10},{9,11},{10,... | collective-permute-start | bytes 786440 | tf_op jit(solution)/shard_map/ppermute | solution.py:555
  53.4 9.2 %collective-permute-start.27 = (bf16[64,1024]{1,0:T(8,128)(2,1)S(1)}, bf16[64,1024]{1,0:T(8,128)(2,1)S(1)}, u32[]{:S(2)}, u32[]{:S(2)}) collective-permute-start(bf16[64,1024]{1,0:T(8,128)(2,1)S(1)} %get-tuple-element.187), channel_id=1, source_target_pairs={{0,8},{4,12},{8,0},{12,4},{1,9},{5,13},{9,1},{13,5},{2,10},{6,14},... | collective-permute-start | bytes 393224 | tf_op jit(solution)/shard_map/ppermute | solution.py:537
  59.9 7.9 %collective-permute-start.26 = (bf16[64,1024]{1,0:T(8,128)(2,1)S(1)}, bf16[64,1024]{1,0:T(8,128)(2,1)S(1)}, u32[]{:S(2)}, u32[]{:S(2)}) collective-permute-start(bf16[64,1024]{1,0:T(8,128)(2,1)S(1)} %get-tuple-element.202), channel_id=1, source_target_pairs={{0,8},{4,12},{8,0},{12,4},{1,9},{5,13},{9,1},{13,5},{2,10},{6,14},... | collective-permute-start | bytes 393224 | tf_op jit(solution)/shard_map/ppermute | solution.py:537
  (5 other events, 10.3 us)

commit v7 on v6

--- a/solution.py
+++ b/solution.py
@@ -152,15 +152,25 @@
         put_quarters(db_refs, spread[half:], cols)
 
 
-def far_body(tensor, steps, rows, start, chunks, *refs):
-    slot_ref, meta_a, meta_b, xa_ref = refs[:4]
-    xb_refs = refs[4:4 + chunks]
-    weight_ref = refs[4 + chunks]
-    da_ref, *db_refs, _, xc_ref, scatter_ref = refs[-4 - QUARTERS:]
+def ready_body(tensor, steps, rows, slot_ref, meta_a, meta_b, xa_ref, *refs):
+    got_ref, picks_ref, scatter_ref = refs[-3:]
     picks, scatter, _ = place_rows(tensor, steps, rows, slot_ref, (meta_a, meta_b))
+    half = steps * rows
     scatter_ref[...] = scatter
+    picks_ref[...] = picks[:, half:]
+    got_ref[...] = jnp.dot(
+        picks[:, :half], xa_ref[...], preferred_element_type=jnp.float32
+    ).astype(jnp.bfloat16)
+
+
+def far_body(start, chunks, *refs):
+    got_ref, picks_ref, scatter_ref = refs[:3]
+    xb_refs = refs[3:3 + chunks]
+    weight_ref = refs[3 + chunks]
+    da_ref, *db_refs, _, xc_ref = refs[-3 - QUARTERS:]
     xb = jnp.concatenate([ref[...] for ref in xb_refs], axis=0)
-    xc_ref[...] = gather_rows(picks, xa_ref[...], xb)
+    more = jnp.dot(picks_ref[...], xb, preferred_element_type=jnp.float32)
+    xc_ref[...] = (got_ref[...].astype(jnp.float32) + more).astype(jnp.bfloat16)
     far_columns(start, xc_ref, scatter_ref, weight_ref, da_ref, db_refs)
 
 
@@ -219,21 +229,37 @@
     )(*in_hbm(slots), *metas, *in_hbm(xa), *in_vmem(xb), *in_hbm(values, scales, base))
 
 
-def far_delta(slots, metas, xa, xb, weights, tensor, start, columns, gates):
+def far_ready(slots, metas, xa, tensor, gates):
     steps = 2
     half, width = xa.shape
     taken = SLOTS * 2 * steps * SEG_MOST
-    kept = [pltpu.VMEM((taken, width), jnp.bfloat16), pltpu.VMEM((2 * half, taken), jnp.bfloat16)]
-    outs = [*sums_shapes(half, columns), FLAG, *kept]
-    return pl.pallas_call(
-        functools.partial(far_body, tensor, steps, half // steps, start, len(xb)),
-        in_specs=[SMEM, SMEM, SMEM] + [VMEM] * (2 + len(xb)) + [HBM] * len(gates),
-        out_specs=[VMEM] * (1 + QUARTERS) + [HBM, VMEM, VMEM],
+    return pl.pallas_call(
+        functools.partial(ready_body, tensor, steps, half // steps),
+        in_specs=[SMEM, SMEM, SMEM, VMEM] + [HBM] * len(gates),
+        out_specs=[VMEM] * 3,
+        out_shape=[
+            pltpu.VMEM((taken, width), jnp.bfloat16),
+            pltpu.VMEM((taken, half), jnp.bfloat16),
+            pltpu.VMEM((2 * half, taken), jnp.bfloat16),
+        ],
+        cost_estimate=LIGHT,
+        compiler_params=pltpu.CompilerParams(vmem_limit_bytes=12 << 20),
+        name="far_ready",
+    )(*in_hbm(slots), *metas, *in_vmem(xa), *in_hbm(*gates))
+
+
+def far_delta(ready, xb, weights, start, columns, gates):
+    got, picks, scatter = ready
+    outs = [*sums_shapes(picks.shape[1], columns), FLAG, pltpu.VMEM(got.shape, jnp.bfloat16)]
+    return pl.pallas_call(
+        functools.partial(far_body, start, len(xb)),
+        in_specs=[VMEM] * (4 + len(xb)) + [HBM] * len(gates),
+        out_specs=[VMEM] * (1 + QUARTERS) + [HBM, VMEM],
         out_shape=outs,
         cost_estimate=LIGHT,
         compiler_params=pltpu.CompilerParams(vmem_limit_bytes=12 << 20),
         name="far_delta",
-    )(*in_hbm(slots), *metas, *in_vmem(xa, *xb, weights), *in_hbm(*gates))
+    )(*in_vmem(got, picks, scatter, *xb, weights), *in_hbm(*gates))
 
 
 def more_delta(gathered, scatter, weights, start, columns, gates):
@@ -591,8 +617,10 @@
         pair = far_metas[mask - 2:mask]
         for start in (0, half):
             if start == 0:
-                mine, *theirs, flag, gathered, spread = far_delta(
-                    tenant_slot, pair, far_rows, far_sibling, weights, tensor, start, half, [flag]
+                ready = far_ready(tenant_slot, pair, far_rows, tensor, [flag])
+                spread = ready[2]
+                mine, *theirs, flag, gathered = far_delta(
+                    ready, far_sibling, weights, start, half, [flag]
                 )
             else:
                 mine, *theirs, flag = more_delta(gathered, spread, weights, start, half, [flag])

time: 70.5 us -> 69.5 us (0.986)
  waiting for transfers between devices: 11.7 us -> 10.6 us
    ppermute x23, waiting for transfers between devices: 7.15 us -> 5.91 us  [swap(): lax.ppermute(value, 'replica', [(i, i ^ mask) for i in range(replicas)])]
    pallas_call x1 -> x2, Pallas kernels: 3.68 us -> 3.84 us  [the longest x1 2.64 us: far_delta(): pl.pallas_call(functools.partial(far_body, start, len(xb)), in_specs=[VME...]
  transfers between devices with their start and end apart: 28 -> 28, of which waited for: 22 -> 20; matrix products, arithmetic and copies ran while one was open for 2% -> 2% of each run, Pallas kernels for 47% -> 48%
where the time goes in v7:
time: 69.5 us; the launch traced here: 69.3 us
  Pallas kernels  35.7 us (51%)
  starting transfers between devices  20.8 us (30%)
  waiting for transfers between devices  10.6 us (15%)
  other arithmetic  1.22 us (2%)
  between operations  0.98 us (1%)
    pallas_call x3, Pallas kernels, attend_cache(): pl.pallas_call(functools.partial(cache_body, start, count), grid=(count /...  12.3 us
    pallas_call x1, Pallas kernels, first_delta(): pl.pallas_call(functools.partial(first_body, tensor, steps, rows), in_spe...  11.7 us
    ppermute x23, starting transfers between devices, swap(): lax.ppermute(value, 'replica', [(i, i ^ mask) for i in range(replicas)])  11.7 us
    ppermute x5, starting transfers between devices, cross(): return lax.ppermute(value, 'tensor', [(i, i ^ mask) for i in range(tensor)])  9.09 us
    ppermute x23, waiting for transfers between devices, swap(): lax.ppermute(value, 'replica', [(i, i ^ mask) for i in range(replicas)])  5.91 us
    ppermute x5, waiting for transfers between devices, cross(): return lax.ppermute(value, 'tensor', [(i, i ^ mask) for i in range(tensor)])  4.69 us
    pallas_call x1, Pallas kernels, far_delta(): pl.pallas_call(functools.partial(far_body, start, len(xb)), in_specs=[VME...  2.64 us
    pallas_call x1, Pallas kernels, weigh_new(): pl.pallas_call(weigh_body, in_specs=[VMEM] * 4, out_specs=[VMEM] * 2, out...  2.54 us
  transfers between devices with their start and end apart: 28, of which 20 were waited for; matrix products, arithmetic and copies ran while one was open for 2% of the time, Pallas kernels for 48%

profile of v7, /device:TPU:0, one launch (start us, length us, event | category | flops | bytes accessed | tf_op | source)
XLA Modules:
  0.0 69.3 jit_solution(5739632987925383452)
XLA Ops:
  0.6 0.5 collective-permute-start.1
  1.1 2.6 %collective-permute-start.7 = (bf16[256,2048]{1,0:T(8,128)(2,1)}, bf16[256,2048]{1,0:T(8,128)(2,1)S(1)}, u32[]{:S(2)}, u32[]{:S(2)}) collective-permute-start(bf16[256,2048]{1,0:T(8,128)(2,1)} %bitcast.13), channel_id=1, source_target_pairs={{0,2},{1,3},{2,0},{3,1},{4,6},{5,7},{6,4},{7,5},{8,10},{9,11},{10,... | collective-permute-start | bytes 3145736 | tf_op jit(solution)/shard_map/ppermute | solution.py:581
  3.7 0.7 %pad_add_fusion.refs_1_ = s32[1,8]{1,0:T(1,128)S(1)} fusion(s32[1,4]{1,0:T(1,128)} %param.16, s32[1,4]{1,0:T(1,128)} %param.15), kind=kLoop, calls=%fused_computation.10 | loop fusion | flops 8 | bytes 64 | tf_op jit(solution)/shard_map/concatenate | solution.py:594
  4.6 1.0 %collective-permute-done.refs_2_ = s32[1,8]{1,0:T(1,128)S(1)} collective-permute-done((s32[1,8]{1,0:T(1,128)S(1)}, s32[1,8]{1,0:T(1,128)S(1)}, u32[]{:S(2)}, u32[]{:S(2)}) %collective-permute-start) | collective-permute-done | bytes 64 | tf_op jit(solution)/shard_map/ppermute | solution.py:581
  5.6 11.7 %first_delta.1 = (bf16[256,2048]{1,0:T(8,128)(2,1)S(1)}, bf16[64,2048]{1,0:T(8,128)(2,1)S(1)}, bf16[64,2048]{1,0:T(8,128)(2,1)S(1)}, bf16[64,2048]{1,0:T(8,128)(...) custom-call(s32[8]{0:T(128)} %slot_ref.1, ...), custom_call_target="tpu_custom_call" | custom-call | flops 1 | bytes 1 | tf_op jit(solution)/shard_map/first_delta/pallas_call | solution.py:212
  18.4 0.5 collective-permute-done.2.refs_0_
  20.3 1.6 %collective-permute-start.6 = (bf16[128,2048]{1,0:T(8,128)(2,1)S(1)}, bf16[128,2048]{1,0:T(8,128)(2,1)S(1)}, u32[]{:S(2)}, u32[]{:S(2)}) collective-permute-start(bf16[128,2048]{1,0:T(8,128)(2,1)S(1)} %get-tuple-element.115), channel_id=1, source_target_pairs={{0,4},{4,0},{8,12},{12,8},{1,5},{5,1},{9,13},{13,9},{2,6},{6,2},{1... | collective-permute-start | bytes 1572872 | tf_op jit(solution)/shard_map/ppermute | solution.py:563
  22.3 1.2 %collective-permute-start.8 = (s32[1,8]{1,0:T(1,128)S(1)}, s32[1,8]{1,0:T(1,128)S(1)}, u32[]{:S(2)}, u32[]{:S(2)}) collective-permute-start(s32[1,8]{1,0:T(1,128)S(1)} %pad_add_fusion.refs_1_), channel_id=1, source_target_pairs={{0,2},{1,3},{2,0},{3,1},{4,6},{5,7},{6,4},{7,5},{8,10},{9,11},{10,... | collective-permute-start | bytes 104 | tf_op jit(solution)/shard_map/ppermute | solution.py:581
  23.5 3.5 %attend_cache.3 = (f32[32,128,128]{2,1,0:T(8,128)S(1)}, f32[32,1,128]{2,1,0:T(1,128)S(1)}, bf16[32,128,128]{2,1,0:T(8,128)(2,1)S(1)}, f32[8,128]{1,0:T(8,128)}) custom-call(s32[32]{0:T(128)S(1)} %copy-done, bf16[2,32,8192]{2,1,0:T(8,128)(2,1)} %q_ref.5, bf16[32,128,2048]{2,1,0:T(8,128)(2,1)} %kv_ref.5, f32[8,128]{1,0:T(8,128)} %marker.3.refs_0_), custom_call_target="tpu_custom_call" | custom-call | flops 1 | bytes 1 | tf_op jit(solution)/shard_map/attend_cache/pallas_call | solution.py:381
  27.9 0.5 collective-permute-start.11
  28.9 1.2 %far_ready.1 = (bf16[320,2048]{1,0:T(8,128)(2,1)S(1)}, bf16[320,256]{1,0:T(8,128)(2,1)S(1)}, bf16[512,320]{1,0:T(8,128)(2,1)S(1)}) custom-call(s32[8]{0:T(128)} %slot_ref.1, s32[1,8]{1,0:T(1,128)S(1)} %collective-permute-done.8.meta_a, s32[1,8]{1,0:T(1,128)S(1)} %collective-permute-done.9.meta_b, ...), custom_call_target="tpu_custom_call" | custom-call | flops 1 | bytes 1 | tf_op jit(solution)/shard_map/far_ready/pallas_call | solution.py:236
  30.6 2.6 %far_delta.1 = (bf16[256,1024]{1,0:T(8,128)(2,1)S(1)}, bf16[64,1024]{1,0:T(8,128)(2,1)S(1)}, bf16[64,1024]{1,0:T(8,128)(2,1)S(1)}, bf16[64,1024]{1,0:T(8,128)(2,...) custom-call(bf16[320,2048]{1,0:T(8,128)(2,1)S(1)} %get-tuple-element.122.refs_0_, ...), custom_call_target="tpu_custom_call" | custom-call | flops 1 | bytes 1 | tf_op jit(solution)/shard_map/far_delta/pallas_call | solution.py:254
  35.4 1.9 %collective-permute-start.23 = (bf16[128,1024]{1,0:T(8,128)(2,1)S(1)}, bf16[128,1024]{1,0:T(8,128)(2,1)S(1)}, u32[]{:S(2)}, u32[]{:S(2)}) collective-permute-start(bf16[128,1024]{1,0:T(8,128)(2,1)S(1)} %get-tuple-element.165), channel_id=1, source_target_pairs={{0,4},{4,0},{8,12},{12,8},{1,5},{5,1},{9,13},{13,9},{2,6},{6,2},{1... | collective-permute-start | bytes 786440 | tf_op jit(solution)/shard_map/ppermute | solution.py:563
  37.3 2.3 %more_delta.1 = (bf16[256,1024]{1,0:T(8,128)(2,1)S(1)}, bf16[64,1024]{1,0:T(8,128)(2,1)S(1)}, bf16[64,1024]{1,0:T(8,128)(2,1)S(1)}, bf16[64,1024]{1,0:T(8,128)(2...) custom-call(bf16[320,2048]{1,0:T(8,128)(2,1)S(1)} %get-tuple-element.133.xc_ref, ...), custom_call_target="tpu_custom_call" | custom-call | flops 1 | bytes 1 | tf_op jit(solution)/shard_map/more_delta/pallas_call | solution.py:267
  42.1 2.0 %collective-permute-done.23 = bf16[128,1024]{1,0:T(8,128)(2,1)S(1)} collective-permute-done((bf16[128,1024]{1,0:T(8,128)(2,1)S(1)}, bf16[128,1024]{1,0:T(8,128)(2,1)S(1)}, u32[]{:S(2)}, u32[]{:S(2)}) %collective-permute-start.23) | collective-permute-done | bytes 262176 | tf_op jit(solution)/shard_map/ppermute | solution.py:563
  44.2 1.7 %collective-permute-start.25 = (bf16[128,1024]{1,0:T(8,128)(2,1)S(1)}, bf16[128,1024]{1,0:T(8,128)(2,1)S(1)}, u32[]{:S(2)}, u32[]{:S(2)}) collective-permute-start(bf16[128,1024]{1,0:T(8,128)(2,1)S(1)} %add_convert_fusion.2), channel_id=1, source_target_pairs={{0,2},{1,3},{2,0},{3,1},{4,6},{5,7},{6,4},{7,5},{8,10},{9,11},{10,... | collective-permute-start | bytes 786440 | tf_op jit(solution)/shard_map/ppermute | solution.py:581
  45.9 5.3 %attend_cache.4 = (f32[32,128,128]{2,1,0:T(8,128)S(1)}, f32[32,1,128]{2,1,0:T(1,128)S(1)}, bf16[32,128,128]{2,1,0:T(8,128)(2,1)S(1)}, f32[8,128]{1,0:T(8,128)}) custom-call(s32[32]{0:T(128)S(1)} %copy-done, bf16[2,32,8192]{2,1,0:T(8,128)(2,1)} %q_ref.5, bf16[32,128,2048]{2,1,0:T(8,128)(2,1)} %kv_ref.5, ...), custom_call_target="tpu_custom_call", output_to_operand_aliasing={{0}: (3, {}), {1}: (4, {}), {2}: (5, {})} | custom-call | flops 1 | bytes 1 | tf_op jit(solution)/shard_map/attend_cache/pallas_call | solution.py:381
  51.3 0.8 %collective-permute-start.24 = (bf16[128,1024]{1,0:T(8,128)(2,1)S(1)}, bf16[128,1024]{1,0:T(8,128)(2,1)S(1)}, u32[]{:S(2)}, u32[]{:S(2)}) collective-permute-start(bf16[128,1024]{1,0:T(8,128)(2,1)S(1)} %add_convert_fusion.1), channel_id=1, source_target_pairs={{0,2},{1,3},{2,0},{3,1},{4,6},{5,7},{6,4},{7,5},{8,10},{9,11},{10,... | collective-permute-start | bytes 786440 | tf_op jit(solution)/shard_map/ppermute | solution.py:581
  52.4 2.6 %collective-permute-start.27 = (bf16[64,1024]{1,0:T(8,128)(2,1)S(1)}, bf16[64,1024]{1,0:T(8,128)(2,1)S(1)}, u32[]{:S(2)}, u32[]{:S(2)}) collective-permute-start(bf16[64,1024]{1,0:T(8,128)(2,1)S(1)} %get-tuple-element.191), channel_id=1, source_target_pairs={{0,8},{4,12},{8,0},{12,4},{1,9},{5,13},{9,1},{13,5},{2,10},{6,14},... | collective-permute-start | bytes 393224 | tf_op jit(solution)/shard_map/ppermute | solution.py:563
  55.0 3.5 %attend_cache.5 = (f32[32,128,128]{2,1,0:T(8,128)S(1)}, f32[32,1,128]{2,1,0:T(1,128)S(1)}, bf16[32,128,128]{2,1,0:T(8,128)(2,1)S(1)}, f32[8,128]{1,0:T(8,128)}) custom-call(s32[32]{0:T(128)S(1)} %copy-done, bf16[2,32,8192]{2,1,0:T(8,128)(2,1)} %q_ref.5, bf16[32,128,2048]{2,1,0:T(8,128)(2,1)} %kv_ref.5, ...), custom_call_target="tpu_custom_call", output_to_operand_aliasing={{0}: (3, {}), {1}: (4, {}), {2}: (5, {})} | custom-call | flops 1 | bytes 1 | tf_op jit(solution)/shard_map/attend_cache/pallas_call | solution.py:381
  58.9 2.7 %collective-permute-start.26 = (bf16[64,1024]{1,0:T(8,128)(2,1)S(1)}, bf16[64,1024]{1,0:T(8,128)(2,1)S(1)}, u32[]{:S(2)}, u32[]{:S(2)}) collective-permute-start(bf16[64,1024]{1,0:T(8,128)(2,1)S(1)} %get-tuple-element.206), channel_id=1, source_target_pairs={{0,8},{4,12},{8,0},{12,4},{1,9},{5,13},{9,1},{13,5},{2,10},{6,14},... | collective-permute-start | bytes 393224 | tf_op jit(solution)/shard_map/ppermute | solution.py:563
  61.7 2.5 %weigh_new.1 = (f32[3,32,128]{2,1,0:T(8,128)S(1)}, f32[2,32,8192]{2,1,0:T(8,128)S(1)}) custom-call(f32[32,1,128]{2,1,0:T(1,128)S(1)} %get-tuple-element.189.lse_ref, bf16[32,128,128]{2,1,0:T(8,128)(2,1)S(1)} %get-tuple-element.190.turned_ref, f32[2,32,8,128]{3,2,1,0:T(8,128)S(1)} %bitcast.9, f32[4096,128]{1,0:T(8,128)S(1)} %bitcast.8), custom_call_target="tpu_custom_call" | custom-call | flops 1 | bytes 1 | tf_op jit(solution)/shard_map/weigh_new/pallas_call | solution.py:454
  64.2 2.6 %collective-permute-done.26 = bf16[64,1024]{1,0:T(8,128)(2,1)S(1)} collective-permute-done((bf16[64,1024]{1,0:T(8,128)(2,1)S(1)}, bf16[64,1024]{1,0:T(8,128)(2,1)S(1)}, u32[]{:S(2)}, u32[]{:S(2)}) %collective-permute-start.26) | collective-permute-done | bytes 131104 | tf_op jit(solution)/shard_map/ppermute | solution.py:563
  66.8 2.4 %add_new.1 = (bf16[2,32,8192]{2,1,0:T(8,128)(2,1)}, bf16[2,32,2048]{2,1,0:T(8,128)(2,1)}) custom-call(f32[3,32,128]{2,1,0:T(8,128)S(1)} %get-tuple-element.196.share_ref, f32[2,32,8192]{2,1,0:T(8,128)S(1)} %get-tuple-element.197.early_ref, bf16[2,32,1024]{2,1,0:T(8,128)(2,1)S(1)} %bitcast.10, bf16[2,32,1024]{2,1,0:T(8,128)(2,1)S(1)} %bitcast.11), custom_call_target="tpu_custom_call" | custom-call | flops 1 | bytes 1 | tf_op jit(solution)/shard_map/add_new/pallas_call | solution.py:511
  (60 shorter events, 10.3 us)
Async XLA Ops:
  0.6 5.0 %collective-permute-start.1 = (bf16[256,2048]{1,0:T(8,128)(2,1)}, bf16[256,2048]{1,0:T(8,128)(2,1)S(1)}, u32[]{:S(2)}, u32[]{:S(2)}) collective-permute-start(bf16[256,2048]{1,0:T(8,128)(2,1)} %bitcast.12), channel_id=1, source_target_pairs={{0,1},{1,0},{2,3},{3,2},{4,5},{5,4},{6,7},{7,6},{8,9},{9,8},{10,11... | collective-permute-start | bytes 3145736 | tf_op jit(solution)/shard_map/ppermute | solution.py:581
  1.1 26.6 %collective-permute-start.7 = (bf16[256,2048]{1,0:T(8,128)(2,1)}, bf16[256,2048]{1,0:T(8,128)(2,1)S(1)}, u32[]{:S(2)}, u32[]{:S(2)}) collective-permute-start(bf16[256,2048]{1,0:T(8,128)(2,1)} %bitcast.13), channel_id=1, source_target_pairs={{0,2},{1,3},{2,0},{3,1},{4,6},{5,7},{6,4},{7,5},{8,10},{9,11},{10,... | collective-permute-start | bytes 3145736 | tf_op jit(solution)/shard_map/ppermute | solution.py:581
  17.3 1.6 %collective-permute-start.2 = (bf16[64,2048]{1,0:T(8,128)(2,1)S(1)}, bf16[64,2048]{1,0:T(8,128)(2,1)S(1)}, u32[]{:S(2)}, u32[]{:S(2)}) collective-permute-start(bf16[64,2048]{1,0:T(8,128)(2,1)S(1)} %get-tuple-element.103), channel_id=1, source_target_pairs={{0,1},{1,0},{2,3},{3,2},{4,5},{5,4},{6,7},{7,6},{8,9},{9,8},{10,11... | collective-permute-start | bytes 786440 | tf_op jit(solution)/shard_map/ppermute | solution.py:581
  17.6 1.7 %collective-permute-start.3 = (bf16[64,2048]{1,0:T(8,128)(2,1)S(1)}, bf16[64,2048]{1,0:T(8,128)(2,1)S(1)}, u32[]{:S(2)}, u32[]{:S(2)}) collective-permute-start(bf16[64,2048]{1,0:T(8,128)(2,1)S(1)} %get-tuple-element.104), channel_id=1, source_target_pairs={{0,1},{1,0},{2,3},{3,2},{4,5},{5,4},{6,7},{7,6},{8,9},{9,8},{10,11... | collective-permute-start | bytes 786440 | tf_op jit(solution)/shard_map/ppermute | solution.py:581
  17.9 1.8 %collective-permute-start.4 = (bf16[64,2048]{1,0:T(8,128)(2,1)S(1)}, bf16[64,2048]{1,0:T(8,128)(2,1)S(1)}, u32[]{:S(2)}, u32[]{:S(2)}) collective-permute-start(bf16[64,2048]{1,0:T(8,128)(2,1)S(1)} %get-tuple-element.105), channel_id=1, source_target_pairs={{0,1},{1,0},{2,3},{3,2},{4,5},{5,4},{6,7},{7,6},{8,9},{9,8},{10,11... | collective-permute-start | bytes 786440 | tf_op jit(solution)/shard_map/ppermute | solution.py:581
  18.1 1.9 %collective-permute-start.5 = (bf16[64,2048]{1,0:T(8,128)(2,1)S(1)}, bf16[64,2048]{1,0:T(8,128)(2,1)S(1)}, u32[]{:S(2)}, u32[]{:S(2)}) collective-permute-start(bf16[64,2048]{1,0:T(8,128)(2,1)S(1)} %get-tuple-element.106), channel_id=1, source_target_pairs={{0,1},{1,0},{2,3},{3,2},{4,5},{5,4},{6,7},{7,6},{8,9},{9,8},{10,11... | collective-permute-start | bytes 786440 | tf_op jit(solution)/shard_map/ppermute | solution.py:581
  20.3 14.1 %collective-permute-start.6 = (bf16[128,2048]{1,0:T(8,128)(2,1)S(1)}, bf16[128,2048]{1,0:T(8,128)(2,1)S(1)}, u32[]{:S(2)}, u32[]{:S(2)}) collective-permute-start(bf16[128,2048]{1,0:T(8,128)(2,1)S(1)} %get-tuple-element.115), channel_id=1, source_target_pairs={{0,4},{4,0},{8,12},{12,8},{1,5},{5,1},{9,13},{13,9},{2,6},{6,2},{1... | collective-permute-start | bytes 1572872 | tf_op jit(solution)/shard_map/ppermute | solution.py:563
  21.9 5.5 %collective-permute-start.9 = (s32[1,8]{1,0:T(1,128)S(1)}, s32[1,8]{1,0:T(1,128)S(1)}, u32[]{:S(2)}, u32[]{:S(2)}) collective-permute-start(s32[1,8]{1,0:T(1,128)S(1)} %pad_add_fusion.refs_1_), channel_id=1, source_target_pairs={{0,3},{1,2},{2,1},{3,0},{4,7},{5,6},{6,5},{7,4},{8,11},{9,10},{10,... | collective-permute-start | bytes 104 | tf_op jit(solution)/shard_map/ppermute | solution.py:581
  22.3 5.4 %collective-permute-start.8 = (s32[1,8]{1,0:T(1,128)S(1)}, s32[1,8]{1,0:T(1,128)S(1)}, u32[]{:S(2)}, u32[]{:S(2)}) collective-permute-start(s32[1,8]{1,0:T(1,128)S(1)} %pad_add_fusion.refs_1_), channel_id=1, source_target_pairs={{0,2},{1,3},{2,0},{3,1},{4,6},{5,7},{6,4},{7,5},{8,10},{9,11},{10,... | collective-permute-start | bytes 104 | tf_op jit(solution)/shard_map/ppermute | solution.py:581
  27.8 2.3 %collective-permute-start.10 = (bf16[64,2048]{1,0:T(8,128)(2,1)S(1)}, bf16[64,2048]{1,0:T(8,128)(2,1)S(1)}, u32[]{:S(2)}, u32[]{:S(2)}) collective-permute-start(bf16[64,2048]{1,0:T(8,128)(2,1)S(1)} %get-tuple-element.125), channel_id=1, source_target_pairs={{0,1},{1,0},{2,3},{3,2},{4,5},{5,4},{6,7},{7,6},{8,9},{9,8},{10,11... | collective-permute-start | bytes 786440 | tf_op jit(solution)/shard_map/ppermute | solution.py:581
  27.9 2.2 %collective-permute-start.11 = (bf16[64,2048]{1,0:T(8,128)(2,1)S(1)}, bf16[64,2048]{1,0:T(8,128)(2,1)S(1)}, u32[]{:S(2)}, u32[]{:S(2)}) collective-permute-start(bf16[64,2048]{1,0:T(8,128)(2,1)S(1)} %get-tuple-element.126), channel_id=1, source_target_pairs={{0,1},{1,0},{2,3},{3,2},{4,5},{5,4},{6,7},{7,6},{8,9},{9,8},{10,11... | collective-permute-start | bytes 786440 | tf_op jit(solution)/shard_map/ppermute | solution.py:581
  28.4 1.8 %collective-permute-start.12 = (bf16[64,2048]{1,0:T(8,128)(2,1)S(1)}, bf16[64,2048]{1,0:T(8,128)(2,1)S(1)}, u32[]{:S(2)}, u32[]{:S(2)}) collective-permute-start(bf16[64,2048]{1,0:T(8,128)(2,1)S(1)} %get-tuple-element.127), channel_id=1, source_target_pairs={{0,1},{1,0},{2,3},{3,2},{4,5},{5,4},{6,7},{7,6},{8,9},{9,8},{10,11... | collective-permute-start | bytes 786440 | tf_op jit(solution)/shard_map/ppermute | solution.py:581
  28.5 2.1 %collective-permute-start.13 = (bf16[64,2048]{1,0:T(8,128)(2,1)S(1)}, bf16[64,2048]{1,0:T(8,128)(2,1)S(1)}, u32[]{:S(2)}, u32[]{:S(2)}) collective-permute-start(bf16[64,2048]{1,0:T(8,128)(2,1)S(1)} %get-tuple-element.128), channel_id=1, source_target_pairs={{0,1},{1,0},{2,3},{3,2},{4,5},{5,4},{6,7},{7,6},{8,9},{9,8},{10,11... | collective-permute-start | bytes 786440 | tf_op jit(solution)/shard_map/ppermute | solution.py:581
  33.2 1.4 %collective-permute-start.14 = (bf16[64,1024]{1,0:T(8,128)(2,1)S(1)}, bf16[64,1024]{1,0:T(8,128)(2,1)S(1)}, u32[]{:S(2)}, u32[]{:S(2)}) collective-permute-start(bf16[64,1024]{1,0:T(8,128)(2,1)S(1)} %get-tuple-element.135), channel_id=1, source_target_pairs={{0,1},{1,0},{2,3},{3,2},{4,5},{5,4},{6,7},{7,6},{8,9},{9,8},{10,11... | collective-permute-start | bytes 393224 | tf_op jit(solution)/shard_map/ppermute | solution.py:581
  33.4 1.4 %collective-permute-start.15 = (bf16[64,1024]{1,0:T(8,128)(2,1)S(1)}, bf16[64,1024]{1,0:T(8,128)(2,1)S(1)}, u32[]{:S(2)}, u32[]{:S(2)}) collective-permute-start(bf16[64,1024]{1,0:T(8,128)(2,1)S(1)} %get-tuple-element.136), channel_id=1, source_target_pairs={{0,1},{1,0},{2,3},{3,2},{4,5},{5,4},{6,7},{7,6},{8,9},{9,8},{10,11... | collective-permute-start | bytes 393224 | tf_op jit(solution)/shard_map/ppermute | solution.py:581
  35.4 8.7 %collective-permute-start.23 = (bf16[128,1024]{1,0:T(8,128)(2,1)S(1)}, bf16[128,1024]{1,0:T(8,128)(2,1)S(1)}, u32[]{:S(2)}, u32[]{:S(2)}) collective-permute-start(bf16[128,1024]{1,0:T(8,128)(2,1)S(1)} %get-tuple-element.165), channel_id=1, source_target_pairs={{0,4},{4,0},{8,12},{12,8},{1,5},{5,1},{9,13},{13,9},{2,6},{6,2},{1... | collective-permute-start | bytes 786440 | tf_op jit(solution)/shard_map/ppermute | solution.py:563
  39.6 1.4 %collective-permute-start.18 = (bf16[64,1024]{1,0:T(8,128)(2,1)S(1)}, bf16[64,1024]{1,0:T(8,128)(2,1)S(1)}, u32[]{:S(2)}, u32[]{:S(2)}) collective-permute-start(bf16[64,1024]{1,0:T(8,128)(2,1)S(1)} %get-tuple-element.148), channel_id=1, source_target_pairs={{0,1},{1,0},{2,3},{3,2},{4,5},{5,4},{6,7},{7,6},{8,9},{9,8},{10,11... | collective-permute-start | bytes 393224 | tf_op jit(solution)/shard_map/ppermute | solution.py:581
  39.8 1.5 %collective-permute-start.19 = (bf16[64,1024]{1,0:T(8,128)(2,1)S(1)}, bf16[64,1024]{1,0:T(8,128)(2,1)S(1)}, u32[]{:S(2)}, u32[]{:S(2)}) collective-permute-start(bf16[64,1024]{1,0:T(8,128)(2,1)S(1)} %get-tuple-element.149), channel_id=1, source_target_pairs={{0,1},{1,0},{2,3},{3,2},{4,5},{5,4},{6,7},{7,6},{8,9},{9,8},{10,11... | collective-permute-start | bytes 393224 | tf_op jit(solution)/shard_map/ppermute | solution.py:581
  40.3 1.5 %collective-permute-start.21 = (bf16[64,1024]{1,0:T(8,128)(2,1)S(1)}, bf16[64,1024]{1,0:T(8,128)(2,1)S(1)}, u32[]{:S(2)}, u32[]{:S(2)}) collective-permute-start(bf16[64,1024]{1,0:T(8,128)(2,1)S(1)} %get-tuple-element.151), channel_id=1, source_target_pairs={{0,1},{1,0},{2,3},{3,2},{4,5},{5,4},{6,7},{7,6},{8,9},{9,8},{10,11... | collective-permute-start | bytes 393224 | tf_op jit(solution)/shard_map/ppermute | solution.py:581
  41.9 9.3 %collective-permute-start.22 = (bf16[128,1024]{1,0:T(8,128)(2,1)S(1)}, bf16[128,1024]{1,0:T(8,128)(2,1)S(1)}, u32[]{:S(2)}, u32[]{:S(2)}) collective-permute-start(bf16[128,1024]{1,0:T(8,128)(2,1)S(1)} %get-tuple-element.160), channel_id=1, source_target_pairs={{0,4},{4,0},{8,12},{12,8},{1,5},{5,1},{9,13},{13,9},{2,6},{6,2},{1... | collective-permute-start | bytes 786440 | tf_op jit(solution)/shard_map/ppermute | solution.py:563
  44.2 8.1 %collective-permute-start.25 = (bf16[128,1024]{1,0:T(8,128)(2,1)S(1)}, bf16[128,1024]{1,0:T(8,128)(2,1)S(1)}, u32[]{:S(2)}, u32[]{:S(2)}) collective-permute-start(bf16[128,1024]{1,0:T(8,128)(2,1)S(1)} %add_convert_fusion.2), channel_id=1, source_target_pairs={{0,2},{1,3},{2,0},{3,1},{4,6},{5,7},{6,4},{7,5},{8,10},{9,11},{10,... | collective-permute-start | bytes 786440 | tf_op jit(solution)/shard_map/ppermute | solution.py:581
  51.3 7.5 %collective-permute-start.24 = (bf16[128,1024]{1,0:T(8,128)(2,1)S(1)}, bf16[128,1024]{1,0:T(8,128)(2,1)S(1)}, u32[]{:S(2)}, u32[]{:S(2)}) collective-permute-start(bf16[128,1024]{1,0:T(8,128)(2,1)S(1)} %add_convert_fusion.1), channel_id=1, source_target_pairs={{0,2},{1,3},{2,0},{3,1},{4,6},{5,7},{6,4},{7,5},{8,10},{9,11},{10,... | collective-permute-start | bytes 786440 | tf_op jit(solution)/shard_map/ppermute | solution.py:581
  52.4 9.2 %collective-permute-start.27 = (bf16[64,1024]{1,0:T(8,128)(2,1)S(1)}, bf16[64,1024]{1,0:T(8,128)(2,1)S(1)}, u32[]{:S(2)}, u32[]{:S(2)}) collective-permute-start(bf16[64,1024]{1,0:T(8,128)(2,1)S(1)} %get-tuple-element.191), channel_id=1, source_target_pairs={{0,8},{4,12},{8,0},{12,4},{1,9},{5,13},{9,1},{13,5},{2,10},{6,14},... | collective-permute-start | bytes 393224 | tf_op jit(solution)/shard_map/ppermute | solution.py:563
  58.9 7.9 %collective-permute-start.26 = (bf16[64,1024]{1,0:T(8,128)(2,1)S(1)}, bf16[64,1024]{1,0:T(8,128)(2,1)S(1)}, u32[]{:S(2)}, u32[]{:S(2)}) collective-permute-start(bf16[64,1024]{1,0:T(8,128)(2,1)S(1)} %get-tuple-element.206), channel_id=1, source_target_pairs={{0,8},{4,12},{8,0},{12,4},{1,9},{5,13},{9,1},{13,5},{2,10},{6,14},... | collective-permute-start | bytes 393224 | tf_op jit(solution)/shard_map/ppermute | solution.py:563
  (5 other events, 10.3 us)

commit v8 on v7

--- a/solution.py
+++ b/solution.py
@@ -319,10 +319,10 @@
     )(*in_vmem(value))
 
 
-def cache_body(start, count, len_ref, q_ref, kv_ref, *refs):
+def cache_body(start, count, len_ref, q_ref, key_ref, val_ref, *refs):
     o_ref, lse_ref, turned_ref, _, sorted_ref = refs[-5:]
     block = o_ref.shape[0]
-    cached = kv_ref.shape[1]
+    cached = key_ref.shape[1]
     some = 4 * GROUP
     scale = 1.0 / math.sqrt(HD)
 
@@ -351,7 +351,7 @@
         wide = jnp.concatenate(
             [jnp.where(heads == k, turned, jnp.zeros_like(turned)) for k in range(KVH)], axis=0
         )
-        scores = scale * jnp.dot(kv_ref[r, :, :KEYS], wide, preferred_element_type=jnp.float32)
+        scores = scale * jnp.dot(key_ref[r], wide, preferred_element_type=jnp.float32)
         length = len_ref[start + pl.program_id(0) * block + r]
         scores = jnp.where(position < length, scores, NEG)
         top = jnp.max(scores, axis=0, keepdims=True)
@@ -364,7 +364,7 @@
         for p in range(KVH // 2):
             out = jnp.dot(
                 probs[r][p * some:(p + 1) * some],
-                kv_ref[r, :, KEYS + p * 2 * HD:KEYS + (p + 1) * 2 * HD],
+                val_ref[r, :, p * 2 * HD:(p + 1) * 2 * HD],
                 preferred_element_type=jnp.float32,
             )
             parts.append(jnp.where(first, out[:, :HD], out[:, HD:]))
@@ -384,7 +384,8 @@
         in_specs=[
             pl.BlockSpec(memory_space=pltpu.SMEM),
             pl.BlockSpec((2, together, queries.shape[2]), lambda i: (0, start // together, 0)),
-            pl.BlockSpec((block, cached, width), lambda i: (i + skip, 0, 0)),
+            pl.BlockSpec((block, cached, width // 2), lambda i: (i + skip, 0, 0)),
+            pl.BlockSpec((block, cached, width // 2), lambda i: (i + skip, 0, 1)),
             *[in_place for _ in (*before, *gates)],
         ],
         out_specs=(
@@ -400,11 +401,11 @@
             FLAG,
         ),
         scratch_shapes=[pltpu.VMEM((count * 2 * HEADS, HD), jnp.float32)],
-        input_output_aliases={3 + i: i for i in range(len(before))},
+        input_output_aliases={4 + i: i for i in range(len(before))},
         cost_estimate=cost,
         compiler_params=pltpu.CompilerParams(vmem_limit_bytes=22 << 20),
         name="attend_cache",
-    )(lengths, *in_hbm(queries, kv_cache), *in_vmem(*before), *in_hbm(*gates))
+    )(lengths, *in_hbm(queries, kv_cache, kv_cache), *in_vmem(*before), *in_hbm(*gates))
 
 
 def weigh_body(lse_ref, turned_ref, keys_ref, o_ref, share_ref, early_ref):

time: 69.5 us -> 69.5 us (level)
  no operation moved by 1% of the time
where the time goes in v8:
time: 69.5 us; the launch traced here: 69.3 us
  Pallas kernels  35.7 us (51%)
  starting transfers between devices  20.8 us (30%)
  waiting for transfers between devices  10.6 us (15%)
  other arithmetic  1.22 us (2%)
  between operations  0.98 us (1%)
    pallas_call x3, Pallas kernels, attend_cache(): pl.pallas_call(functools.partial(cache_body, start, count), grid=(count /...  12.4 us
    pallas_call x1, Pallas kernels, first_delta(): pl.pallas_call(functools.partial(first_body, tensor, steps, rows), in_spe...  11.7 us
    ppermute x23, starting transfers between devices, swap(): lax.ppermute(value, 'replica', [(i, i ^ mask) for i in range(replicas)])  11.7 us
    ppermute x5, starting transfers between devices, cross(): return lax.ppermute(value, 'tensor', [(i, i ^ mask) for i in range(tensor)])  9.09 us
    ppermute x23, waiting for transfers between devices, swap(): lax.ppermute(value, 'replica', [(i, i ^ mask) for i in range(replicas)])  5.91 us
    ppermute x5, waiting for transfers between devices, cross(): return lax.ppermute(value, 'tensor', [(i, i ^ mask) for i in range(tensor)])  4.69 us
    pallas_call x1, Pallas kernels, far_delta(): pl.pallas_call(functools.partial(far_body, start, len(xb)), in_specs=[VME...  2.64 us
    pallas_call x1, Pallas kernels, weigh_new(): pl.pallas_call(weigh_body, in_specs=[VMEM] * 4, out_specs=[VMEM] * 2, out...  2.54 us
  transfers between devices with their start and end apart: 28, of which 20 were waited for; matrix products, arithmetic and copies ran while one was open for 2% of the time, Pallas kernels for 48%

profile of v8, /device:TPU:0, one launch (start us, length us, event | category | flops | bytes accessed | tf_op | source)
XLA Modules:
  0.0 69.3 jit_solution(16691928192064562292)
XLA Ops:
  0.6 0.5 collective-permute-start.1
  1.1 2.6 %collective-permute-start.7 = (bf16[256,2048]{1,0:T(8,128)(2,1)}, bf16[256,2048]{1,0:T(8,128)(2,1)S(1)}, u32[]{:S(2)}, u32[]{:S(2)}) collective-permute-start(bf16[256,2048]{1,0:T(8,128)(2,1)} %bitcast.13), channel_id=1, source_target_pairs={{0,2},{1,3},{2,0},{3,1},{4,6},{5,7},{6,4},{7,5},{8,10},{9,11},{10,... | collective-permute-start | bytes 3145736 | tf_op jit(solution)/shard_map/ppermute | solution.py:582
  3.7 0.7 %pad_add_fusion.refs_1_ = s32[1,8]{1,0:T(1,128)S(1)} fusion(s32[1,4]{1,0:T(1,128)} %param.16, s32[1,4]{1,0:T(1,128)} %param.15), kind=kLoop, calls=%fused_computation.10 | loop fusion | flops 8 | bytes 64 | tf_op jit(solution)/shard_map/concatenate | solution.py:595
  4.6 1.0 %collective-permute-done.refs_2_ = s32[1,8]{1,0:T(1,128)S(1)} collective-permute-done((s32[1,8]{1,0:T(1,128)S(1)}, s32[1,8]{1,0:T(1,128)S(1)}, u32[]{:S(2)}, u32[]{:S(2)}) %collective-permute-start) | collective-permute-done | bytes 64 | tf_op jit(solution)/shard_map/ppermute | solution.py:582
  5.6 11.7 %first_delta.1 = (bf16[256,2048]{1,0:T(8,128)(2,1)S(1)}, bf16[64,2048]{1,0:T(8,128)(2,1)S(1)}, bf16[64,2048]{1,0:T(8,128)(2,1)S(1)}, bf16[64,2048]{1,0:T(8,128)(...) custom-call(s32[8]{0:T(128)} %slot_ref.1, ...), custom_call_target="tpu_custom_call" | custom-call | flops 1 | bytes 1 | tf_op jit(solution)/shard_map/first_delta/pallas_call | solution.py:212
  18.4 0.5 collective-permute-done.2.refs_0_
  20.3 1.6 %collective-permute-start.6 = (bf16[128,2048]{1,0:T(8,128)(2,1)S(1)}, bf16[128,2048]{1,0:T(8,128)(2,1)S(1)}, u32[]{:S(2)}, u32[]{:S(2)}) collective-permute-start(bf16[128,2048]{1,0:T(8,128)(2,1)S(1)} %get-tuple-element.115), channel_id=1, source_target_pairs={{0,4},{4,0},{8,12},{12,8},{1,5},{5,1},{9,13},{13,9},{2,6},{6,2},{1... | collective-permute-start | bytes 1572872 | tf_op jit(solution)/shard_map/ppermute | solution.py:564
  22.3 1.2 %collective-permute-start.8 = (s32[1,8]{1,0:T(1,128)S(1)}, s32[1,8]{1,0:T(1,128)S(1)}, u32[]{:S(2)}, u32[]{:S(2)}) collective-permute-start(s32[1,8]{1,0:T(1,128)S(1)} %pad_add_fusion.refs_1_), channel_id=1, source_target_pairs={{0,2},{1,3},{2,0},{3,1},{4,6},{5,7},{6,4},{7,5},{8,10},{9,11},{10,... | collective-permute-start | bytes 104 | tf_op jit(solution)/shard_map/ppermute | solution.py:582
  23.5 3.5 %attend_cache.3 = (f32[32,128,128]{2,1,0:T(8,128)S(1)}, f32[32,1,128]{2,1,0:T(1,128)S(1)}, bf16[32,128,128]{2,1,0:T(8,128)(2,1)S(1)}, f32[8,128]{1,0:T(8,128)}) custom-call(s32[32]{0:T(128)S(1)} %copy-done, bf16[2,32,8192]{2,1,0:T(8,128)(2,1)} %q_ref.5, bf16[32,128,2048]{2,1,0:T(8,128)(2,1)} %val_ref.5, bf16[32,128,2048]{2,1,0:T(8,128)(2,1)} %val_ref.5, ...), custom_call_target="tpu_custom_call" | custom-call | flops 1 | bytes 1 | tf_op jit(solution)/shard_map/attend_cache/pallas_call | solution.py:381
  27.9 0.5 collective-permute-start.11
  28.9 1.2 %far_ready.1 = (bf16[320,2048]{1,0:T(8,128)(2,1)S(1)}, bf16[320,256]{1,0:T(8,128)(2,1)S(1)}, bf16[512,320]{1,0:T(8,128)(2,1)S(1)}) custom-call(s32[8]{0:T(128)} %slot_ref.1, s32[1,8]{1,0:T(1,128)S(1)} %collective-permute-done.8.meta_a, s32[1,8]{1,0:T(1,128)S(1)} %collective-permute-done.9.meta_b, ...), custom_call_target="tpu_custom_call" | custom-call | flops 1 | bytes 1 | tf_op jit(solution)/shard_map/far_ready/pallas_call | solution.py:236
  30.6 2.6 %far_delta.1 = (bf16[256,1024]{1,0:T(8,128)(2,1)S(1)}, bf16[64,1024]{1,0:T(8,128)(2,1)S(1)}, bf16[64,1024]{1,0:T(8,128)(2,1)S(1)}, bf16[64,1024]{1,0:T(8,128)(2,...) custom-call(bf16[320,2048]{1,0:T(8,128)(2,1)S(1)} %get-tuple-element.122.refs_0_, ...), custom_call_target="tpu_custom_call" | custom-call | flops 1 | bytes 1 | tf_op jit(solution)/shard_map/far_delta/pallas_call | solution.py:254
  35.4 1.9 %collective-permute-start.23 = (bf16[128,1024]{1,0:T(8,128)(2,1)S(1)}, bf16[128,1024]{1,0:T(8,128)(2,1)S(1)}, u32[]{:S(2)}, u32[]{:S(2)}) collective-permute-start(bf16[128,1024]{1,0:T(8,128)(2,1)S(1)} %get-tuple-element.165), channel_id=1, source_target_pairs={{0,4},{4,0},{8,12},{12,8},{1,5},{5,1},{9,13},{13,9},{2,6},{6,2},{1... | collective-permute-start | bytes 786440 | tf_op jit(solution)/shard_map/ppermute | solution.py:564
  37.3 2.3 %more_delta.1 = (bf16[256,1024]{1,0:T(8,128)(2,1)S(1)}, bf16[64,1024]{1,0:T(8,128)(2,1)S(1)}, bf16[64,1024]{1,0:T(8,128)(2,1)S(1)}, bf16[64,1024]{1,0:T(8,128)(2...) custom-call(bf16[320,2048]{1,0:T(8,128)(2,1)S(1)} %get-tuple-element.133.xc_ref, ...), custom_call_target="tpu_custom_call" | custom-call | flops 1 | bytes 1 | tf_op jit(solution)/shard_map/more_delta/pallas_call | solution.py:267
  42.1 2.0 %collective-permute-done.23 = bf16[128,1024]{1,0:T(8,128)(2,1)S(1)} collective-permute-done((bf16[128,1024]{1,0:T(8,128)(2,1)S(1)}, bf16[128,1024]{1,0:T(8,128)(2,1)S(1)}, u32[]{:S(2)}, u32[]{:S(2)}) %collective-permute-start.23) | collective-permute-done | bytes 262176 | tf_op jit(solution)/shard_map/ppermute | solution.py:564
  44.2 1.7 %collective-permute-start.25 = (bf16[128,1024]{1,0:T(8,128)(2,1)S(1)}, bf16[128,1024]{1,0:T(8,128)(2,1)S(1)}, u32[]{:S(2)}, u32[]{:S(2)}) collective-permute-start(bf16[128,1024]{1,0:T(8,128)(2,1)S(1)} %add_convert_fusion.2), channel_id=1, source_target_pairs={{0,2},{1,3},{2,0},{3,1},{4,6},{5,7},{6,4},{7,5},{8,10},{9,11},{10,... | collective-permute-start | bytes 786440 | tf_op jit(solution)/shard_map/ppermute | solution.py:582
  45.9 5.3 %attend_cache.4 = (f32[32,128,128]{2,1,0:T(8,128)S(1)}, f32[32,1,128]{2,1,0:T(1,128)S(1)}, bf16[32,128,128]{2,1,0:T(8,128)(2,1)S(1)}, f32[8,128]{1,0:T(8,128)}) custom-call(s32[32]{0:T(128)S(1)} %copy-done, bf16[2,32,8192]{2,1,0:T(8,128)(2,1)} %q_ref.5, bf16[32,128,2048]{2,1,0:T(8,128)(2,1)} %val_ref.5, ...), custom_call_target="tpu_custom_call", output_to_operand_aliasing={{0}: (4, {}), {1}: (5, {}), {2}: (6, {})} | custom-call | flops 1 | bytes 1 | tf_op jit(solution)/shard_map/attend_cache/pallas_call | solution.py:381
  51.3 0.8 %collective-permute-start.24 = (bf16[128,1024]{1,0:T(8,128)(2,1)S(1)}, bf16[128,1024]{1,0:T(8,128)(2,1)S(1)}, u32[]{:S(2)}, u32[]{:S(2)}) collective-permute-start(bf16[128,1024]{1,0:T(8,128)(2,1)S(1)} %add_convert_fusion.1), channel_id=1, source_target_pairs={{0,2},{1,3},{2,0},{3,1},{4,6},{5,7},{6,4},{7,5},{8,10},{9,11},{10,... | collective-permute-start | bytes 786440 | tf_op jit(solution)/shard_map/ppermute | solution.py:582
  52.4 2.6 %collective-permute-start.27 = (bf16[64,1024]{1,0:T(8,128)(2,1)S(1)}, bf16[64,1024]{1,0:T(8,128)(2,1)S(1)}, u32[]{:S(2)}, u32[]{:S(2)}) collective-permute-start(bf16[64,1024]{1,0:T(8,128)(2,1)S(1)} %get-tuple-element.191), channel_id=1, source_target_pairs={{0,8},{4,12},{8,0},{12,4},{1,9},{5,13},{9,1},{13,5},{2,10},{6,14},... | collective-permute-start | bytes 393224 | tf_op jit(solution)/shard_map/ppermute | solution.py:564
  55.0 3.5 %attend_cache.5 = (f32[32,128,128]{2,1,0:T(8,128)S(1)}, f32[32,1,128]{2,1,0:T(1,128)S(1)}, bf16[32,128,128]{2,1,0:T(8,128)(2,1)S(1)}, f32[8,128]{1,0:T(8,128)}) custom-call(s32[32]{0:T(128)S(1)} %copy-done, bf16[2,32,8192]{2,1,0:T(8,128)(2,1)} %q_ref.5, bf16[32,128,2048]{2,1,0:T(8,128)(2,1)} %val_ref.5, ...), custom_call_target="tpu_custom_call", output_to_operand_aliasing={{0}: (4, {}), {1}: (5, {}), {2}: (6, {})} | custom-call | flops 1 | bytes 1 | tf_op jit(solution)/shard_map/attend_cache/pallas_call | solution.py:381
  58.9 2.7 %collective-permute-start.26 = (bf16[64,1024]{1,0:T(8,128)(2,1)S(1)}, bf16[64,1024]{1,0:T(8,128)(2,1)S(1)}, u32[]{:S(2)}, u32[]{:S(2)}) collective-permute-start(bf16[64,1024]{1,0:T(8,128)(2,1)S(1)} %get-tuple-element.206), channel_id=1, source_target_pairs={{0,8},{4,12},{8,0},{12,4},{1,9},{5,13},{9,1},{13,5},{2,10},{6,14},... | collective-permute-start | bytes 393224 | tf_op jit(solution)/shard_map/ppermute | solution.py:564
  61.7 2.5 %weigh_new.1 = (f32[3,32,128]{2,1,0:T(8,128)S(1)}, f32[2,32,8192]{2,1,0:T(8,128)S(1)}) custom-call(f32[32,1,128]{2,1,0:T(1,128)S(1)} %get-tuple-element.189.lse_ref, bf16[32,128,128]{2,1,0:T(8,128)(2,1)S(1)} %get-tuple-element.190.turned_ref, f32[2,32,8,128]{3,2,1,0:T(8,128)S(1)} %bitcast.9, f32[4096,128]{1,0:T(8,128)S(1)} %bitcast.8), custom_call_target="tpu_custom_call" | custom-call | flops 1 | bytes 1 | tf_op jit(solution)/shard_map/weigh_new/pallas_call | solution.py:455
  64.2 2.6 %collective-permute-done.26 = bf16[64,1024]{1,0:T(8,128)(2,1)S(1)} collective-permute-done((bf16[64,1024]{1,0:T(8,128)(2,1)S(1)}, bf16[64,1024]{1,0:T(8,128)(2,1)S(1)}, u32[]{:S(2)}, u32[]{:S(2)}) %collective-permute-start.26) | collective-permute-done | bytes 131104 | tf_op jit(solution)/shard_map/ppermute | solution.py:564
  66.8 2.4 %add_new.1 = (bf16[2,32,8192]{2,1,0:T(8,128)(2,1)}, bf16[2,32,2048]{2,1,0:T(8,128)(2,1)}) custom-call(f32[3,32,128]{2,1,0:T(8,128)S(1)} %get-tuple-element.196.share_ref, f32[2,32,8192]{2,1,0:T(8,128)S(1)} %get-tuple-element.197.early_ref, bf16[2,32,1024]{2,1,0:T(8,128)(2,1)S(1)} %bitcast.10, bf16[2,32,1024]{2,1,0:T(8,128)(2,1)S(1)} %bitcast.11), custom_call_target="tpu_custom_call" | custom-call | flops 1 | bytes 1 | tf_op jit(solution)/shard_map/add_new/pallas_call | solution.py:512
  (60 shorter events, 10.3 us)
Async XLA Ops:
  0.6 5.0 %collective-permute-start.1 = (bf16[256,2048]{1,0:T(8,128)(2,1)}, bf16[256,2048]{1,0:T(8,128)(2,1)S(1)}, u32[]{:S(2)}, u32[]{:S(2)}) collective-permute-start(bf16[256,2048]{1,0:T(8,128)(2,1)} %bitcast.12), channel_id=1, source_target_pairs={{0,1},{1,0},{2,3},{3,2},{4,5},{5,4},{6,7},{7,6},{8,9},{9,8},{10,11... | collective-permute-start | bytes 3145736 | tf_op jit(solution)/shard_map/ppermute | solution.py:582
  1.1 26.6 %collective-permute-start.7 = (bf16[256,2048]{1,0:T(8,128)(2,1)}, bf16[256,2048]{1,0:T(8,128)(2,1)S(1)}, u32[]{:S(2)}, u32[]{:S(2)}) collective-permute-start(bf16[256,2048]{1,0:T(8,128)(2,1)} %bitcast.13), channel_id=1, source_target_pairs={{0,2},{1,3},{2,0},{3,1},{4,6},{5,7},{6,4},{7,5},{8,10},{9,11},{10,... | collective-permute-start | bytes 3145736 | tf_op jit(solution)/shard_map/ppermute | solution.py:582
  17.3 1.6 %collective-permute-start.2 = (bf16[64,2048]{1,0:T(8,128)(2,1)S(1)}, bf16[64,2048]{1,0:T(8,128)(2,1)S(1)}, u32[]{:S(2)}, u32[]{:S(2)}) collective-permute-start(bf16[64,2048]{1,0:T(8,128)(2,1)S(1)} %get-tuple-element.103), channel_id=1, source_target_pairs={{0,1},{1,0},{2,3},{3,2},{4,5},{5,4},{6,7},{7,6},{8,9},{9,8},{10,11... | collective-permute-start | bytes 786440 | tf_op jit(solution)/shard_map/ppermute | solution.py:582
  17.6 1.7 %collective-permute-start.3 = (bf16[64,2048]{1,0:T(8,128)(2,1)S(1)}, bf16[64,2048]{1,0:T(8,128)(2,1)S(1)}, u32[]{:S(2)}, u32[]{:S(2)}) collective-permute-start(bf16[64,2048]{1,0:T(8,128)(2,1)S(1)} %get-tuple-element.104), channel_id=1, source_target_pairs={{0,1},{1,0},{2,3},{3,2},{4,5},{5,4},{6,7},{7,6},{8,9},{9,8},{10,11... | collective-permute-start | bytes 786440 | tf_op jit(solution)/shard_map/ppermute | solution.py:582
  17.9 1.8 %collective-permute-start.4 = (bf16[64,2048]{1,0:T(8,128)(2,1)S(1)}, bf16[64,2048]{1,0:T(8,128)(2,1)S(1)}, u32[]{:S(2)}, u32[]{:S(2)}) collective-permute-start(bf16[64,2048]{1,0:T(8,128)(2,1)S(1)} %get-tuple-element.105), channel_id=1, source_target_pairs={{0,1},{1,0},{2,3},{3,2},{4,5},{5,4},{6,7},{7,6},{8,9},{9,8},{10,11... | collective-permute-start | bytes 786440 | tf_op jit(solution)/shard_map/ppermute | solution.py:582
  18.1 1.9 %collective-permute-start.5 = (bf16[64,2048]{1,0:T(8,128)(2,1)S(1)}, bf16[64,2048]{1,0:T(8,128)(2,1)S(1)}, u32[]{:S(2)}, u32[]{:S(2)}) collective-permute-start(bf16[64,2048]{1,0:T(8,128)(2,1)S(1)} %get-tuple-element.106), channel_id=1, source_target_pairs={{0,1},{1,0},{2,3},{3,2},{4,5},{5,4},{6,7},{7,6},{8,9},{9,8},{10,11... | collective-permute-start | bytes 786440 | tf_op jit(solution)/shard_map/ppermute | solution.py:582
  20.3 14.1 %collective-permute-start.6 = (bf16[128,2048]{1,0:T(8,128)(2,1)S(1)}, bf16[128,2048]{1,0:T(8,128)(2,1)S(1)}, u32[]{:S(2)}, u32[]{:S(2)}) collective-permute-start(bf16[128,2048]{1,0:T(8,128)(2,1)S(1)} %get-tuple-element.115), channel_id=1, source_target_pairs={{0,4},{4,0},{8,12},{12,8},{1,5},{5,1},{9,13},{13,9},{2,6},{6,2},{1... | collective-permute-start | bytes 1572872 | tf_op jit(solution)/shard_map/ppermute | solution.py:564
  21.9 5.5 %collective-permute-start.9 = (s32[1,8]{1,0:T(1,128)S(1)}, s32[1,8]{1,0:T(1,128)S(1)}, u32[]{:S(2)}, u32[]{:S(2)}) collective-permute-start(s32[1,8]{1,0:T(1,128)S(1)} %pad_add_fusion.refs_1_), channel_id=1, source_target_pairs={{0,3},{1,2},{2,1},{3,0},{4,7},{5,6},{6,5},{7,4},{8,11},{9,10},{10,... | collective-permute-start | bytes 104 | tf_op jit(solution)/shard_map/ppermute | solution.py:582
  22.3 5.4 %collective-permute-start.8 = (s32[1,8]{1,0:T(1,128)S(1)}, s32[1,8]{1,0:T(1,128)S(1)}, u32[]{:S(2)}, u32[]{:S(2)}) collective-permute-start(s32[1,8]{1,0:T(1,128)S(1)} %pad_add_fusion.refs_1_), channel_id=1, source_target_pairs={{0,2},{1,3},{2,0},{3,1},{4,6},{5,7},{6,4},{7,5},{8,10},{9,11},{10,... | collective-permute-start | bytes 104 | tf_op jit(solution)/shard_map/ppermute | solution.py:582
  27.8 2.3 %collective-permute-start.10 = (bf16[64,2048]{1,0:T(8,128)(2,1)S(1)}, bf16[64,2048]{1,0:T(8,128)(2,1)S(1)}, u32[]{:S(2)}, u32[]{:S(2)}) collective-permute-start(bf16[64,2048]{1,0:T(8,128)(2,1)S(1)} %get-tuple-element.125), channel_id=1, source_target_pairs={{0,1},{1,0},{2,3},{3,2},{4,5},{5,4},{6,7},{7,6},{8,9},{9,8},{10,11... | collective-permute-start | bytes 786440 | tf_op jit(solution)/shard_map/ppermute | solution.py:582
  27.9 2.2 %collective-permute-start.11 = (bf16[64,2048]{1,0:T(8,128)(2,1)S(1)}, bf16[64,2048]{1,0:T(8,128)(2,1)S(1)}, u32[]{:S(2)}, u32[]{:S(2)}) collective-permute-start(bf16[64,2048]{1,0:T(8,128)(2,1)S(1)} %get-tuple-element.126), channel_id=1, source_target_pairs={{0,1},{1,0},{2,3},{3,2},{4,5},{5,4},{6,7},{7,6},{8,9},{9,8},{10,11... | collective-permute-start | bytes 786440 | tf_op jit(solution)/shard_map/ppermute | solution.py:582
  28.4 1.8 %collective-permute-start.12 = (bf16[64,2048]{1,0:T(8,128)(2,1)S(1)}, bf16[64,2048]{1,0:T(8,128)(2,1)S(1)}, u32[]{:S(2)}, u32[]{:S(2)}) collective-permute-start(bf16[64,2048]{1,0:T(8,128)(2,1)S(1)} %get-tuple-element.127), channel_id=1, source_target_pairs={{0,1},{1,0},{2,3},{3,2},{4,5},{5,4},{6,7},{7,6},{8,9},{9,8},{10,11... | collective-permute-start | bytes 786440 | tf_op jit(solution)/shard_map/ppermute | solution.py:582
  28.5 2.1 %collective-permute-start.13 = (bf16[64,2048]{1,0:T(8,128)(2,1)S(1)}, bf16[64,2048]{1,0:T(8,128)(2,1)S(1)}, u32[]{:S(2)}, u32[]{:S(2)}) collective-permute-start(bf16[64,2048]{1,0:T(8,128)(2,1)S(1)} %get-tuple-element.128), channel_id=1, source_target_pairs={{0,1},{1,0},{2,3},{3,2},{4,5},{5,4},{6,7},{7,6},{8,9},{9,8},{10,11... | collective-permute-start | bytes 786440 | tf_op jit(solution)/shard_map/ppermute | solution.py:582
  33.2 1.4 %collective-permute-start.14 = (bf16[64,1024]{1,0:T(8,128)(2,1)S(1)}, bf16[64,1024]{1,0:T(8,128)(2,1)S(1)}, u32[]{:S(2)}, u32[]{:S(2)}) collective-permute-start(bf16[64,1024]{1,0:T(8,128)(2,1)S(1)} %get-tuple-element.135), channel_id=1, source_target_pairs={{0,1},{1,0},{2,3},{3,2},{4,5},{5,4},{6,7},{7,6},{8,9},{9,8},{10,11... | collective-permute-start | bytes 393224 | tf_op jit(solution)/shard_map/ppermute | solution.py:582
  33.9 1.4 %collective-permute-start.17 = (bf16[64,1024]{1,0:T(8,128)(2,1)S(1)}, bf16[64,1024]{1,0:T(8,128)(2,1)S(1)}, u32[]{:S(2)}, u32[]{:S(2)}) collective-permute-start(bf16[64,1024]{1,0:T(8,128)(2,1)S(1)} %get-tuple-element.138), channel_id=1, source_target_pairs={{0,1},{1,0},{2,3},{3,2},{4,5},{5,4},{6,7},{7,6},{8,9},{9,8},{10,11... | collective-permute-start | bytes 393224 | tf_op jit(solution)/shard_map/ppermute | solution.py:582
  35.4 8.7 %collective-permute-start.23 = (bf16[128,1024]{1,0:T(8,128)(2,1)S(1)}, bf16[128,1024]{1,0:T(8,128)(2,1)S(1)}, u32[]{:S(2)}, u32[]{:S(2)}) collective-permute-start(bf16[128,1024]{1,0:T(8,128)(2,1)S(1)} %get-tuple-element.165), channel_id=1, source_target_pairs={{0,4},{4,0},{8,12},{12,8},{1,5},{5,1},{9,13},{13,9},{2,6},{6,2},{1... | collective-permute-start | bytes 786440 | tf_op jit(solution)/shard_map/ppermute | solution.py:564
  39.6 1.4 %collective-permute-start.18 = (bf16[64,1024]{1,0:T(8,128)(2,1)S(1)}, bf16[64,1024]{1,0:T(8,128)(2,1)S(1)}, u32[]{:S(2)}, u32[]{:S(2)}) collective-permute-start(bf16[64,1024]{1,0:T(8,128)(2,1)S(1)} %get-tuple-element.148), channel_id=1, source_target_pairs={{0,1},{1,0},{2,3},{3,2},{4,5},{5,4},{6,7},{7,6},{8,9},{9,8},{10,11... | collective-permute-start | bytes 393224 | tf_op jit(solution)/shard_map/ppermute | solution.py:582
  39.8 1.5 %collective-permute-start.19 = (bf16[64,1024]{1,0:T(8,128)(2,1)S(1)}, bf16[64,1024]{1,0:T(8,128)(2,1)S(1)}, u32[]{:S(2)}, u32[]{:S(2)}) collective-permute-start(bf16[64,1024]{1,0:T(8,128)(2,1)S(1)} %get-tuple-element.149), channel_id=1, source_target_pairs={{0,1},{1,0},{2,3},{3,2},{4,5},{5,4},{6,7},{7,6},{8,9},{9,8},{10,11... | collective-permute-start | bytes 393224 | tf_op jit(solution)/shard_map/ppermute | solution.py:582
  40.3 1.5 %collective-permute-start.21 = (bf16[64,1024]{1,0:T(8,128)(2,1)S(1)}, bf16[64,1024]{1,0:T(8,128)(2,1)S(1)}, u32[]{:S(2)}, u32[]{:S(2)}) collective-permute-start(bf16[64,1024]{1,0:T(8,128)(2,1)S(1)} %get-tuple-element.151), channel_id=1, source_target_pairs={{0,1},{1,0},{2,3},{3,2},{4,5},{5,4},{6,7},{7,6},{8,9},{9,8},{10,11... | collective-permute-start | bytes 393224 | tf_op jit(solution)/shard_map/ppermute | solution.py:582
  41.9 9.4 %collective-permute-start.22 = (bf16[128,1024]{1,0:T(8,128)(2,1)S(1)}, bf16[128,1024]{1,0:T(8,128)(2,1)S(1)}, u32[]{:S(2)}, u32[]{:S(2)}) collective-permute-start(bf16[128,1024]{1,0:T(8,128)(2,1)S(1)} %get-tuple-element.160), channel_id=1, source_target_pairs={{0,4},{4,0},{8,12},{12,8},{1,5},{5,1},{9,13},{13,9},{2,6},{6,2},{1... | collective-permute-start | bytes 786440 | tf_op jit(solution)/shard_map/ppermute | solution.py:564
  44.2 8.1 %collective-permute-start.25 = (bf16[128,1024]{1,0:T(8,128)(2,1)S(1)}, bf16[128,1024]{1,0:T(8,128)(2,1)S(1)}, u32[]{:S(2)}, u32[]{:S(2)}) collective-permute-start(bf16[128,1024]{1,0:T(8,128)(2,1)S(1)} %add_convert_fusion.2), channel_id=1, source_target_pairs={{0,2},{1,3},{2,0},{3,1},{4,6},{5,7},{6,4},{7,5},{8,10},{9,11},{10,... | collective-permute-start | bytes 786440 | tf_op jit(solution)/shard_map/ppermute | solution.py:582
  51.3 7.5 %collective-permute-start.24 = (bf16[128,1024]{1,0:T(8,128)(2,1)S(1)}, bf16[128,1024]{1,0:T(8,128)(2,1)S(1)}, u32[]{:S(2)}, u32[]{:S(2)}) collective-permute-start(bf16[128,1024]{1,0:T(8,128)(2,1)S(1)} %add_convert_fusion.1), channel_id=1, source_target_pairs={{0,2},{1,3},{2,0},{3,1},{4,6},{5,7},{6,4},{7,5},{8,10},{9,11},{10,... | collective-permute-start | bytes 786440 | tf_op jit(solution)/shard_map/ppermute | solution.py:582
  52.4 9.2 %collective-permute-start.27 = (bf16[64,1024]{1,0:T(8,128)(2,1)S(1)}, bf16[64,1024]{1,0:T(8,128)(2,1)S(1)}, u32[]{:S(2)}, u32[]{:S(2)}) collective-permute-start(bf16[64,1024]{1,0:T(8,128)(2,1)S(1)} %get-tuple-element.191), channel_id=1, source_target_pairs={{0,8},{4,12},{8,0},{12,4},{1,9},{5,13},{9,1},{13,5},{2,10},{6,14},... | collective-permute-start | bytes 393224 | tf_op jit(solution)/shard_map/ppermute | solution.py:564
  58.9 7.9 %collective-permute-start.26 = (bf16[64,1024]{1,0:T(8,128)(2,1)S(1)}, bf16[64,1024]{1,0:T(8,128)(2,1)S(1)}, u32[]{:S(2)}, u32[]{:S(2)}) collective-permute-start(bf16[64,1024]{1,0:T(8,128)(2,1)S(1)} %get-tuple-element.206), channel_id=1, source_target_pairs={{0,8},{4,12},{8,0},{12,4},{1,9},{5,13},{9,1},{13,5},{2,10},{6,14},... | collective-permute-start | bytes 393224 | tf_op jit(solution)/shard_map/ppermute | solution.py:564
  (5 other events, 10.3 us)
